TPU v7x, 32 devices: a whole 2x2x4 slice. The times are simulated.
32 devices in a mesh: groups: 2 (over x), gx: 16 (over z, y, core).
Axes of the slice: x: 2, y: 2, z: 4, core: 2. Of those that a mesh axis runs over, the one named last changes fastest.
Arguments:
- tokens: bfloat16 [1024, 16384], P('groups', 'gx'), parts along dimension 0, may hold values from -6 to 6
- gate_weight: bfloat16 [16384, 5120], P('gx'), may hold values from -0.046875 to 0.046875
- up_weight: bfloat16 [16384, 5120], P('gx'), may hold values from -0.046875 to 0.046875
- down_weight: bfloat16 [5120, 16384], P(None, 'gx'), may hold values from -0.078125 to 0.078125
Outputs:
- mixed: bfloat16 [1024, 16384], P('groups', 'gx'), parts along dimension 0
There are 2 independent parts, one for each index of `groups`. A program takes and returns all parts, laid end to end along the dimension named above; an argument that names none is the same for every part. Nothing has to cross between parts.
All inputs are finite; a program needn't handle non-finite values.
Results may differ from a plain program's by a relative error of at most 0.0049.
Values may be sent and summed in bfloat16 or wider, within the bound.
No kernel may reach another device: no remote copies, remote signals or barrier semaphores. Data moves between devices by JAX's collectives and lax.ppermute only.
A program may use at most 128 MiB of HBM per device.

v0:
```python
import jax
import jax.numpy as jnp
from jax import lax
from jax.sharding import PartitionSpec as P


def on_device(tokens, gate_weight, up_weight, down_weight):
    width = gate_weight.shape[1]
    gate_part = jnp.dot(tokens, gate_weight, preferred_element_type=jnp.float32)
    up_part = jnp.dot(tokens, up_weight, preferred_element_type=jnp.float32)
    summed = lax.psum_scatter(
        jnp.concatenate([gate_part, up_part], axis=1), "gx", scatter_dimension=0, tiled=True
    )
    hidden = (jax.nn.silu(summed[:, :width]) * summed[:, width:]).astype(jnp.bfloat16)
    result = jnp.dot(
        lax.all_gather(hidden, "gx", axis=0, tiled=True),
        down_weight,
        preferred_element_type=jnp.float32,
    )
    return result.astype(jnp.bfloat16)


def solution(mesh):
    placed = (P("groups", "gx"), P("gx", None), P("gx", None), P(None, "gx"))
    return jax.shard_map(
        on_device, mesh=mesh, in_specs=placed, out_specs=P("groups", "gx"), check_vma=False
    )
```

profile of v0, /device:TPU:0, one launch (start us, length us, event | category | flops | bytes accessed | tf_op | source)
XLA Modules:
  0.0 317.9 jit_solution(17249724953355924325)
XLA Ops:
  6.5 0.0 copy-start
  6.5 0.0 reduce-scatter.2.cloned.1.call-start
  6.5 1.2 copy-done
  7.8 0.0 copy-start.2
  7.8 8.4 %fusion.1 = f32[512,5120]{1,0:T(8,128)S(1)} fusion(bf16[512,1024]{1,0:T(8,128)(2,1)S(1)} %copy-done, bf16[1024,5120]{1,0:T(8,128)(2,1)} %param.5), kind=kOutput, calls=%fused_computation.4 | convolution fusion | flops 5368709120 | bytes 22020096 | tf_op jit(solution)/shard_map/dot_general | solution.py:9
  16.2 0.0 copy-done.2
  16.2 5.7 %fusion.2 = f32[512,5120]{1,0:T(8,128)S(1)} fusion(bf16[512,1024]{1,0:T(8,128)(2,1)S(1)} %copy-done, bf16[1024,5120]{1,0:T(8,128)(2,1)S(1)} %copy-done.2), kind=kOutput, calls=%fused_computation.5 | convolution fusion | flops 5368709120 | bytes 22020096 | tf_op jit(solution)/shard_map/dot_general | solution.py:10
  21.9 7.3 %pad_maximum_fusion = f32[512,10240]{1,0:T(8,128)} fusion(f32[512,5120]{1,0:T(8,128)S(1)} %fusion.2, f32[512,5120]{1,0:T(8,128)S(1)} %fusion.1), kind=kLoop, calls=%fused_computation | loop fusion | flops 5242880 | bytes 41943040 | tf_op jit(solution)/shard_map/concatenate | solution.py:12
  29.2 0.0 reduce-scatter.2.cloned.1.call-update
  29.2 0.0 all-gather.2.cloned.1.call-start
  29.2 213.7 %reduce-scatter.2.cloned.1.call-done = f32[32,10240]{1,0:T(8,128)} async-done(((f32[512,10240]{1,0:T(8,128)}), f32[32,10240]{1,0:T(8,128)}) %reduce-scatter.2.cloned.1.call-update) | async-done | bytes 1310736 | tf_op jit(solution)/shard_map/reduce_scatter | solution.py:11
  242.9 2.2 fusion
  245.1 0.0 all-gather.2.cloned.1.call-update
  245.1 55.3 %all-gather.2.cloned.1.call-done = bf16[512,5120]{1,0:T(8,128)(2,1)} async-done(((bf16[32,5120]{1,0:T(8,128)(2,1)}), bf16[512,5120]{1,0:T(8,128)(2,1)}) %all-gather.2.cloned.1.call-update) | async-done | bytes 5242896 | tf_op jit(solution)/shard_map/all_gather | solution.py:16
  300.4 0.0 copy-start.1
  300.4 10.7 %convolution_convert_fusion = bf16[512,1024]{1,0:T(8,128)(2,1)} fusion(bf16[512,5120]{1,0:T(8,128)(2,1)} %all-gather.2.cloned.1.call-done, bf16[5120,1024]{1,0:T(8,128)(2,1)} %param.7), kind=kOutput, calls=%fused_computation.1 | convolution fusion | flops 5369233408 | bytes 16777216 | tf_op jit(solution)/shard_map/dot_general | solution.py:15
  311.1 0.0 copy-done.1
Async XLA Ops:
  6.5 1.2 copy-start
  6.5 236.4 %reduce-scatter.2.cloned.1.call-start = ((), (), s32[]{:S(2)}) async-start(), calls=%async_computation.1 | async-start | bytes 22282240 | tf_op jit(solution)/shard_map/reduce_scatter | solution.py:11
  7.8 8.4 %copy-start.2 = (bf16[1024,5120]{1,0:T(8,128)(2,1)S(1)}, bf16[1024,5120]{1,0:T(8,128)(2,1)}, u32[]{:S(2)}) copy-start(bf16[1024,5120]{1,0:T(8,128)(2,1)} %param.6) | copy-start | bytes 31457284
  29.2 271.2 %all-gather.2.cloned.1.call-start = ((), (), s32[]{:S(2)}) async-start(), calls=%async_computation.2 | async-start | bytes 5570560 | tf_op jit(solution)/shard_map/all_gather | solution.py:16
  300.4 10.7 %copy-start.1 = (bf16[512,1024]{1,0:T(8,128)(2,1)S(1)}, bf16[512,1024]{1,0:T(8,128)(2,1)}, u32[]{:S(2)}) copy-start(bf16[512,1024]{1,0:T(8,128)(2,1)} %param.4) | copy-start | bytes 3145732
Sparse Core Ops, SparseCore 0:
  29.3 213.5 reduce-scatter.1
  245.3 55.0 all-gather.1
where the time goes:
time: 318 us
  waiting for transfers between devices  269 us (85%)
  matrix products  24.8 us (8%)
  between operations  13.4 us (4%)
  other arithmetic  9.5 us (3%)
    reduce_scatter x1, waiting for transfers between devices, on_device(): lax.psum_scatter(jnp.concatenate([gate_part, up_part], axis=1), 'gx', sca...  214 us
    all_gather x1, waiting for transfers between devices, on_device(): lax.all_gather(hidden, 'gx', axis=0, tiled=True)  55.3 us
    dot_general x1, matrix products, on_device(): jnp.dot(lax.all_gather(hidden, 'gx', axis=0, tiled=True), down_weight, pr...  10.7 us
    dot_general x1, matrix products, on_device(): gate_part = jnp.dot(tokens, gate_weight, preferred_element_type=jnp.float32)  8.41 us
    concatenate x1, other arithmetic, on_device(): jnp.concatenate([gate_part, up_part], axis=1)  7.31 us
  transfers between devices with their start and end apart: 2, of which 2 were waited for; matrix products, arithmetic and copies ran while one was open for 0% of the time, Pallas kernels for 0%

commit v1 on v0

v1 whole, which is shorter than its diff:
```python
import functools

import jax
import jax.numpy as jnp
from jax import lax
from jax.experimental import pallas as pl
from jax.experimental.pallas import tpu as pltpu
from jax.sharding import PartitionSpec as P

F16, F32, BF16 = jnp.float16, jnp.float32, jnp.bfloat16
PARTS = (10, 10, 10, 10)
CHAIN = True
SCALE = 4.0


def order_of(masks):
    order = [0]
    for m in reversed(masks):
        order = order + [m ^ o for o in order]
    return order


def reorder_kernel(order, back, x_ref, o_ref):
    me = lax.axis_index("gx")
    rows = x_ref.shape[0] // len(order)
    for p, mask in enumerate(order):
        there = pl.ds(pl.multiple_of((me ^ mask) * rows, rows), rows)
        here = slice(p * rows, (p + 1) * rows)
        if back:
            o_ref[there, :] = x_ref[here, :]
        else:
            o_ref[here, :] = x_ref[there, :] * jnp.asarray(SCALE, x_ref.dtype)


def reorder(x, order, back):
    return pl.pallas_call(
        functools.partial(reorder_kernel, order, back),
        out_shape=jax.ShapeDtypeStruct(x.shape, x.dtype),
        in_specs=[pl.BlockSpec(memory_space=pltpu.VMEM)],
        out_specs=pl.BlockSpec(memory_space=pltpu.VMEM),
    )(x)


def schedule(chunks, levels):
    sends = [11, 59, 30, 22] if levels == 4 else [11] + [40] * (levels - 1)
    shares = [p / sum(PARTS) for p in PARTS]
    keys = []
    start = 0.0
    for c, share in enumerate(shares):
        t = start
        keys.append((t, c, 0))
        for s in range(levels):
            t += 4 + sends[s] * share
            keys.append((t, c, s + 1))
        for s in reversed(range(levels)):
            t += 4 + sends[s] * share / 2
            keys.append((t, c, 2 * levels - s))
        start += 59 * share
    return [(c, s) for _, c, s in sorted(keys)]


def on_device(n, tokens, gate_weight, up_weight, down_weight):
    masks = [1 << k for k in range(n.bit_length() - 1)]
    levels = len(masks)
    order = order_of(masks)
    width = gate_weight.shape[1]
    x = reorder(tokens, order, False)
    total = [None, None]
    last = None
    state = {}
    bounds = [sum(PARTS[:c]) * width // sum(PARTS) for c in range(len(PARTS) + 1)]

    def swap(v, mask):
        return lax.ppermute(v, "gx", [(i, i ^ mask) for i in range(n)])

    for c, stage in schedule(len(PARTS), levels):
        cols = slice(bounds[c], bounds[c + 1])
        w = bounds[c + 1] - bounds[c]
        ins = state.pop(c, x)
        if CHAIN and last is not None:
            ins, _ = lax.optimization_barrier((ins, last))
        if stage == 0:
            gate = jnp.dot(ins, gate_weight[:, cols], preferred_element_type=F32)
            up = jnp.dot(ins, up_weight[:, cols], preferred_element_type=F32)
            acc = jnp.concatenate([gate, up], axis=1)
        elif stage <= levels:
            acc, got = ins
            acc = acc + got.astype(F32)
        else:
            hidden, got = ins
        if stage < levels:
            half = acc.shape[0] // 2
            send = acc[half:].astype(F16)
            state[c] = (acc[:half], swap(send, masks[stage]))
            last = send
        elif stage == levels:
            acc = acc * (1 / SCALE)
            hidden = (jax.nn.silu(acc[:, :w]) * acc[:, w:]).astype(BF16)
            state[c] = (hidden, swap(hidden, masks[-1]))
            last = hidden
        elif stage < 2 * levels:
            hidden = jnp.concatenate([hidden, got], axis=0)
            last = hidden
            state[c] = (hidden, swap(hidden, masks[2 * levels - 1 - stage]))
            if stage == 2 * levels - 1:
                lo = jnp.dot(hidden, down_weight[cols], preferred_element_type=F32)
                total[0] = lo if total[0] is None else total[0] + lo
        else:
            hi = jnp.dot(got, down_weight[cols], preferred_element_type=F32)
            total[1] = hi if total[1] is None else total[1] + hi
            last = total[1][:8, :128]
    result = jnp.concatenate([t.astype(BF16) for t in total], axis=0)
    return reorder(result, order, True)


def solution(mesh):
    placed = (P("groups", "gx"), P("gx", None), P("gx", None), P(None, "gx"))
    return jax.shard_map(
        functools.partial(on_device, mesh.shape["gx"]),
        mesh=mesh, in_specs=placed, out_specs=P("groups", "gx"), check_vma=False,
    )
```

time: 318 us -> 153 us (0.48)
  waiting for transfers between devices: 269 us -> 78.4 us
  starting transfers between devices: 0.04 us -> 32.9 us
  between operations: 13.4 us -> 0.66 us
  Pallas kernels: 0 us -> 4.57 us
  matrix products: 24.8 us -> 28.4 us
    reduce_scatter x1 -> x0, waiting for transfers between devices: 214 us -> none  [on_device(): lax.psum_scatter(jnp.concatenate([gate_part, up_part], axis=1), 'gx', sca...]
    ppermute x0 -> x32, waiting for transfers between devices: none -> 78.4 us  [swap(): return lax.ppermute(v, 'gx', [(i, i ^ mask) for i in range(n)])]
    all_gather x1 -> x0, waiting for transfers between devices: 55.3 us -> none  [on_device(): lax.all_gather(hidden, 'gx', axis=0, tiled=True)]
    ppermute x0 -> x32, starting transfers between devices: none -> 32.9 us  [swap(): return lax.ppermute(v, 'gx', [(i, i ^ mask) for i in range(n)])]
    concatenate x1, other arithmetic: 7.31 us -> 1.08 us  [on_device(): result = jnp.concatenate([t.astype(BF16) for t in total], axis=0)]
    pallas_call x0 -> x2, Pallas kernels: none -> 4.57 us  [reorder(): pl.pallas_call(functools.partial(reorder_kernel, order, back), out_shape=...]
    dot_general x3 -> x16, matrix products: 24.8 us -> 28.4 us  [the longest x4 13.1 us: on_device(): gate = jnp.dot(ins, gate_weight[:, cols], preferred_element_type=F32)]
  transfers between devices with their start and end apart: 2 -> 32, of which waited for: 2 -> 18; matrix products, arithmetic and copies ran while one was open for 0% -> 9% of each run, Pallas kernels for 0% -> 0%
where the time goes in v1:
time: 153 us
  waiting for transfers between devices  78.4 us (51%)
  starting transfers between devices  32.9 us (22%)
  matrix products  28.4 us (19%)
  other arithmetic  6.57 us (4%)
  Pallas kernels  4.57 us (3%)
    ppermute x32, waiting for transfers between devices, swap(): return lax.ppermute(v, 'gx', [(i, i ^ mask) for i in range(n)])  78.4 us
    ppermute x32, starting transfers between devices, swap(): return lax.ppermute(v, 'gx', [(i, i ^ mask) for i in range(n)])  32.9 us
    dot_general x4, matrix products, on_device(): gate = jnp.dot(ins, gate_weight[:, cols], preferred_element_type=F32)  13.1 us
    dot_general x4, matrix products, on_device(): up = jnp.dot(ins, up_weight[:, cols], preferred_element_type=F32)  8.48 us
    pallas_call x2, Pallas kernels, reorder(): pl.pallas_call(functools.partial(reorder_kernel, order, back), out_shape=...  4.57 us
    dot_general x4, matrix products, on_device(): lo = jnp.dot(hidden, down_weight[cols], preferred_element_type=F32)  3.42 us
    dot_general x4, matrix products, on_device(): hi = jnp.dot(got, down_weight[cols], preferred_element_type=F32)  3.41 us
  transfers between devices with their start and end apart: 32, of which 18 were waited for; matrix products, arithmetic and copies ran while one was open for 9% of the time, Pallas kernels for 0%

profile of v1, /device:TPU:0, one launch (start us, length us, event | category | flops | bytes accessed | tf_op | source)
XLA Modules:
  0.0 152.9 jit_solution(5953284583749868700)
XLA Ops:
  0.0 2.3 %shard_map.46 = bf16[512,1024]{1,0:T(8,128)(2,1)} custom-call(bf16[512,1024]{1,0:T(8,128)(2,1)} %x_ref.1), custom_call_target="tpu_custom_call" | custom-call | tf_op jit(solution)/shard_map/pallas_call | solution.py:36
  2.3 3.7 %fusion.20 = f32[512,1280]{1,0:T(8,128)S(1)} fusion(bf16[512,1024]{1,0:T(8,128)(2,1)} %shard_map.46, bf16[1024,5120]{1,0:T(8,128)(2,1)} %param.6), kind=kOutput, calls=%fused_computation.36 | convolution fusion | flops 1342177280 | bytes 6291456 | tf_op jit(solution)/shard_map/dot_general | solution.py:84
  6.0 3.3 %fusion.22 = f32[512,1280]{1,0:T(8,128)S(1)} fusion(bf16[512,1024]{1,0:T(8,128)(2,1)S(1)} %copy-done, bf16[1024,5120]{1,0:T(8,128)(2,1)} %param.5), kind=kOutput, calls=%fused_computation.38 | convolution fusion | flops 1342177280 | bytes 6291456 | tf_op jit(solution)/shard_map/dot_general | solution.py:83
  9.3 0.4 fusion.7
  9.7 0.5 collective-permute-start
  10.2 2.7 %collective-permute-done = f16[256,2560]{1,0:T(8,128)(2,1)S(1)} collective-permute-done((f16[256,2560]{1,0:T(8,128)(2,1)S(1)}, f16[256,2560]{1,0:T(8,128)(2,1)S(1)}, u32[]{:S(2)}, u32[]{:S(2)}) %collective-permute-start) | collective-permute-done | bytes 1310752 | tf_op jit(solution)/shard_map/ppermute | solution.py:74
  13.4 1.1 slice-done.5
  14.5 1.5 %fusion.16 = f32[512,1280]{1,0:T(8,128)S(1)} fusion(bf16[512,1024]{1,0:T(8,128)(2,1)S(1)} %copy-done, bf16[1024,5120]{1,0:T(8,128)(2,1)S(1)} %bitcast.19), kind=kOutput, calls=%fused_computation.31 | convolution fusion | flops 1342177280 | bytes 6291456 | tf_op jit(solution)/shard_map/dot_general | solution.py:84
  16.0 3.3 %fusion.18 = f32[512,1280]{1,0:T(8,128)S(1)} fusion(bf16[512,1024]{1,0:T(8,128)(2,1)S(1)} %copy-done, bf16[1024,5120]{1,0:T(8,128)(2,1)} %param.5), kind=kOutput, calls=%fused_computation.33 | convolution fusion | flops 1342177280 | bytes 6291456 | tf_op jit(solution)/shard_map/dot_general | solution.py:83
  19.3 0.4 fusion.6
  19.7 0.4 collective-permute-start.2
  20.2 2.7 %collective-permute-start.1 = (f16[128,2560]{1,0:T(8,128)(2,1)S(1)}, f16[128,2560]{1,0:T(8,128)(2,1)S(1)}, u32[]{:S(2)}, u32[]{:S(2)}) collective-permute-start(f16[128,2560]{1,0:T(8,128)(2,1)S(1)} %get-tuple-element.144), channel_id=1, source_target_pairs={{0,2},{1,3},{2,0},{3,1},{4,6},{5,7},{6,4},{7,5},{8,10},{9,11},{10,... | collective-permute-start | bytes 1966088 | tf_op jit(solution)/shard_map/ppermute | solution.py:74
  23.3 14.8 %collective-permute-done.1 = f16[128,2560]{1,0:T(8,128)(2,1)S(1)} collective-permute-done((f16[128,2560]{1,0:T(8,128)(2,1)S(1)}, f16[128,2560]{1,0:T(8,128)(2,1)S(1)}, u32[]{:S(2)}, u32[]{:S(2)}) %collective-permute-start.1) | collective-permute-done | bytes 655392 | tf_op jit(solution)/shard_map/ppermute | solution.py:74
  38.3 1.6 %fusion.12 = f32[512,1280]{1,0:T(8,128)S(1)} fusion(bf16[512,1024]{1,0:T(8,128)(2,1)S(1)} %copy-done, bf16[1024,5120]{1,0:T(8,128)(2,1)S(1)} %bitcast.19), kind=kOutput, calls=%fused_computation.26 | convolution fusion | flops 1342177280 | bytes 6291456 | tf_op jit(solution)/shard_map/dot_general | solution.py:84
  39.9 3.3 %fusion.14 = f32[512,1280]{1,0:T(8,128)S(1)} fusion(bf16[512,1024]{1,0:T(8,128)(2,1)S(1)} %copy-done, bf16[1024,5120]{1,0:T(8,128)(2,1)} %param.5), kind=kOutput, calls=%fused_computation.28 | convolution fusion | flops 1342177280 | bytes 6291456 | tf_op jit(solution)/shard_map/dot_general | solution.py:83
  43.2 0.4 fusion.5
  43.7 1.9 %collective-permute-start.3 = (f16[64,2560]{1,0:T(8,128)(2,1)S(1)}, f16[64,2560]{1,0:T(8,128)(2,1)S(1)}, u32[]{:S(2)}, u32[]{:S(2)}) collective-permute-start(f16[64,2560]{1,0:T(8,128)(2,1)S(1)} %get-tuple-element.153), channel_id=1, source_target_pairs={{0,4},{1,5},{2,6},{3,7},{4,0},{5,1},{6,2},{7,3},{8,12},{9,13},{10,... | collective-permute-start | bytes 983048 | tf_op jit(solution)/shard_map/ppermute | solution.py:74
  45.6 1.5 collective-permute-start.6
  47.1 0.4 convert_add_fusion.1
  47.6 6.2 %collective-permute-done.3 = f16[64,2560]{1,0:T(8,128)(2,1)S(1)} collective-permute-done((f16[64,2560]{1,0:T(8,128)(2,1)S(1)}, f16[64,2560]{1,0:T(8,128)(2,1)S(1)}, u32[]{:S(2)}, u32[]{:S(2)}) %collective-permute-start.3) | collective-permute-done | bytes 327712 | tf_op jit(solution)/shard_map/ppermute | solution.py:74
  54.0 2.8 %collective-permute-start.5 = (f16[32,2560]{1,0:T(8,128)(2,1)S(1)}, f16[32,2560]{1,0:T(8,128)(2,1)S(1)}, u32[]{:S(2)}, u32[]{:S(2)}) collective-permute-start(f16[32,2560]{1,0:T(8,128)(2,1)S(1)} %get-tuple-element.162), channel_id=1, source_target_pairs={{0,8},{1,9},{2,10},{3,11},{4,12},{5,13},{6,14},{7,15},{8,0},{9,1},... | collective-permute-start | bytes 491528 | tf_op jit(solution)/shard_map/ppermute | solution.py:74
  56.8 5.6 %collective-permute-done.6 = f16[128,2560]{1,0:T(8,128)(2,1)S(1)} collective-permute-done((f16[128,2560]{1,0:T(8,128)(2,1)S(1)}, f16[128,2560]{1,0:T(8,128)(2,1)S(1)}, u32[]{:S(2)}, u32[]{:S(2)}) %collective-permute-start.6) | collective-permute-done | bytes 655392 | tf_op jit(solution)/shard_map/ppermute | solution.py:74
  62.6 1.7 %fusion.8 = f32[512,1280]{1,0:T(8,128)S(1)} fusion(bf16[512,1024]{1,0:T(8,128)(2,1)S(1)} %copy-done, bf16[1024,5120]{1,0:T(8,128)(2,1)S(1)} %bitcast.19), kind=kOutput, calls=%fused_computation.21 | convolution fusion | flops 1342177280 | bytes 6291456 | tf_op jit(solution)/shard_map/dot_general | solution.py:84
  64.3 3.3 %fusion.10 = f32[512,1280]{1,0:T(8,128)S(1)} fusion(bf16[512,1024]{1,0:T(8,128)(2,1)S(1)} %copy-done, bf16[1024,5120]{1,0:T(8,128)(2,1)} %param.5), kind=kOutput, calls=%fused_computation.23 | convolution fusion | flops 1342177280 | bytes 6291456 | tf_op jit(solution)/shard_map/dot_general | solution.py:83
  67.6 0.4 fusion.1
  68.5 1.7 %collective-permute-start.11 = (f16[128,2560]{1,0:T(8,128)(2,1)S(1)}, f16[128,2560]{1,0:T(8,128)(2,1)S(1)}, u32[]{:S(2)}, u32[]{:S(2)}) collective-permute-start(f16[128,2560]{1,0:T(8,128)(2,1)S(1)} %get-tuple-element.140), channel_id=1, source_target_pairs={{0,2},{1,3},{2,0},{3,1},{4,6},{5,7},{6,4},{7,5},{8,10},{9,11},{10,... | collective-permute-start | bytes 1966088 | tf_op jit(solution)/shard_map/ppermute | solution.py:74
  70.3 2.7 %collective-permute-start.7 = (bf16[32,1280]{1,0:T(8,128)(2,1)S(1)}, bf16[32,1280]{1,0:T(8,128)(2,1)S(1)}, u32[]{:S(2)}, u32[]{:S(2)}) collective-permute-start(bf16[32,1280]{1,0:T(8,128)(2,1)S(1)} %fusion.67), channel_id=1, source_target_pairs={{0,8},{1,9},{2,10},{3,11},{4,12},{5,13},{6,14},{7,15},{8,0},{9,1},... | collective-permute-start | bytes 245768 | tf_op jit(solution)/shard_map/ppermute | solution.py:74
  73.4 0.6 collective-permute-start.13
  74.0 6.0 %collective-permute-done.8 = f16[64,2560]{1,0:T(8,128)(2,1)S(1)} collective-permute-done((f16[64,2560]{1,0:T(8,128)(2,1)S(1)}, f16[64,2560]{1,0:T(8,128)(2,1)S(1)}, u32[]{:S(2)}, u32[]{:S(2)}) %collective-permute-start.8) | collective-permute-done | bytes 327712 | tf_op jit(solution)/shard_map/ppermute | solution.py:74
  80.1 1.3 collective-permute-start.14
  81.5 1.8 %collective-permute-start.10 = (bf16[64,1280]{1,0:T(8,128)(2,1)S(1)}, bf16[64,1280]{1,0:T(8,128)(2,1)S(1)}, u32[]{:S(2)}, u32[]{:S(2)}) collective-permute-start(bf16[64,1280]{1,0:T(8,128)(2,1)S(1)} %constant_dynamic-update-slice_fusion), channel_id=1, source_target_pairs={{0,4},{1,5},{2,6},{3,7},{4,0},{5,1},{6,2},{7,3},{8,12},{9,13},{10,... | collective-permute-start | bytes 491528 | tf_op jit(solution)/shard_map/ppermute | solution.py:74
  83.3 2.7 %collective-permute-done.11 = f16[128,2560]{1,0:T(8,128)(2,1)S(1)} collective-permute-done((f16[128,2560]{1,0:T(8,128)(2,1)S(1)}, f16[128,2560]{1,0:T(8,128)(2,1)S(1)}, u32[]{:S(2)}, u32[]{:S(2)}) %collective-permute-start.11) | collective-permute-done | bytes 655392 | tf_op jit(solution)/shard_map/ppermute | solution.py:74
  86.3 1.8 %collective-permute-start.16 = (f16[64,2560]{1,0:T(8,128)(2,1)S(1)}, f16[64,2560]{1,0:T(8,128)(2,1)S(1)}, u32[]{:S(2)}, u32[]{:S(2)}) collective-permute-start(f16[64,2560]{1,0:T(8,128)(2,1)S(1)} %get-tuple-element.150), channel_id=1, source_target_pairs={{0,4},{1,5},{2,6},{3,7},{4,0},{5,1},{6,2},{7,3},{8,12},{9,13},{10,... | collective-permute-start | bytes 983048 | tf_op jit(solution)/shard_map/ppermute | solution.py:74
  88.1 2.9 %collective-permute-done.10 = bf16[64,1280]{1,0:T(8,128)(2,1)S(1)} collective-permute-done((bf16[64,1280]{1,0:T(8,128)(2,1)S(1)}, bf16[64,1280]{1,0:T(8,128)(2,1)S(1)}, u32[]{:S(2)}, u32[]{:S(2)}) %collective-permute-start.10) | collective-permute-done | bytes 163872 | tf_op jit(solution)/shard_map/ppermute | solution.py:74
  91.0 1.5 collective-permute-start.12
  92.6 0.4 collective-permute-start.15
  93.1 6.2 %collective-permute-done.16 = f16[64,2560]{1,0:T(8,128)(2,1)S(1)} collective-permute-done((f16[64,2560]{1,0:T(8,128)(2,1)S(1)}, f16[64,2560]{1,0:T(8,128)(2,1)S(1)}, u32[]{:S(2)}, u32[]{:S(2)}) %collective-permute-start.16) | collective-permute-done | bytes 327712 | tf_op jit(solution)/shard_map/ppermute | solution.py:74
  99.6 2.1 %collective-permute-start.17 = (bf16[64,1280]{1,0:T(8,128)(2,1)S(1)}, bf16[64,1280]{1,0:T(8,128)(2,1)S(1)}, u32[]{:S(2)}, u32[]{:S(2)}) collective-permute-start(bf16[64,1280]{1,0:T(8,128)(2,1)S(1)} %constant_dynamic-update-slice_fusion.4), channel_id=1, source_target_pairs={{0,4},{1,5},{2,6},{3,7},{4,0},{5,1},{6,2},{7,3},{8,12},{9,13},{10,... | collective-permute-start | bytes 491528 | tf_op jit(solution)/shard_map/ppermute | solution.py:74
  102.2 4.1 %collective-permute-done.12 = bf16[128,1280]{1,0:T(8,128)(2,1)S(1)} collective-permute-done((bf16[128,1280]{1,0:T(8,128)(2,1)S(1)}, bf16[128,1280]{1,0:T(8,128)(2,1)S(1)}, u32[]{:S(2)}, u32[]{:S(2)}) %collective-permute-start.12) | collective-permute-done | bytes 327712 | tf_op jit(solution)/shard_map/ppermute | solution.py:74
  106.5 3.8 %collective-permute-done.17 = bf16[64,1280]{1,0:T(8,128)(2,1)S(1)} collective-permute-done((bf16[64,1280]{1,0:T(8,128)(2,1)S(1)}, bf16[64,1280]{1,0:T(8,128)(2,1)S(1)}, u32[]{:S(2)}, u32[]{:S(2)}) %collective-permute-start.17) | collective-permute-done | bytes 163872 | tf_op jit(solution)/shard_map/ppermute | solution.py:74
  110.3 1.6 %collective-permute-start.18 = (bf16[128,1280]{1,0:T(8,128)(2,1)S(1)}, bf16[128,1280]{1,0:T(8,128)(2,1)S(1)}, u32[]{:S(2)}, u32[]{:S(2)}) collective-permute-start(bf16[128,1280]{1,0:T(8,128)(2,1)S(1)} %constant_dynamic-update-slice_fusion.8), channel_id=1, source_target_pairs={{0,2},{1,3},{2,0},{3,1},{4,6},{5,7},{6,4},{7,5},{8,10},{9,11},{10,... | collective-permute-start | bytes 983048 | tf_op jit(solution)/shard_map/ppermute | solution.py:74
  112.0 0.4 collective-permute-start.20
  112.4 4.5 %collective-permute-done.21 = f16[64,2560]{1,0:T(8,128)(2,1)S(1)} collective-permute-done((f16[64,2560]{1,0:T(8,128)(2,1)S(1)}, f16[64,2560]{1,0:T(8,128)(2,1)S(1)}, u32[]{:S(2)}, u32[]{:S(2)}) %collective-permute-start.21) | collective-permute-done | bytes 327712 | tf_op jit(solution)/shard_map/ppermute | solution.py:74
  117.3 1.0 collective-permute-done.20
  118.3 1.3 collective-permute-start.22
  119.7 6.3 %collective-permute-done.22 = bf16[64,1280]{1,0:T(8,128)(2,1)S(1)} collective-permute-done((bf16[64,1280]{1,0:T(8,128)(2,1)S(1)}, bf16[64,1280]{1,0:T(8,128)(2,1)S(1)}, u32[]{:S(2)}, u32[]{:S(2)}) %collective-permute-start.22) | collective-permute-done | bytes 163872 | tf_op jit(solution)/shard_map/ppermute | solution.py:74
  126.1 0.6 collective-permute-start.25
  126.7 0.8 fusion.34
  127.6 1.9 %collective-permute-start.23 = (bf16[128,1280]{1,0:T(8,128)(2,1)S(1)}, bf16[128,1280]{1,0:T(8,128)(2,1)S(1)}, u32[]{:S(2)}, u32[]{:S(2)}) collective-permute-start(bf16[128,1280]{1,0:T(8,128)(2,1)S(1)} %constant_dynamic-update-slice_fusion.14), channel_id=1, source_target_pairs={{0,2},{1,3},{2,0},{3,1},{4,6},{5,7},{6,4},{7,5},{8,10},{9,11},{10,... | collective-permute-start | bytes 983048 | tf_op jit(solution)/shard_map/ppermute | solution.py:74
  129.5 2.2 %collective-permute-done.25 = bf16[32,1280]{1,0:T(8,128)(2,1)S(1)} collective-permute-done((bf16[32,1280]{1,0:T(8,128)(2,1)S(1)}, bf16[32,1280]{1,0:T(8,128)(2,1)S(1)}, u32[]{:S(2)}, u32[]{:S(2)}) %collective-permute-start.25) | collective-permute-done | bytes 81952 | tf_op jit(solution)/shard_map/ppermute | solution.py:74
  131.8 3.5 %collective-permute-done.23 = bf16[128,1280]{1,0:T(8,128)(2,1)S(1)} collective-permute-done((bf16[128,1280]{1,0:T(8,128)(2,1)S(1)}, bf16[128,1280]{1,0:T(8,128)(2,1)S(1)}, u32[]{:S(2)}, u32[]{:S(2)}) %collective-permute-start.23) | collective-permute-done | bytes 327712 | tf_op jit(solution)/shard_map/ppermute | solution.py:74
  135.4 1.7 %collective-permute-done.26 = bf16[64,1280]{1,0:T(8,128)(2,1)S(1)} collective-permute-done((bf16[64,1280]{1,0:T(8,128)(2,1)S(1)}, bf16[64,1280]{1,0:T(8,128)(2,1)S(1)}, u32[]{:S(2)}, u32[]{:S(2)}) %collective-permute-start.26) | collective-permute-done | bytes 163872 | tf_op jit(solution)/shard_map/ppermute | solution.py:74
  137.1 2.0 %collective-permute-start.27 = (bf16[128,1280]{1,0:T(8,128)(2,1)S(1)}, bf16[128,1280]{1,0:T(8,128)(2,1)S(1)}, u32[]{:S(2)}, u32[]{:S(2)}) collective-permute-start(bf16[128,1280]{1,0:T(8,128)(2,1)S(1)} %constant_dynamic-update-slice_fusion.20), channel_id=1, source_target_pairs={{0,2},{1,3},{2,0},{3,1},{4,6},{5,7},{6,4},{7,5},{8,10},{9,11},{10,... | collective-permute-start | bytes 983048 | tf_op jit(solution)/shard_map/ppermute | solution.py:74
  139.1 0.8 fusion.30
  140.0 0.9 fusion.52
  140.9 0.8 fusion.32
  141.7 3.9 %collective-permute-done.27 = bf16[128,1280]{1,0:T(8,128)(2,1)S(1)} collective-permute-done((bf16[128,1280]{1,0:T(8,128)(2,1)S(1)}, bf16[128,1280]{1,0:T(8,128)(2,1)S(1)}, u32[]{:S(2)}, u32[]{:S(2)}) %collective-permute-start.27) | collective-permute-done | bytes 327712 | tf_op jit(solution)/shard_map/ppermute | solution.py:74
  145.7 0.9 fusion.61
  146.6 0.8 fusion.28
  147.5 0.4 collective-permute-done.31
  147.8 0.8 fusion.24
  148.7 0.9 fusion.58
  149.6 1.1 pad_maximum_fusion.4.x_ref
  150.6 2.3 %shard_map.47 = bf16[512,1024]{1,0:T(8,128)(2,1)} custom-call(bf16[512,1024]{1,0:T(8,128)(2,1)} %pad_maximum_fusion.4.x_ref), custom_call_target="tpu_custom_call" | custom-call | tf_op jit(solution)/shard_map/pallas_call | solution.py:36
  (95 shorter events, 5.1 us)
Async XLA Ops:
  2.3 3.7 %copy-start = (bf16[512,1024]{1,0:T(8,128)(2,1)S(1)}, bf16[512,1024]{1,0:T(8,128)(2,1)}, u32[]{:S(2)}) copy-start(bf16[512,1024]{1,0:T(8,128)(2,1)} %shard_map.46) | copy-start | bytes 3145732
  9.3 4.1 %slice-start.3 = ((s8[10485760]{0:T(1024)(128)(4,1)}), s8[4194304]{0:T(1024)(128)(4,1)S(1)}, s32[]{:S(2)}) async-start(s8[10485760]{0:T(1024)(128)(4,1)} %bitcast.18), calls=%async_computation.3 | async-start | bytes 8388608
  9.3 4.1 %slice-start.4 = ((s8[10485760]{0:T(1024)(128)(4,1)}), s8[4194304]{0:T(1024)(128)(4,1)S(1)}, s32[]{:S(2)}) async-start(s8[10485760]{0:T(1024)(128)(4,1)} %bitcast.18), calls=%async_computation.4 | async-start | bytes 8388608
  9.7 3.2 %collective-permute-start = (f16[256,2560]{1,0:T(8,128)(2,1)S(1)}, f16[256,2560]{1,0:T(8,128)(2,1)S(1)}, u32[]{:S(2)}, u32[]{:S(2)}) collective-permute-start(f16[256,2560]{1,0:T(8,128)(2,1)S(1)} %get-tuple-element.137), channel_id=1, source_target_pairs={{0,1},{1,0},{2,3},{3,2},{4,5},{5,4},{6,7},{7,6},{8,9},{9,8},{10,11... | collective-permute-start | bytes 3932168 | tf_op jit(solution)/shard_map/ppermute | solution.py:74
  12.9 1.6 %slice-start.5 = ((s8[10485760]{0:T(1024)(128)(4,1)}), s8[2097152]{0:T(1024)(128)(4,1)S(1)}, s32[]{:S(2)}) async-start(s8[10485760]{0:T(1024)(128)(4,1)} %bitcast.18), calls=%async_computation.5 | async-start | bytes 4194304
  19.7 3.1 %collective-permute-start.2 = (f16[256,2560]{1,0:T(8,128)(2,1)S(1)}, f16[256,2560]{1,0:T(8,128)(2,1)S(1)}, u32[]{:S(2)}, u32[]{:S(2)}) collective-permute-start(f16[256,2560]{1,0:T(8,128)(2,1)S(1)} %get-tuple-element.135), channel_id=1, source_target_pairs={{0,1},{1,0},{2,3},{3,2},{4,5},{5,4},{6,7},{7,6},{8,9},{9,8},{10,11... | collective-permute-start | bytes 3932168 | tf_op jit(solution)/shard_map/ppermute | solution.py:74
  20.2 17.9 %collective-permute-start.1 = (f16[128,2560]{1,0:T(8,128)(2,1)S(1)}, f16[128,2560]{1,0:T(8,128)(2,1)S(1)}, u32[]{:S(2)}, u32[]{:S(2)}) collective-permute-start(f16[128,2560]{1,0:T(8,128)(2,1)S(1)} %get-tuple-element.144), channel_id=1, source_target_pairs={{0,2},{1,3},{2,0},{3,1},{4,6},{5,7},{6,4},{7,5},{8,10},{9,11},{10,... | collective-permute-start | bytes 1966088 | tf_op jit(solution)/shard_map/ppermute | solution.py:74
  43.6 3.5 %collective-permute-start.4 = (f16[256,2560]{1,0:T(8,128)(2,1)S(1)}, f16[256,2560]{1,0:T(8,128)(2,1)S(1)}, u32[]{:S(2)}, u32[]{:S(2)}) collective-permute-start(f16[256,2560]{1,0:T(8,128)(2,1)S(1)} %get-tuple-element.133), channel_id=1, source_target_pairs={{0,1},{1,0},{2,3},{3,2},{4,5},{5,4},{6,7},{7,6},{8,9},{9,8},{10,11... | collective-permute-start | bytes 3932168 | tf_op jit(solution)/shard_map/ppermute | solution.py:74
  43.7 10.2 %collective-permute-start.3 = (f16[64,2560]{1,0:T(8,128)(2,1)S(1)}, f16[64,2560]{1,0:T(8,128)(2,1)S(1)}, u32[]{:S(2)}, u32[]{:S(2)}) collective-permute-start(f16[64,2560]{1,0:T(8,128)(2,1)S(1)} %get-tuple-element.153), channel_id=1, source_target_pairs={{0,4},{1,5},{2,6},{3,7},{4,0},{5,1},{6,2},{7,3},{8,12},{9,13},{10,... | collective-permute-start | bytes 983048 | tf_op jit(solution)/shard_map/ppermute | solution.py:74
  45.6 16.8 %collective-permute-start.6 = (f16[128,2560]{1,0:T(8,128)(2,1)S(1)}, f16[128,2560]{1,0:T(8,128)(2,1)S(1)}, u32[]{:S(2)}, u32[]{:S(2)}) collective-permute-start(f16[128,2560]{1,0:T(8,128)(2,1)S(1)} %get-tuple-element.145), channel_id=1, source_target_pairs={{0,2},{1,3},{2,0},{3,1},{4,6},{5,7},{6,4},{7,5},{8,10},{9,11},{10,... | collective-permute-start | bytes 1966088 | tf_op jit(solution)/shard_map/ppermute | solution.py:74
  54.0 16.2 %collective-permute-start.5 = (f16[32,2560]{1,0:T(8,128)(2,1)S(1)}, f16[32,2560]{1,0:T(8,128)(2,1)S(1)}, u32[]{:S(2)}, u32[]{:S(2)}) collective-permute-start(f16[32,2560]{1,0:T(8,128)(2,1)S(1)} %get-tuple-element.162), channel_id=1, source_target_pairs={{0,8},{1,9},{2,10},{3,11},{4,12},{5,13},{6,14},{7,15},{8,0},{9,1},... | collective-permute-start | bytes 491528 | tf_op jit(solution)/shard_map/ppermute | solution.py:74
  68.0 4.9 %collective-permute-start.9 = (f16[256,2560]{1,0:T(8,128)(2,1)S(1)}, f16[256,2560]{1,0:T(8,128)(2,1)S(1)}, u32[]{:S(2)}, u32[]{:S(2)}) collective-permute-start(f16[256,2560]{1,0:T(8,128)(2,1)S(1)} %get-tuple-element.131), channel_id=1, source_target_pairs={{0,1},{1,0},{2,3},{3,2},{4,5},{5,4},{6,7},{7,6},{8,9},{9,8},{10,11... | collective-permute-start | bytes 3932168 | tf_op jit(solution)/shard_map/ppermute | solution.py:74
  68.1 11.9 %collective-permute-start.8 = (f16[64,2560]{1,0:T(8,128)(2,1)S(1)}, f16[64,2560]{1,0:T(8,128)(2,1)S(1)}, u32[]{:S(2)}, u32[]{:S(2)}) collective-permute-start(f16[64,2560]{1,0:T(8,128)(2,1)S(1)} %get-tuple-element.152), channel_id=1, source_target_pairs={{0,4},{1,5},{2,6},{3,7},{4,0},{5,1},{6,2},{7,3},{8,12},{9,13},{10,... | collective-permute-start | bytes 983048 | tf_op jit(solution)/shard_map/ppermute | solution.py:74
  68.5 17.6 %collective-permute-start.11 = (f16[128,2560]{1,0:T(8,128)(2,1)S(1)}, f16[128,2560]{1,0:T(8,128)(2,1)S(1)}, u32[]{:S(2)}, u32[]{:S(2)}) collective-permute-start(f16[128,2560]{1,0:T(8,128)(2,1)S(1)} %get-tuple-element.140), channel_id=1, source_target_pairs={{0,2},{1,3},{2,0},{3,1},{4,6},{5,7},{6,4},{7,5},{8,10},{9,11},{10,... | collective-permute-start | bytes 1966088 | tf_op jit(solution)/shard_map/ppermute | solution.py:74
  70.3 11.2 %collective-permute-start.7 = (bf16[32,1280]{1,0:T(8,128)(2,1)S(1)}, bf16[32,1280]{1,0:T(8,128)(2,1)S(1)}, u32[]{:S(2)}, u32[]{:S(2)}) collective-permute-start(bf16[32,1280]{1,0:T(8,128)(2,1)S(1)} %fusion.67), channel_id=1, source_target_pairs={{0,8},{1,9},{2,10},{3,11},{4,12},{5,13},{6,14},{7,15},{8,0},{9,1},... | collective-permute-start | bytes 245768 | tf_op jit(solution)/shard_map/ppermute | solution.py:74
  73.4 28.3 %collective-permute-start.13 = (f16[128,2560]{1,0:T(8,128)(2,1)S(1)}, f16[128,2560]{1,0:T(8,128)(2,1)S(1)}, u32[]{:S(2)}, u32[]{:S(2)}) collective-permute-start(f16[128,2560]{1,0:T(8,128)(2,1)S(1)} %get-tuple-element.141), channel_id=1, source_target_pairs={{0,2},{1,3},{2,0},{3,1},{4,6},{5,7},{6,4},{7,5},{8,10},{9,11},{10,... | collective-permute-start | bytes 1966088 | tf_op jit(solution)/shard_map/ppermute | solution.py:74
  80.1 12.4 %collective-permute-start.14 = (f16[32,2560]{1,0:T(8,128)(2,1)S(1)}, f16[32,2560]{1,0:T(8,128)(2,1)S(1)}, u32[]{:S(2)}, u32[]{:S(2)}) collective-permute-start(f16[32,2560]{1,0:T(8,128)(2,1)S(1)} %get-tuple-element.159), channel_id=1, source_target_pairs={{0,8},{1,9},{2,10},{3,11},{4,12},{5,13},{6,14},{7,15},{8,0},{9,1},... | collective-permute-start | bytes 491528 | tf_op jit(solution)/shard_map/ppermute | solution.py:74
  81.5 9.5 %collective-permute-start.10 = (bf16[64,1280]{1,0:T(8,128)(2,1)S(1)}, bf16[64,1280]{1,0:T(8,128)(2,1)S(1)}, u32[]{:S(2)}, u32[]{:S(2)}) collective-permute-start(bf16[64,1280]{1,0:T(8,128)(2,1)S(1)} %constant_dynamic-update-slice_fusion), channel_id=1, source_target_pairs={{0,4},{1,5},{2,6},{3,7},{4,0},{5,1},{6,2},{7,3},{8,12},{9,13},{10,... | collective-permute-start | bytes 491528 | tf_op jit(solution)/shard_map/ppermute | solution.py:74
  86.0 40.7 %slice-start = ((s8[10485760]{0:T(1024)(128)(4,1)}), s8[4194304]{0:T(1024)(128)(4,1)S(1)}, s32[]{:S(2)}) async-start(s8[10485760]{0:T(1024)(128)(4,1)} %bitcast.16), calls=%async_computation | async-start | bytes 8388608
  86.3 13.1 %collective-permute-start.16 = (f16[64,2560]{1,0:T(8,128)(2,1)S(1)}, f16[64,2560]{1,0:T(8,128)(2,1)S(1)}, u32[]{:S(2)}, u32[]{:S(2)}) collective-permute-start(f16[64,2560]{1,0:T(8,128)(2,1)S(1)} %get-tuple-element.150), channel_id=1, source_target_pairs={{0,4},{1,5},{2,6},{3,7},{4,0},{5,1},{6,2},{7,3},{8,12},{9,13},{10,... | collective-permute-start | bytes 983048 | tf_op jit(solution)/shard_map/ppermute | solution.py:74
  91.0 15.3 %collective-permute-start.12 = (bf16[128,1280]{1,0:T(8,128)(2,1)S(1)}, bf16[128,1280]{1,0:T(8,128)(2,1)S(1)}, u32[]{:S(2)}, u32[]{:S(2)}) collective-permute-start(bf16[128,1280]{1,0:T(8,128)(2,1)S(1)} %constant_dynamic-update-slice_fusion.2), channel_id=1, source_target_pairs={{0,2},{1,3},{2,0},{3,1},{4,6},{5,7},{6,4},{7,5},{8,10},{9,11},{10,... | collective-permute-start | bytes 983048 | tf_op jit(solution)/shard_map/ppermute | solution.py:74
  92.6 6.9 %collective-permute-start.15 = (bf16[32,1280]{1,0:T(8,128)(2,1)S(1)}, bf16[32,1280]{1,0:T(8,128)(2,1)S(1)}, u32[]{:S(2)}, u32[]{:S(2)}) collective-permute-start(bf16[32,1280]{1,0:T(8,128)(2,1)S(1)} %fusion.66), channel_id=1, source_target_pairs={{0,8},{1,9},{2,10},{3,11},{4,12},{5,13},{6,14},{7,15},{8,0},{9,1},... | collective-permute-start | bytes 245768 | tf_op jit(solution)/shard_map/ppermute | solution.py:74
  99.3 27.4 %slice-start.1 = ((s8[10485760]{0:T(1024)(128)(4,1)}), s8[4194304]{0:T(1024)(128)(4,1)S(1)}, s32[]{:S(2)}) async-start(s8[10485760]{0:T(1024)(128)(4,1)} %bitcast.16), calls=%async_computation.1 | async-start | bytes 8388608
  99.5 12.4 %collective-permute-start.19 = (f16[32,2560]{1,0:T(8,128)(2,1)S(1)}, f16[32,2560]{1,0:T(8,128)(2,1)S(1)}, u32[]{:S(2)}, u32[]{:S(2)}) collective-permute-start(f16[32,2560]{1,0:T(8,128)(2,1)S(1)} %get-tuple-element.156), channel_id=1, source_target_pairs={{0,8},{1,9},{2,10},{3,11},{4,12},{5,13},{6,14},{7,15},{8,0},{9,1},... | collective-permute-start | bytes 491528 | tf_op jit(solution)/shard_map/ppermute | solution.py:74
  99.6 10.7 %collective-permute-start.17 = (bf16[64,1280]{1,0:T(8,128)(2,1)S(1)}, bf16[64,1280]{1,0:T(8,128)(2,1)S(1)}, u32[]{:S(2)}, u32[]{:S(2)}) collective-permute-start(bf16[64,1280]{1,0:T(8,128)(2,1)S(1)} %constant_dynamic-update-slice_fusion.4), channel_id=1, source_target_pairs={{0,4},{1,5},{2,6},{3,7},{4,0},{5,1},{6,2},{7,3},{8,12},{9,13},{10,... | collective-permute-start | bytes 491528 | tf_op jit(solution)/shard_map/ppermute | solution.py:74
  102.0 14.9 %collective-permute-start.21 = (f16[64,2560]{1,0:T(8,128)(2,1)S(1)}, f16[64,2560]{1,0:T(8,128)(2,1)S(1)}, u32[]{:S(2)}, u32[]{:S(2)}) collective-permute-start(f16[64,2560]{1,0:T(8,128)(2,1)S(1)} %get-tuple-element.147), channel_id=1, source_target_pairs={{0,4},{1,5},{2,6},{3,7},{4,0},{5,1},{6,2},{7,3},{8,12},{9,13},{10,... | collective-permute-start | bytes 983048 | tf_op jit(solution)/shard_map/ppermute | solution.py:74
  106.3 20.4 %slice-start.2 = ((s8[10485760]{0:T(1024)(128)(4,1)}), s8[2097152]{0:T(1024)(128)(4,1)S(1)}, s32[]{:S(2)}) async-start(s8[10485760]{0:T(1024)(128)(4,1)} %bitcast.16), calls=%async_computation.2 | async-start | bytes 4194304
  106.4 25.4 %collective-permute-start.28 = (bf16[256,1280]{1,0:T(8,128)(2,1)S(1)}, bf16[256,1280]{1,0:T(8,128)(2,1)S(1)}, u32[]{:S(2)}, u32[]{:S(2)}) collective-permute-start(bf16[256,1280]{1,0:T(8,128)(2,1)S(1)} %constant_dynamic-update-slice_fusion.6), channel_id=1, source_target_pairs={{0,1},{1,0},{2,3},{3,2},{4,5},{5,4},{6,7},{7,6},{8,9},{9,8},{10,11... | collective-permute-start | bytes 1966088 | tf_op jit(solution)/shard_map/ppermute | solution.py:74
  110.3 9.2 %collective-permute-start.18 = (bf16[128,1280]{1,0:T(8,128)(2,1)S(1)}, bf16[128,1280]{1,0:T(8,128)(2,1)S(1)}, u32[]{:S(2)}, u32[]{:S(2)}) collective-permute-start(bf16[128,1280]{1,0:T(8,128)(2,1)S(1)} %constant_dynamic-update-slice_fusion.8), channel_id=1, source_target_pairs={{0,2},{1,3},{2,0},{3,1},{4,6},{5,7},{6,4},{7,5},{8,10},{9,11},{10,... | collective-permute-start | bytes 983048 | tf_op jit(solution)/shard_map/ppermute | solution.py:74
  112.0 6.2 %collective-permute-start.20 = (bf16[32,1280]{1,0:T(8,128)(2,1)S(1)}, bf16[32,1280]{1,0:T(8,128)(2,1)S(1)}, u32[]{:S(2)}, u32[]{:S(2)}) collective-permute-start(bf16[32,1280]{1,0:T(8,128)(2,1)S(1)} %fusion.65), channel_id=1, source_target_pairs={{0,8},{1,9},{2,10},{3,11},{4,12},{5,13},{6,14},{7,15},{8,0},{9,1},... | collective-permute-start | bytes 245768 | tf_op jit(solution)/shard_map/ppermute | solution.py:74
  117.1 8.9 %collective-permute-start.24 = (f16[32,2560]{1,0:T(8,128)(2,1)S(1)}, f16[32,2560]{1,0:T(8,128)(2,1)S(1)}, u32[]{:S(2)}, u32[]{:S(2)}) collective-permute-start(f16[32,2560]{1,0:T(8,128)(2,1)S(1)} %get-tuple-element.157), channel_id=1, source_target_pairs={{0,8},{1,9},{2,10},{3,11},{4,12},{5,13},{6,14},{7,15},{8,0},{9,1},... | collective-permute-start | bytes 491528 | tf_op jit(solution)/shard_map/ppermute | solution.py:74
  118.3 7.6 %collective-permute-start.22 = (bf16[64,1280]{1,0:T(8,128)(2,1)S(1)}, bf16[64,1280]{1,0:T(8,128)(2,1)S(1)}, u32[]{:S(2)}, u32[]{:S(2)}) collective-permute-start(bf16[64,1280]{1,0:T(8,128)(2,1)S(1)} %constant_dynamic-update-slice_fusion.10), channel_id=1, source_target_pairs={{0,4},{1,5},{2,6},{3,7},{4,0},{5,1},{6,2},{7,3},{8,12},{9,13},{10,... | collective-permute-start | bytes 491528 | tf_op jit(solution)/shard_map/ppermute | solution.py:74
  119.6 21.3 %collective-permute-start.29 = (bf16[256,1280]{1,0:T(8,128)(2,1)S(1)}, bf16[256,1280]{1,0:T(8,128)(2,1)S(1)}, u32[]{:S(2)}, u32[]{:S(2)}) collective-permute-start(bf16[256,1280]{1,0:T(8,128)(2,1)S(1)} %constant_dynamic-update-slice_fusion.12), channel_id=1, source_target_pairs={{0,1},{1,0},{2,3},{3,2},{4,5},{5,4},{6,7},{7,6},{8,9},{9,8},{10,11... | collective-permute-start | bytes 1966088 | tf_op jit(solution)/shard_map/ppermute | solution.py:74
  126.1 5.6 %collective-permute-start.25 = (bf16[32,1280]{1,0:T(8,128)(2,1)S(1)}, bf16[32,1280]{1,0:T(8,128)(2,1)S(1)}, u32[]{:S(2)}, u32[]{:S(2)}) collective-permute-start(bf16[32,1280]{1,0:T(8,128)(2,1)S(1)} %fusion.64), channel_id=1, source_target_pairs={{0,8},{1,9},{2,10},{3,11},{4,12},{5,13},{6,14},{7,15},{8,0},{9,1},... | collective-permute-start | bytes 245768 | tf_op jit(solution)/shard_map/ppermute | solution.py:74
  127.6 7.7 %collective-permute-start.23 = (bf16[128,1280]{1,0:T(8,128)(2,1)S(1)}, bf16[128,1280]{1,0:T(8,128)(2,1)S(1)}, u32[]{:S(2)}, u32[]{:S(2)}) collective-permute-start(bf16[128,1280]{1,0:T(8,128)(2,1)S(1)} %constant_dynamic-update-slice_fusion.14), channel_id=1, source_target_pairs={{0,2},{1,3},{2,0},{3,1},{4,6},{5,7},{6,4},{7,5},{8,10},{9,11},{10,... | collective-permute-start | bytes 983048 | tf_op jit(solution)/shard_map/ppermute | solution.py:74
  131.7 5.4 %collective-permute-start.26 = (bf16[64,1280]{1,0:T(8,128)(2,1)S(1)}, bf16[64,1280]{1,0:T(8,128)(2,1)S(1)}, u32[]{:S(2)}, u32[]{:S(2)}) collective-permute-start(bf16[64,1280]{1,0:T(8,128)(2,1)S(1)} %constant_dynamic-update-slice_fusion.16), channel_id=1, source_target_pairs={{0,4},{1,5},{2,6},{3,7},{4,0},{5,1},{6,2},{7,3},{8,12},{9,13},{10,... | collective-permute-start | bytes 491528 | tf_op jit(solution)/shard_map/ppermute | solution.py:74
  135.3 11.3 %collective-permute-start.30 = (bf16[256,1280]{1,0:T(8,128)(2,1)S(1)}, bf16[256,1280]{1,0:T(8,128)(2,1)S(1)}, u32[]{:S(2)}, u32[]{:S(2)}) collective-permute-start(bf16[256,1280]{1,0:T(8,128)(2,1)S(1)} %constant_dynamic-update-slice_fusion.18), channel_id=1, source_target_pairs={{0,1},{1,0},{2,3},{3,2},{4,5},{5,4},{6,7},{7,6},{8,9},{9,8},{10,11... | collective-permute-start | bytes 1966088 | tf_op jit(solution)/shard_map/ppermute | solution.py:74
  137.1 8.5 %collective-permute-start.27 = (bf16[128,1280]{1,0:T(8,128)(2,1)S(1)}, bf16[128,1280]{1,0:T(8,128)(2,1)S(1)}, u32[]{:S(2)}, u32[]{:S(2)}) collective-permute-start(bf16[128,1280]{1,0:T(8,128)(2,1)S(1)} %constant_dynamic-update-slice_fusion.20), channel_id=1, source_target_pairs={{0,2},{1,3},{2,0},{3,1},{4,6},{5,7},{6,4},{7,5},{8,10},{9,11},{10,... | collective-permute-start | bytes 983048 | tf_op jit(solution)/shard_map/ppermute | solution.py:74
  145.7 2.2 %collective-permute-start.31 = (bf16[256,1280]{1,0:T(8,128)(2,1)S(1)}, bf16[256,1280]{1,0:T(8,128)(2,1)S(1)}, u32[]{:S(2)}, u32[]{:S(2)}) collective-permute-start(bf16[256,1280]{1,0:T(8,128)(2,1)S(1)} %constant_dynamic-update-slice_fusion.22), channel_id=1, source_target_pairs={{0,1},{1,0},{2,3},{3,2},{4,5},{5,4},{6,7},{7,6},{8,9},{9,8},{10,11... | collective-permute-start | bytes 1966088 | tf_op jit(solution)/shard_map/ppermute | solution.py:74

commit v2 on v0

v2 whole, which is shorter than its diff:
```python
import functools

import jax
import jax.numpy as jnp
from jax import lax
from jax.experimental import pallas as pl
from jax.experimental.pallas import tpu as pltpu
from jax.sharding import PartitionSpec as P

F16, F32, BF16 = jnp.float16, jnp.float32, jnp.bfloat16
PARTS = (4,4,4,4,4)
SCALE = 4.0
FREE = pl.CostEstimate(flops=0, bytes_accessed=0, transcendentals=0)


def order_of(masks):
    order = [0]
    for m in reversed(masks):
        order = order + [m ^ o for o in order]
    return order


def schedule(levels, chunks):
    steps = [(0, 0), (1, 0), (0, 1), *((c, 0) for c in range(2, chunks)), (1, 1)]
    for tick in range(chunks + 2 * levels):
        steps += [(tick, 2), (tick + 2, 1), *((tick + 2 - s, s) for s in range(3, 2 * levels + 1))]
    return [(c, s) for c, s in steps if 0 <= c < chunks]


def reorder_kernel(order, x_ref, o_ref):
    me = lax.axis_index("gx")
    rows = x_ref.shape[0] // len(order)
    for p, mask in enumerate(order):
        there = pl.ds(pl.multiple_of((me ^ mask) * rows, rows), rows)
        o_ref[p * rows : (p + 1) * rows, :] = x_ref[there, :] * jnp.asarray(SCALE, BF16)


def reorder(x, order):
    return pl.pallas_call(
        functools.partial(reorder_kernel, order),
        out_shape=jax.ShapeDtypeStruct(x.shape, x.dtype),
        in_specs=[pl.BlockSpec(memory_space=pltpu.VMEM)],
        out_specs=pl.BlockSpec(memory_space=pltpu.VMEM),
        cost_estimate=FREE,
    )(x)


def last_kernel(order, lo_ref, hi_ref, hidden_ref, down_ref, out_ref):
    me = lax.axis_index("gx")
    rows = out_ref.shape[0] // len(order)
    half = len(order) // 2
    hi = hi_ref[...] + jnp.dot(hidden_ref[...], down_ref[...], preferred_element_type=F32)
    for p, mask in enumerate(order):
        there = pl.ds(pl.multiple_of((me ^ mask) * rows, rows), rows)
        if p < half:
            block = lo_ref[p * rows : (p + 1) * rows, :]
        else:
            block = hi[(p - half) * rows : (p - half + 1) * rows]
        out_ref[there, :] = block.astype(BF16)


def finish(order, lo, hi, hidden, down_weight):
    rows, w = hidden.shape
    columns = down_weight.shape[1]
    tile = min(512, columns)
    return pl.pallas_call(
        functools.partial(last_kernel, order),
        grid=(columns // tile,),
        in_specs=[
            pl.BlockSpec((rows, tile), lambda j: (0, j)),
            pl.BlockSpec((rows, tile), lambda j: (0, j)),
            pl.BlockSpec((rows, w), lambda j: (0, 0)),
            pl.BlockSpec((w, tile), lambda j: (0, j)),
        ],
        out_specs=pl.BlockSpec((2 * rows, tile), lambda j: (0, j)),
        out_shape=jax.ShapeDtypeStruct((2 * rows, columns), BF16),
        cost_estimate=FREE,
        compiler_params=pltpu.CompilerParams(vmem_limit_bytes=24 << 20),
    )(lo, hi, hidden, down_weight)


def on_device(n, tokens, gate_weight, up_weight, down_weight):
    masks = [1 << k for k in range(n.bit_length() - 1)]
    levels = len(masks)
    order = order_of(masks)
    width = gate_weight.shape[1]
    widths = [p * width // sum(PARTS) for p in PARTS]
    starts = [sum(widths[c + 1 :]) for c in range(len(PARTS))]
    total, state, last, result = [None, None], {}, None, None
    steps = schedule(levels, len(PARTS))
    final = len(PARTS) - 1
    steps = [p for p in steps if p != (final, 2 * levels)] + [(final, 2 * levels)]

    def swap(v, mask):
        return lax.ppermute(v, "gx", [(i, i ^ mask) for i in range(n)])

    def split(v):
        half = v.shape[1] // 2
        return v[:, :half], v[:, half:]

    def add(v, got):
        return v.astype(F32) + got.astype(F32)

    x = reorder(tokens, order)
    x = [jnp.dot(x, v, preferred_element_type=F32).astype(F16) for v in (gate_weight, up_weight)]
    for c, stage in steps:
        at, w = starts[c], widths[c]
        cols = slice(at, at + w)
        ins = state.pop(c, x)
        if last is not None:
            ins, _ = lax.optimization_barrier((ins, last))
        if stage == 0:
            acc = jnp.stack([ins[0][:, cols], ins[1][:, cols]])
            keep, send = split(acc)
        elif stage < levels:
            (keep, send), (got_keep, got_send) = split(ins[0]), split(ins[1])
            keep, send = add(keep, got_keep), add(send, got_send)
        if stage < levels:
            send = send.astype(F16)
            state[c] = (keep, swap(send, masks[stage]))
            last = send
        elif stage == levels:
            acc = add(*ins) * (1 / SCALE)
            last = (jax.nn.silu(acc[0]) * acc[1]).astype(BF16)
            state[c] = (last, swap(last, masks[-1]))
        elif stage < 2 * levels:
            last = jnp.concatenate(ins, axis=0)
            state[c] = (last, swap(last, masks[2 * levels - 1 - stage]))
            if stage == 2 * levels - 1:
                lo = jnp.dot(last, down_weight[cols], preferred_element_type=F32)
                total[0] = lo if total[0] is None else total[0] + lo
        elif c == final:
            result = finish(order, total[0], total[1], ins[1], down_weight)
        else:
            hi = jnp.dot(ins[1], down_weight[cols], preferred_element_type=F32)
            total[1] = hi if total[1] is None else total[1] + hi
            last = ins[1]
    return result


def solution(mesh):
    placed = (P("groups", "gx"), P("gx", None), P("gx", None), P(None, "gx"))
    return jax.shard_map(
        functools.partial(on_device, mesh.shape["gx"]),
        mesh=mesh, in_specs=placed, out_specs=P("groups", "gx"), check_vma=False,
    )
```

time: 318 us -> 133 us (0.42)
  waiting for transfers between devices: 269 us -> 47.5 us
  starting transfers between devices: 0.04 us -> 48.5 us
  between operations: 13.4 us -> 0.73 us
  Pallas kernels: 0 us -> 4.44 us
  matrix products: 24.8 us -> 21.4 us
    reduce_scatter x1 -> x0, waiting for transfers between devices: 214 us -> none  [on_device(): lax.psum_scatter(jnp.concatenate([gate_part, up_part], axis=1), 'gx', sca...]
    all_gather x1 -> x0, waiting for transfers between devices: 55.3 us -> none  [on_device(): lax.all_gather(hidden, 'gx', axis=0, tiled=True)]
    ppermute x0 -> x40, starting transfers between devices: none -> 48.5 us  [swap(): return lax.ppermute(v, 'gx', [(i, i ^ mask) for i in range(n)])]
    ppermute x0 -> x40, waiting for transfers between devices: none -> 47.5 us  [swap(): return lax.ppermute(v, 'gx', [(i, i ^ mask) for i in range(n)])]
    concatenate x1 -> x0, other arithmetic: 7.31 us -> none  [on_device(): jnp.concatenate([gate_part, up_part], axis=1)]
    pallas_call x0 -> x2, Pallas kernels: none -> 4.44 us  [the longest x1 2.44 us: reorder(): pl.pallas_call(functools.partial(reorder_kernel, order), out_shape=jax.Sh...]
    another operation x0 -> x5, other arithmetic: none -> 3.39 us  [on_device(): acc = jnp.stack([ins[0][:, cols], ins[1][:, cols]])]
    dot_general x3 -> x11, matrix products: 24.8 us -> 21.4 us  [the longest x2 14.8 us: on_device(): jnp.dot(x, v, preferred_element_type=F32).astype(F16)]
  transfers between devices with their start and end apart: 2 -> 40, of which waited for: 2 -> 16; matrix products, arithmetic and copies ran while one was open for 0% -> 12% of each run, Pallas kernels for 0% -> 0%
where the time goes in v2:
time: 133 us
  starting transfers between devices  48.5 us (36%)
  waiting for transfers between devices  47.5 us (36%)
  matrix products  21.4 us (16%)
  other arithmetic  7.47 us (6%)
  Pallas kernels  4.44 us (3%)
  local copies, waits for them, and re-layouts  3.11 us (2%)
    ppermute x40, starting transfers between devices, swap(): return lax.ppermute(v, 'gx', [(i, i ^ mask) for i in range(n)])  48.5 us
    ppermute x40, waiting for transfers between devices, swap(): return lax.ppermute(v, 'gx', [(i, i ^ mask) for i in range(n)])  47.5 us
    dot_general x2, matrix products, on_device(): jnp.dot(x, v, preferred_element_type=F32).astype(F16)  14.8 us
    dot_general x5, matrix products, on_device(): lo = jnp.dot(last, down_weight[cols], preferred_element_type=F32)  3.67 us
    another operation x5, other arithmetic, on_device(): acc = jnp.stack([ins[0][:, cols], ins[1][:, cols]])  3.39 us
    dot_general x4, matrix products, on_device(): hi = jnp.dot(ins[1], down_weight[cols], preferred_element_type=F32)  2.94 us
    another operation x9, local copies, waits for them, and re-layouts, on_device(): acc = jnp.stack([ins[0][:, cols], ins[1][:, cols]])  2.73 us
  transfers between devices with their start and end apart: 40, of which 16 were waited for; matrix products, arithmetic and copies ran while one was open for 12% of the time, Pallas kernels for 0%

profile of v2, /device:TPU:0, one launch (start us, length us, event | category | flops | bytes accessed | tf_op | source)
XLA Modules:
  0.0 133.1 jit_solution(6634389376119850307)
XLA Ops:
  0.0 2.4 %shard_map.46 = bf16[512,1024]{1,0:T(8,128)(2,1)} custom-call(bf16[512,1024]{1,0:T(8,128)(2,1)} %x_ref.1), custom_call_target="tpu_custom_call" | custom-call | tf_op jit(solution)/shard_map/pallas_call | solution.py:39
  2.5 8.7 %convolution_convert_fusion = f16[512,5120]{1,0:T(8,128)(2,1)S(1)} fusion(bf16[512,1024]{1,0:T(8,128)(2,1)} %shard_map.46, bf16[1024,5120]{1,0:T(8,128)(2,1)} %param.6), kind=kOutput, calls=%fused_computation | convolution fusion | flops 5371330560 | bytes 16777216 | tf_op jit(solution)/shard_map/dot_general | solution.py:105
  11.2 6.0 %convolution_convert_fusion.1 = f16[512,5120]{1,0:T(8,128)(2,1)S(1)} fusion(bf16[512,1024]{1,0:T(8,128)(2,1)S(1)} %copy-done, bf16[1024,5120]{1,0:T(8,128)(2,1)S(1)} %bitcast.86), kind=kOutput, calls=%fused_computation.1 | convolution fusion | flops 5371330560 | bytes 16777216 | tf_op jit(solution)/shard_map/dot_general | solution.py:105
  17.3 0.6 slice_bitcast_fusion
  17.9 0.7 pad_maximum_fusion.4
  18.6 0.5 collective-permute-start
  19.6 0.7 pad_maximum_fusion.3
  20.5 0.9 collective-permute-done
  21.4 0.5 convert_add_fusion.4
  21.9 3.0 %collective-permute-start.1 = (f16[2,128,1024]{2,1,0:T(8,128)(2,1)S(1)}, f16[2,128,1024]{2,1,0:T(8,128)(2,1)S(1)}, u32[]{:S(2)}, u32[]{:S(2)}) collective-permute-start(f16[2,128,1024]{2,1,0:T(8,128)(2,1)S(1)} %get-tuple-element.184), channel_id=1, source_target_pairs={{0,2},{1,3},{2,0},{3,1},{4,6},{5,7},{6,4},{7,5},{8,10},{9,11},{10,... | collective-permute-start | bytes 1572872 | tf_op jit(solution)/shard_map/ppermute | solution.py:95
  25.4 0.7 pad_maximum_fusion.1
  26.6 0.7 pad_maximum_fusion.2
  27.4 0.5 collective-permute-start.6
  28.4 0.6 fusion.39
  29.2 0.5 convert_add_fusion.3
  29.9 7.7 %collective-permute-done.1 = f16[2,128,1024]{2,1,0:T(8,128)(2,1)S(1)} collective-permute-done((f16[2,128,1024]{2,1,0:T(8,128)(2,1)S(1)}, f16[2,128,1024]{2,1,0:T(8,128)(2,1)S(1)}, u32[]{:S(2)}, u32[]{:S(2)}) %collective-permute-start.1) | collective-permute-done | bytes 524320 | tf_op jit(solution)/shard_map/ppermute | solution.py:95
  37.7 2.2 %collective-permute-start.3 = (f16[2,64,1024]{2,1,0:T(8,128)(2,1)S(1)}, f16[2,64,1024]{2,1,0:T(8,128)(2,1)S(1)}, u32[]{:S(2)}, u32[]{:S(2)}) collective-permute-start(f16[2,64,1024]{2,1,0:T(8,128)(2,1)S(1)} %get-tuple-element.200), channel_id=1, source_target_pairs={{0,4},{1,5},{2,6},{3,7},{4,0},{5,1},{6,2},{7,3},{8,12},{9,13},{10,... | collective-permute-start | bytes 786440 | tf_op jit(solution)/shard_map/ppermute | solution.py:95
  40.4 1.6 %collective-permute-start.10 = (f16[2,128,1024]{2,1,0:T(8,128)(2,1)S(1)}, f16[2,128,1024]{2,1,0:T(8,128)(2,1)S(1)}, u32[]{:S(2)}, u32[]{:S(2)}) collective-permute-start(f16[2,128,1024]{2,1,0:T(8,128)(2,1)S(1)} %get-tuple-element.179), channel_id=1, source_target_pairs={{0,2},{1,3},{2,0},{3,1},{4,6},{5,7},{6,4},{7,5},{8,10},{9,11},{10,... | collective-permute-start | bytes 1572872 | tf_op jit(solution)/shard_map/ppermute | solution.py:95
  41.9 6.8 %collective-permute-done.5 = f16[2,128,1024]{2,1,0:T(8,128)(2,1)S(1)} collective-permute-done((f16[2,128,1024]{2,1,0:T(8,128)(2,1)S(1)}, f16[2,128,1024]{2,1,0:T(8,128)(2,1)S(1)}, u32[]{:S(2)}, u32[]{:S(2)}) %collective-permute-start.5) | collective-permute-done | bytes 524320 | tf_op jit(solution)/shard_map/ppermute | solution.py:95
  48.9 2.2 %collective-permute-start.8 = (f16[2,64,1024]{2,1,0:T(8,128)(2,1)S(1)}, f16[2,64,1024]{2,1,0:T(8,128)(2,1)S(1)}, u32[]{:S(2)}, u32[]{:S(2)}) collective-permute-start(f16[2,64,1024]{2,1,0:T(8,128)(2,1)S(1)} %get-tuple-element.198), channel_id=1, source_target_pairs={{0,4},{1,5},{2,6},{3,7},{4,0},{5,1},{6,2},{7,3},{8,12},{9,13},{10,... | collective-permute-start | bytes 786440 | tf_op jit(solution)/shard_map/ppermute | solution.py:95
  51.1 0.5 convert_add_fusion.1
  51.6 1.6 %collective-permute-start.14 = (f16[2,128,1024]{2,1,0:T(8,128)(2,1)S(1)}, f16[2,128,1024]{2,1,0:T(8,128)(2,1)S(1)}, u32[]{:S(2)}, u32[]{:S(2)}) collective-permute-start(f16[2,128,1024]{2,1,0:T(8,128)(2,1)S(1)} %get-tuple-element.172), channel_id=1, source_target_pairs={{0,2},{1,3},{2,0},{3,1},{4,6},{5,7},{6,4},{7,5},{8,10},{9,11},{10,... | collective-permute-start | bytes 1572872 | tf_op jit(solution)/shard_map/ppermute | solution.py:95
  53.3 2.7 %collective-permute-start.7 = (f16[2,32,1024]{2,1,0:T(8,128)(2,1)S(1)}, f16[2,32,1024]{2,1,0:T(8,128)(2,1)S(1)}, u32[]{:S(2)}, u32[]{:S(2)}) collective-permute-start(f16[2,32,1024]{2,1,0:T(8,128)(2,1)S(1)} %get-tuple-element.210), channel_id=1, source_target_pairs={{0,8},{1,9},{2,10},{3,11},{4,12},{5,13},{6,14},{7,15},{8,0},{9,1},... | collective-permute-start | bytes 393224 | tf_op jit(solution)/shard_map/ppermute | solution.py:95
  55.9 4.0 %collective-permute-done.10 = f16[2,128,1024]{2,1,0:T(8,128)(2,1)S(1)} collective-permute-done((f16[2,128,1024]{2,1,0:T(8,128)(2,1)S(1)}, f16[2,128,1024]{2,1,0:T(8,128)(2,1)S(1)}, u32[]{:S(2)}, u32[]{:S(2)}) %collective-permute-start.10) | collective-permute-done | bytes 524320 | tf_op jit(solution)/shard_map/ppermute | solution.py:95
  60.2 2.2 %collective-permute-start.13 = (f16[2,64,1024]{2,1,0:T(8,128)(2,1)S(1)}, f16[2,64,1024]{2,1,0:T(8,128)(2,1)S(1)}, u32[]{:S(2)}, u32[]{:S(2)}) collective-permute-start(f16[2,64,1024]{2,1,0:T(8,128)(2,1)S(1)} %get-tuple-element.196), channel_id=1, source_target_pairs={{0,4},{1,5},{2,6},{3,7},{4,0},{5,1},{6,2},{7,3},{8,12},{9,13},{10,... | collective-permute-start | bytes 786440 | tf_op jit(solution)/shard_map/ppermute | solution.py:95
  62.4 0.5 add_convert_fusion
  62.8 1.6 %collective-permute-start.19 = (f16[2,128,1024]{2,1,0:T(8,128)(2,1)S(1)}, f16[2,128,1024]{2,1,0:T(8,128)(2,1)S(1)}, u32[]{:S(2)}, u32[]{:S(2)}) collective-permute-start(f16[2,128,1024]{2,1,0:T(8,128)(2,1)S(1)} %get-tuple-element.173), channel_id=1, source_target_pairs={{0,2},{1,3},{2,0},{3,1},{4,6},{5,7},{6,4},{7,5},{8,10},{9,11},{10,... | collective-permute-start | bytes 1572872 | tf_op jit(solution)/shard_map/ppermute | solution.py:95
  64.5 2.7 %collective-permute-start.12 = (f16[2,32,1024]{2,1,0:T(8,128)(2,1)S(1)}, f16[2,32,1024]{2,1,0:T(8,128)(2,1)S(1)}, u32[]{:S(2)}, u32[]{:S(2)}) collective-permute-start(f16[2,32,1024]{2,1,0:T(8,128)(2,1)S(1)} %get-tuple-element.208), channel_id=1, source_target_pairs={{0,8},{1,9},{2,10},{3,11},{4,12},{5,13},{6,14},{7,15},{8,0},{9,1},... | collective-permute-start | bytes 393224 | tf_op jit(solution)/shard_map/ppermute | solution.py:95
  67.7 3.6 %collective-permute-done.14 = f16[2,128,1024]{2,1,0:T(8,128)(2,1)S(1)} collective-permute-done((f16[2,128,1024]{2,1,0:T(8,128)(2,1)S(1)}, f16[2,128,1024]{2,1,0:T(8,128)(2,1)S(1)}, u32[]{:S(2)}, u32[]{:S(2)}) %collective-permute-start.14) | collective-permute-done | bytes 524320 | tf_op jit(solution)/shard_map/ppermute | solution.py:95
  71.4 2.2 %collective-permute-start.18 = (f16[2,64,1024]{2,1,0:T(8,128)(2,1)S(1)}, f16[2,64,1024]{2,1,0:T(8,128)(2,1)S(1)}, u32[]{:S(2)}, u32[]{:S(2)}) collective-permute-start(f16[2,64,1024]{2,1,0:T(8,128)(2,1)S(1)} %get-tuple-element.192), channel_id=1, source_target_pairs={{0,4},{1,5},{2,6},{3,7},{4,0},{5,1},{6,2},{7,3},{8,12},{9,13},{10,... | collective-permute-start | bytes 786440 | tf_op jit(solution)/shard_map/ppermute | solution.py:95
  73.7 2.7 %collective-permute-start.17 = (f16[2,32,1024]{2,1,0:T(8,128)(2,1)S(1)}, f16[2,32,1024]{2,1,0:T(8,128)(2,1)S(1)}, u32[]{:S(2)}, u32[]{:S(2)}) collective-permute-start(f16[2,32,1024]{2,1,0:T(8,128)(2,1)S(1)} %get-tuple-element.206), channel_id=1, source_target_pairs={{0,8},{1,9},{2,10},{3,11},{4,12},{5,13},{6,14},{7,15},{8,0},{9,1},... | collective-permute-start | bytes 393224 | tf_op jit(solution)/shard_map/ppermute | solution.py:95
  77.1 4.9 %collective-permute-done.19 = f16[2,128,1024]{2,1,0:T(8,128)(2,1)S(1)} collective-permute-done((f16[2,128,1024]{2,1,0:T(8,128)(2,1)S(1)}, f16[2,128,1024]{2,1,0:T(8,128)(2,1)S(1)}, u32[]{:S(2)}, u32[]{:S(2)}) %collective-permute-start.19) | collective-permute-done | bytes 524320 | tf_op jit(solution)/shard_map/ppermute | solution.py:95
  82.2 1.9 %collective-permute-start.24 = (f16[2,64,1024]{2,1,0:T(8,128)(2,1)S(1)}, f16[2,64,1024]{2,1,0:T(8,128)(2,1)S(1)}, u32[]{:S(2)}, u32[]{:S(2)}) collective-permute-start(f16[2,64,1024]{2,1,0:T(8,128)(2,1)S(1)} %get-tuple-element.193), channel_id=1, source_target_pairs={{0,4},{1,5},{2,6},{3,7},{4,0},{5,1},{6,2},{7,3},{8,12},{9,13},{10,... | collective-permute-start | bytes 786440 | tf_op jit(solution)/shard_map/ppermute | solution.py:95
  84.0 1.0 collective-permute-done.18
  85.1 1.7 %collective-permute-start.23 = (f16[2,32,1024]{2,1,0:T(8,128)(2,1)S(1)}, f16[2,32,1024]{2,1,0:T(8,128)(2,1)S(1)}, u32[]{:S(2)}, u32[]{:S(2)}) collective-permute-start(f16[2,32,1024]{2,1,0:T(8,128)(2,1)S(1)} %get-tuple-element.202), channel_id=1, source_target_pairs={{0,8},{1,9},{2,10},{3,11},{4,12},{5,13},{6,14},{7,15},{8,0},{9,1},... | collective-permute-start | bytes 393224 | tf_op jit(solution)/shard_map/ppermute | solution.py:95
  86.9 1.4 %collective-permute-start.22 = (bf16[32,1024]{1,0:T(8,128)(2,1)S(1)}, bf16[32,1024]{1,0:T(8,128)(2,1)S(1)}, u32[]{:S(2)}, u32[]{:S(2)}) collective-permute-start(bf16[32,1024]{1,0:T(8,128)(2,1)S(1)} %fusion.49), channel_id=1, source_target_pairs={{0,8},{1,9},{2,10},{3,11},{4,12},{5,13},{6,14},{7,15},{8,0},{9,1},... | collective-permute-start | bytes 196616 | tf_op jit(solution)/shard_map/ppermute | solution.py:95
  88.3 0.6 collective-permute-start.21
  89.3 4.5 %collective-permute-start.20 = (bf16[128,1024]{1,0:T(8,128)(2,1)S(1)}, bf16[128,1024]{1,0:T(8,128)(2,1)S(1)}, u32[]{:S(2)}, u32[]{:S(2)}) collective-permute-start(bf16[128,1024]{1,0:T(8,128)(2,1)S(1)} %constant_dynamic-update-slice_fusion.4), channel_id=1, source_target_pairs={{0,2},{1,3},{2,0},{3,1},{4,6},{5,7},{6,4},{7,5},{8,10},{9,11},{10,... | collective-permute-start | bytes 786440 | tf_op jit(solution)/shard_map/ppermute | solution.py:95
  93.8 3.9 %collective-permute-done.24 = f16[2,64,1024]{2,1,0:T(8,128)(2,1)S(1)} collective-permute-done((f16[2,64,1024]{2,1,0:T(8,128)(2,1)S(1)}, f16[2,64,1024]{2,1,0:T(8,128)(2,1)S(1)}, u32[]{:S(2)}, u32[]{:S(2)}) %collective-permute-start.24) | collective-permute-done | bytes 262176 | tf_op jit(solution)/shard_map/ppermute | solution.py:95
  97.7 1.0 collective-permute-start.28
  98.9 2.0 %collective-permute-start.27 = (bf16[32,1024]{1,0:T(8,128)(2,1)S(1)}, bf16[32,1024]{1,0:T(8,128)(2,1)S(1)}, u32[]{:S(2)}, u32[]{:S(2)}) collective-permute-start(bf16[32,1024]{1,0:T(8,128)(2,1)S(1)} %fusion.47), channel_id=1, source_target_pairs={{0,8},{1,9},{2,10},{3,11},{4,12},{5,13},{6,14},{7,15},{8,0},{9,1},... | collective-permute-start | bytes 196616 | tf_op jit(solution)/shard_map/ppermute | solution.py:95
  100.9 0.9 collective-permute-start.26
  101.8 1.6 %collective-permute-start.25 = (bf16[128,1024]{1,0:T(8,128)(2,1)S(1)}, bf16[128,1024]{1,0:T(8,128)(2,1)S(1)}, u32[]{:S(2)}, u32[]{:S(2)}) collective-permute-start(bf16[128,1024]{1,0:T(8,128)(2,1)S(1)} %constant_dynamic-update-slice_fusion.8), channel_id=1, source_target_pairs={{0,2},{1,3},{2,0},{3,1},{4,6},{5,7},{6,4},{7,5},{8,10},{9,11},{10,... | collective-permute-start | bytes 786440 | tf_op jit(solution)/shard_map/ppermute | solution.py:95
  103.5 3.8 %collective-permute-done.28 = f16[2,32,1024]{2,1,0:T(8,128)(2,1)S(1)} collective-permute-done((f16[2,32,1024]{2,1,0:T(8,128)(2,1)S(1)}, f16[2,32,1024]{2,1,0:T(8,128)(2,1)S(1)}, u32[]{:S(2)}, u32[]{:S(2)}) %collective-permute-start.28) | collective-permute-done | bytes 131104 | tf_op jit(solution)/shard_map/ppermute | solution.py:95
  107.5 0.5 collective-permute-done.27
  108.0 2.2 %collective-permute-start.30 = (bf16[64,1024]{1,0:T(8,128)(2,1)S(1)}, bf16[64,1024]{1,0:T(8,128)(2,1)S(1)}, u32[]{:S(2)}, u32[]{:S(2)}) collective-permute-start(bf16[64,1024]{1,0:T(8,128)(2,1)S(1)} %constant_dynamic-update-slice_fusion.12), channel_id=1, source_target_pairs={{0,4},{1,5},{2,6},{3,7},{4,0},{5,1},{6,2},{7,3},{8,12},{9,13},{10,... | collective-permute-start | bytes 393224 | tf_op jit(solution)/shard_map/ppermute | solution.py:95
  110.2 1.1 collective-permute-start.29
  111.5 0.7 fusion.12
  112.2 0.6 collective-permute-done.31
  112.9 0.9 collective-permute-done.30
  113.9 1.1 collective-permute-start.33
  115.0 2.8 %collective-permute-done.29 = bf16[128,1024]{1,0:T(8,128)(2,1)S(1)} collective-permute-done((bf16[128,1024]{1,0:T(8,128)(2,1)S(1)}, bf16[128,1024]{1,0:T(8,128)(2,1)S(1)}, u32[]{:S(2)}, u32[]{:S(2)}) %collective-permute-start.29) | collective-permute-done | bytes 262176 | tf_op jit(solution)/shard_map/ppermute | solution.py:95
  117.8 0.7 fusion.8
  118.6 1.2 collective-permute-start.36
  119.8 2.9 %collective-permute-done.33 = bf16[128,1024]{1,0:T(8,128)(2,1)S(1)} collective-permute-done((bf16[128,1024]{1,0:T(8,128)(2,1)S(1)}, bf16[128,1024]{1,0:T(8,128)(2,1)S(1)}, u32[]{:S(2)}, u32[]{:S(2)}) %collective-permute-start.33) | collective-permute-done | bytes 262176 | tf_op jit(solution)/shard_map/ppermute | solution.py:95
  122.8 0.7 fusion.4
  123.5 0.7 fusion.10
  124.3 0.7 fusion.6
  125.0 2.9 %collective-permute-done.36 = bf16[128,1024]{1,0:T(8,128)(2,1)S(1)} collective-permute-done((bf16[128,1024]{1,0:T(8,128)(2,1)S(1)}, bf16[128,1024]{1,0:T(8,128)(2,1)S(1)}, u32[]{:S(2)}, u32[]{:S(2)}) %collective-permute-start.36) | collective-permute-done | bytes 262176 | tf_op jit(solution)/shard_map/ppermute | solution.py:95
  128.0 0.7 fusion
  128.7 0.8 fusion.27.lo_ref
  129.6 0.7 fusion.2
  130.3 0.8 fusion.36.hi_ref
  131.1 2.0 %shard_map.47 = bf16[512,1024]{1,0:T(8,128)(2,1)} custom-call(f32[256,1024]{1,0:T(8,128)S(1)} %fusion.27.lo_ref, f32[256,1024]{1,0:T(8,128)S(1)} %fusion.36.hi_ref, bf16[256,1024]{1,0:T(8,128)(2,1)S(1)} %collective-permute-done.39.hidden_ref, bf16[5120,1024]{1,0:T(8,128)(2,1)S(1)} %bitcast.84), custom_call_target="tpu_custom_call" | custom-call | tf_op jit(solution)/shard_map/pallas_call | solution.py:66
  (114 shorter events, 7.0 us)
Async XLA Ops:
  0.0 11.2 %slice-start.3 = ((s8[10485760]{0:T(1024)(128)(4,1)}), s8[2097152]{0:T(1024)(128)(4,1)S(1)}, s32[]{:S(2)}) async-start(s8[10485760]{0:T(1024)(128)(4,1)} %bitcast.85), calls=%async_computation.3 | async-start | bytes 4194304
  2.4 8.8 %copy-start = (bf16[512,1024]{1,0:T(8,128)(2,1)S(1)}, bf16[512,1024]{1,0:T(8,128)(2,1)}, u32[]{:S(2)}) copy-start(bf16[512,1024]{1,0:T(8,128)(2,1)} %shard_map.46) | copy-start | bytes 3145732
  2.4 8.8 %slice-start.4 = ((s8[10485760]{0:T(1024)(128)(4,1)}), s8[4194304]{0:T(1024)(128)(4,1)S(1)}, s32[]{:S(2)}) async-start(s8[10485760]{0:T(1024)(128)(4,1)} %bitcast.85), calls=%async_computation.4 | async-start | bytes 8388608
  2.4 8.8 %slice-start.5 = ((s8[10485760]{0:T(1024)(128)(4,1)}), s8[4194304]{0:T(1024)(128)(4,1)S(1)}, s32[]{:S(2)}) async-start(s8[10485760]{0:T(1024)(128)(4,1)} %bitcast.85), calls=%async_computation.5 | async-start | bytes 8388608
  18.6 2.8 %collective-permute-start = (f16[2,256,1024]{2,1,0:T(8,128)(2,1)S(1)}, f16[2,256,1024]{2,1,0:T(8,128)(2,1)S(1)}, u32[]{:S(2)}, u32[]{:S(2)}) collective-permute-start(f16[2,256,1024]{2,1,0:T(8,128)(2,1)S(1)} %get-tuple-element.189), channel_id=1, source_target_pairs={{0,1},{1,0},{2,3},{3,2},{4,5},{5,4},{6,7},{7,6},{8,9},{9,8},{10,11... | collective-permute-start | bytes 3145736 | tf_op jit(solution)/shard_map/ppermute | solution.py:95
  20.3 8.9 %collective-permute-start.2 = (f16[2,256,1024]{2,1,0:T(8,128)(2,1)S(1)}, f16[2,256,1024]{2,1,0:T(8,128)(2,1)S(1)}, u32[]{:S(2)}, u32[]{:S(2)}) collective-permute-start(f16[2,256,1024]{2,1,0:T(8,128)(2,1)S(1)} %get-tuple-element.182), channel_id=1, source_target_pairs={{0,1},{1,0},{2,3},{3,2},{4,5},{5,4},{6,7},{7,6},{8,9},{9,8},{10,11... | collective-permute-start | bytes 3145736 | tf_op jit(solution)/shard_map/ppermute | solution.py:95
  21.9 15.7 %collective-permute-start.1 = (f16[2,128,1024]{2,1,0:T(8,128)(2,1)S(1)}, f16[2,128,1024]{2,1,0:T(8,128)(2,1)S(1)}, u32[]{:S(2)}, u32[]{:S(2)}) collective-permute-start(f16[2,128,1024]{2,1,0:T(8,128)(2,1)S(1)} %get-tuple-element.184), channel_id=1, source_target_pairs={{0,2},{1,3},{2,0},{3,1},{4,6},{5,7},{6,4},{7,5},{8,10},{9,11},{10,... | collective-permute-start | bytes 1572872 | tf_op jit(solution)/shard_map/ppermute | solution.py:95
  27.3 23.8 %collective-permute-start.4 = (f16[2,256,1024]{2,1,0:T(8,128)(2,1)S(1)}, f16[2,256,1024]{2,1,0:T(8,128)(2,1)S(1)}, u32[]{:S(2)}, u32[]{:S(2)}) collective-permute-start(f16[2,256,1024]{2,1,0:T(8,128)(2,1)S(1)} %get-tuple-element.178), channel_id=1, source_target_pairs={{0,1},{1,0},{2,3},{3,2},{4,5},{5,4},{6,7},{7,6},{8,9},{9,8},{10,11... | collective-permute-start | bytes 3145736 | tf_op jit(solution)/shard_map/ppermute | solution.py:95
  27.4 12.5 %collective-permute-start.6 = (f16[2,256,1024]{2,1,0:T(8,128)(2,1)S(1)}, f16[2,256,1024]{2,1,0:T(8,128)(2,1)S(1)}, u32[]{:S(2)}, u32[]{:S(2)}) collective-permute-start(f16[2,256,1024]{2,1,0:T(8,128)(2,1)S(1)} %get-tuple-element.186), channel_id=1, source_target_pairs={{0,1},{1,0},{2,3},{3,2},{4,5},{5,4},{6,7},{7,6},{8,9},{9,8},{10,11... | collective-permute-start | bytes 3145736 | tf_op jit(solution)/shard_map/ppermute | solution.py:95
  29.1 33.3 %collective-permute-start.9 = (f16[2,256,1024]{2,1,0:T(8,128)(2,1)S(1)}, f16[2,256,1024]{2,1,0:T(8,128)(2,1)S(1)}, u32[]{:S(2)}, u32[]{:S(2)}) collective-permute-start(f16[2,256,1024]{2,1,0:T(8,128)(2,1)S(1)} %get-tuple-element.187), channel_id=1, source_target_pairs={{0,1},{1,0},{2,3},{3,2},{4,5},{5,4},{6,7},{7,6},{8,9},{9,8},{10,11... | collective-permute-start | bytes 3145736 | tf_op jit(solution)/shard_map/ppermute | solution.py:95
  29.7 19.1 %collective-permute-start.5 = (f16[2,128,1024]{2,1,0:T(8,128)(2,1)S(1)}, f16[2,128,1024]{2,1,0:T(8,128)(2,1)S(1)}, u32[]{:S(2)}, u32[]{:S(2)}) collective-permute-start(f16[2,128,1024]{2,1,0:T(8,128)(2,1)S(1)} %get-tuple-element.176), channel_id=1, source_target_pairs={{0,2},{1,3},{2,0},{3,1},{4,6},{5,7},{6,4},{7,5},{8,10},{9,11},{10,... | collective-permute-start | bytes 1572872 | tf_op jit(solution)/shard_map/ppermute | solution.py:95
  37.7 15.5 %collective-permute-start.3 = (f16[2,64,1024]{2,1,0:T(8,128)(2,1)S(1)}, f16[2,64,1024]{2,1,0:T(8,128)(2,1)S(1)}, u32[]{:S(2)}, u32[]{:S(2)}) collective-permute-start(f16[2,64,1024]{2,1,0:T(8,128)(2,1)S(1)} %get-tuple-element.200), channel_id=1, source_target_pairs={{0,4},{1,5},{2,6},{3,7},{4,0},{5,1},{6,2},{7,3},{8,12},{9,13},{10,... | collective-permute-start | bytes 786440 | tf_op jit(solution)/shard_map/ppermute | solution.py:95
  40.4 19.6 %collective-permute-start.10 = (f16[2,128,1024]{2,1,0:T(8,128)(2,1)S(1)}, f16[2,128,1024]{2,1,0:T(8,128)(2,1)S(1)}, u32[]{:S(2)}, u32[]{:S(2)}) collective-permute-start(f16[2,128,1024]{2,1,0:T(8,128)(2,1)S(1)} %get-tuple-element.179), channel_id=1, source_target_pairs={{0,2},{1,3},{2,0},{3,1},{4,6},{5,7},{6,4},{7,5},{8,10},{9,11},{10,... | collective-permute-start | bytes 1572872 | tf_op jit(solution)/shard_map/ppermute | solution.py:95
  48.9 15.5 %collective-permute-start.8 = (f16[2,64,1024]{2,1,0:T(8,128)(2,1)S(1)}, f16[2,64,1024]{2,1,0:T(8,128)(2,1)S(1)}, u32[]{:S(2)}, u32[]{:S(2)}) collective-permute-start(f16[2,64,1024]{2,1,0:T(8,128)(2,1)S(1)} %get-tuple-element.198), channel_id=1, source_target_pairs={{0,4},{1,5},{2,6},{3,7},{4,0},{5,1},{6,2},{7,3},{8,12},{9,13},{10,... | collective-permute-start | bytes 786440 | tf_op jit(solution)/shard_map/ppermute | solution.py:95
  51.6 19.6 %collective-permute-start.14 = (f16[2,128,1024]{2,1,0:T(8,128)(2,1)S(1)}, f16[2,128,1024]{2,1,0:T(8,128)(2,1)S(1)}, u32[]{:S(2)}, u32[]{:S(2)}) collective-permute-start(f16[2,128,1024]{2,1,0:T(8,128)(2,1)S(1)} %get-tuple-element.172), channel_id=1, source_target_pairs={{0,2},{1,3},{2,0},{3,1},{4,6},{5,7},{6,4},{7,5},{8,10},{9,11},{10,... | collective-permute-start | bytes 1572872 | tf_op jit(solution)/shard_map/ppermute | solution.py:95
  53.3 13.9 %collective-permute-start.7 = (f16[2,32,1024]{2,1,0:T(8,128)(2,1)S(1)}, f16[2,32,1024]{2,1,0:T(8,128)(2,1)S(1)}, u32[]{:S(2)}, u32[]{:S(2)}) collective-permute-start(f16[2,32,1024]{2,1,0:T(8,128)(2,1)S(1)} %get-tuple-element.210), channel_id=1, source_target_pairs={{0,8},{1,9},{2,10},{3,11},{4,12},{5,13},{6,14},{7,15},{8,0},{9,1},... | collective-permute-start | bytes 393224 | tf_op jit(solution)/shard_map/ppermute | solution.py:95
  60.2 13.4 %collective-permute-start.13 = (f16[2,64,1024]{2,1,0:T(8,128)(2,1)S(1)}, f16[2,64,1024]{2,1,0:T(8,128)(2,1)S(1)}, u32[]{:S(2)}, u32[]{:S(2)}) collective-permute-start(f16[2,64,1024]{2,1,0:T(8,128)(2,1)S(1)} %get-tuple-element.196), channel_id=1, source_target_pairs={{0,4},{1,5},{2,6},{3,7},{4,0},{5,1},{6,2},{7,3},{8,12},{9,13},{10,... | collective-permute-start | bytes 786440 | tf_op jit(solution)/shard_map/ppermute | solution.py:95
  62.3 49.1 %slice-start = ((s8[10485760]{0:T(1024)(128)(4,1)}), s8[4194304]{0:T(1024)(128)(4,1)S(1)}, s32[]{:S(2)}) async-start(s8[10485760]{0:T(1024)(128)(4,1)} %bitcast.83), calls=%async_computation | async-start | bytes 8388608
  62.8 19.1 %collective-permute-start.19 = (f16[2,128,1024]{2,1,0:T(8,128)(2,1)S(1)}, f16[2,128,1024]{2,1,0:T(8,128)(2,1)S(1)}, u32[]{:S(2)}, u32[]{:S(2)}) collective-permute-start(f16[2,128,1024]{2,1,0:T(8,128)(2,1)S(1)} %get-tuple-element.173), channel_id=1, source_target_pairs={{0,2},{1,3},{2,0},{3,1},{4,6},{5,7},{6,4},{7,5},{8,10},{9,11},{10,... | collective-permute-start | bytes 1572872 | tf_op jit(solution)/shard_map/ppermute | solution.py:95
  64.5 11.8 %collective-permute-start.12 = (f16[2,32,1024]{2,1,0:T(8,128)(2,1)S(1)}, f16[2,32,1024]{2,1,0:T(8,128)(2,1)S(1)}, u32[]{:S(2)}, u32[]{:S(2)}) collective-permute-start(f16[2,32,1024]{2,1,0:T(8,128)(2,1)S(1)} %get-tuple-element.208), channel_id=1, source_target_pairs={{0,8},{1,9},{2,10},{3,11},{4,12},{5,13},{6,14},{7,15},{8,0},{9,1},... | collective-permute-start | bytes 393224 | tf_op jit(solution)/shard_map/ppermute | solution.py:95
  67.3 9.6 %collective-permute-start.11 = (bf16[32,1024]{1,0:T(8,128)(2,1)S(1)}, bf16[32,1024]{1,0:T(8,128)(2,1)S(1)}, u32[]{:S(2)}, u32[]{:S(2)}) collective-permute-start(bf16[32,1024]{1,0:T(8,128)(2,1)S(1)} %fusion.53), channel_id=1, source_target_pairs={{0,8},{1,9},{2,10},{3,11},{4,12},{5,13},{6,14},{7,15},{8,0},{9,1},... | collective-permute-start | bytes 196616 | tf_op jit(solution)/shard_map/ppermute | solution.py:95
  71.2 40.2 %slice-start.1 = ((s8[10485760]{0:T(1024)(128)(4,1)}), s8[4194304]{0:T(1024)(128)(4,1)S(1)}, s32[]{:S(2)}) async-start(s8[10485760]{0:T(1024)(128)(4,1)} %bitcast.83), calls=%async_computation.1 | async-start | bytes 8388608
  71.4 13.6 %collective-permute-start.18 = (f16[2,64,1024]{2,1,0:T(8,128)(2,1)S(1)}, f16[2,64,1024]{2,1,0:T(8,128)(2,1)S(1)}, u32[]{:S(2)}, u32[]{:S(2)}) collective-permute-start(f16[2,64,1024]{2,1,0:T(8,128)(2,1)S(1)} %get-tuple-element.192), channel_id=1, source_target_pairs={{0,4},{1,5},{2,6},{3,7},{4,0},{5,1},{6,2},{7,3},{8,12},{9,13},{10,... | collective-permute-start | bytes 786440 | tf_op jit(solution)/shard_map/ppermute | solution.py:95
  73.7 13.1 %collective-permute-start.17 = (f16[2,32,1024]{2,1,0:T(8,128)(2,1)S(1)}, f16[2,32,1024]{2,1,0:T(8,128)(2,1)S(1)}, u32[]{:S(2)}, u32[]{:S(2)}) collective-permute-start(f16[2,32,1024]{2,1,0:T(8,128)(2,1)S(1)} %get-tuple-element.206), channel_id=1, source_target_pairs={{0,8},{1,9},{2,10},{3,11},{4,12},{5,13},{6,14},{7,15},{8,0},{9,1},... | collective-permute-start | bytes 393224 | tf_op jit(solution)/shard_map/ppermute | solution.py:95
  76.4 11.8 %collective-permute-start.16 = (bf16[32,1024]{1,0:T(8,128)(2,1)S(1)}, bf16[32,1024]{1,0:T(8,128)(2,1)S(1)}, u32[]{:S(2)}, u32[]{:S(2)}) collective-permute-start(bf16[32,1024]{1,0:T(8,128)(2,1)S(1)} %fusion.51), channel_id=1, source_target_pairs={{0,8},{1,9},{2,10},{3,11},{4,12},{5,13},{6,14},{7,15},{8,0},{9,1},... | collective-permute-start | bytes 196616 | tf_op jit(solution)/shard_map/ppermute | solution.py:95
  76.9 12.4 %collective-permute-start.15 = (bf16[64,1024]{1,0:T(8,128)(2,1)S(1)}, bf16[64,1024]{1,0:T(8,128)(2,1)S(1)}, u32[]{:S(2)}, u32[]{:S(2)}) collective-permute-start(bf16[64,1024]{1,0:T(8,128)(2,1)S(1)} %constant_dynamic-update-slice_fusion), channel_id=1, source_target_pairs={{0,4},{1,5},{2,6},{3,7},{4,0},{5,1},{6,2},{7,3},{8,12},{9,13},{10,... | collective-permute-start | bytes 393224 | tf_op jit(solution)/shard_map/ppermute | solution.py:95
  82.2 15.5 %collective-permute-start.24 = (f16[2,64,1024]{2,1,0:T(8,128)(2,1)S(1)}, f16[2,64,1024]{2,1,0:T(8,128)(2,1)S(1)}, u32[]{:S(2)}, u32[]{:S(2)}) collective-permute-start(f16[2,64,1024]{2,1,0:T(8,128)(2,1)S(1)} %get-tuple-element.193), channel_id=1, source_target_pairs={{0,4},{1,5},{2,6},{3,7},{4,0},{5,1},{6,2},{7,3},{8,12},{9,13},{10,... | collective-permute-start | bytes 786440 | tf_op jit(solution)/shard_map/ppermute | solution.py:95
  85.1 13.7 %collective-permute-start.23 = (f16[2,32,1024]{2,1,0:T(8,128)(2,1)S(1)}, f16[2,32,1024]{2,1,0:T(8,128)(2,1)S(1)}, u32[]{:S(2)}, u32[]{:S(2)}) collective-permute-start(f16[2,32,1024]{2,1,0:T(8,128)(2,1)S(1)} %get-tuple-element.202), channel_id=1, source_target_pairs={{0,8},{1,9},{2,10},{3,11},{4,12},{5,13},{6,14},{7,15},{8,0},{9,1},... | collective-permute-start | bytes 393224 | tf_op jit(solution)/shard_map/ppermute | solution.py:95
  86.9 24.6 %slice-start.2 = ((s8[10485760]{0:T(1024)(128)(4,1)}), s8[2097152]{0:T(1024)(128)(4,1)S(1)}, s32[]{:S(2)}) async-start(s8[10485760]{0:T(1024)(128)(4,1)} %bitcast.83), calls=%async_computation.2 | async-start | bytes 4194304
  86.9 14.0 %collective-permute-start.22 = (bf16[32,1024]{1,0:T(8,128)(2,1)S(1)}, bf16[32,1024]{1,0:T(8,128)(2,1)S(1)}, u32[]{:S(2)}, u32[]{:S(2)}) collective-permute-start(bf16[32,1024]{1,0:T(8,128)(2,1)S(1)} %fusion.49), channel_id=1, source_target_pairs={{0,8},{1,9},{2,10},{3,11},{4,12},{5,13},{6,14},{7,15},{8,0},{9,1},... | collective-permute-start | bytes 196616 | tf_op jit(solution)/shard_map/ppermute | solution.py:95
  88.3 13.5 %collective-permute-start.21 = (bf16[64,1024]{1,0:T(8,128)(2,1)S(1)}, bf16[64,1024]{1,0:T(8,128)(2,1)S(1)}, u32[]{:S(2)}, u32[]{:S(2)}) collective-permute-start(bf16[64,1024]{1,0:T(8,128)(2,1)S(1)} %constant_dynamic-update-slice_fusion.2), channel_id=1, source_target_pairs={{0,4},{1,5},{2,6},{3,7},{4,0},{5,1},{6,2},{7,3},{8,12},{9,13},{10,... | collective-permute-start | bytes 393224 | tf_op jit(solution)/shard_map/ppermute | solution.py:95
  89.3 14.1 %collective-permute-start.20 = (bf16[128,1024]{1,0:T(8,128)(2,1)S(1)}, bf16[128,1024]{1,0:T(8,128)(2,1)S(1)}, u32[]{:S(2)}, u32[]{:S(2)}) collective-permute-start(bf16[128,1024]{1,0:T(8,128)(2,1)S(1)} %constant_dynamic-update-slice_fusion.4), channel_id=1, source_target_pairs={{0,2},{1,3},{2,0},{3,1},{4,6},{5,7},{6,4},{7,5},{8,10},{9,11},{10,... | collective-permute-start | bytes 786440 | tf_op jit(solution)/shard_map/ppermute | solution.py:95
  97.7 9.6 %collective-permute-start.28 = (f16[2,32,1024]{2,1,0:T(8,128)(2,1)S(1)}, f16[2,32,1024]{2,1,0:T(8,128)(2,1)S(1)}, u32[]{:S(2)}, u32[]{:S(2)}) collective-permute-start(f16[2,32,1024]{2,1,0:T(8,128)(2,1)S(1)} %get-tuple-element.203), channel_id=1, source_target_pairs={{0,8},{1,9},{2,10},{3,11},{4,12},{5,13},{6,14},{7,15},{8,0},{9,1},... | collective-permute-start | bytes 393224 | tf_op jit(solution)/shard_map/ppermute | solution.py:95
  98.9 9.1 %collective-permute-start.27 = (bf16[32,1024]{1,0:T(8,128)(2,1)S(1)}, bf16[32,1024]{1,0:T(8,128)(2,1)S(1)}, u32[]{:S(2)}, u32[]{:S(2)}) collective-permute-start(bf16[32,1024]{1,0:T(8,128)(2,1)S(1)} %fusion.47), channel_id=1, source_target_pairs={{0,8},{1,9},{2,10},{3,11},{4,12},{5,13},{6,14},{7,15},{8,0},{9,1},... | collective-permute-start | bytes 196616 | tf_op jit(solution)/shard_map/ppermute | solution.py:95
  100.9 9.3 %collective-permute-start.26 = (bf16[64,1024]{1,0:T(8,128)(2,1)S(1)}, bf16[64,1024]{1,0:T(8,128)(2,1)S(1)}, u32[]{:S(2)}, u32[]{:S(2)}) collective-permute-start(bf16[64,1024]{1,0:T(8,128)(2,1)S(1)} %constant_dynamic-update-slice_fusion.6), channel_id=1, source_target_pairs={{0,4},{1,5},{2,6},{3,7},{4,0},{5,1},{6,2},{7,3},{8,12},{9,13},{10,... | collective-permute-start | bytes 393224 | tf_op jit(solution)/shard_map/ppermute | solution.py:95
  101.8 9.5 %collective-permute-start.25 = (bf16[128,1024]{1,0:T(8,128)(2,1)S(1)}, bf16[128,1024]{1,0:T(8,128)(2,1)S(1)}, u32[]{:S(2)}, u32[]{:S(2)}) collective-permute-start(bf16[128,1024]{1,0:T(8,128)(2,1)S(1)} %constant_dynamic-update-slice_fusion.8), channel_id=1, source_target_pairs={{0,2},{1,3},{2,0},{3,1},{4,6},{5,7},{6,4},{7,5},{8,10},{9,11},{10,... | collective-permute-start | bytes 786440 | tf_op jit(solution)/shard_map/ppermute | solution.py:95
  103.5 8.8 %collective-permute-start.32 = (bf16[256,1024]{1,0:T(8,128)(2,1)S(1)}, bf16[256,1024]{1,0:T(8,128)(2,1)S(1)}, u32[]{:S(2)}, u32[]{:S(2)}) collective-permute-start(bf16[256,1024]{1,0:T(8,128)(2,1)S(1)} %constant_dynamic-update-slice_fusion.10), channel_id=1, source_target_pairs={{0,1},{1,0},{2,3},{3,2},{4,5},{5,4},{6,7},{7,6},{8,9},{9,8},{10,11... | collective-permute-start | bytes 1572872 | tf_op jit(solution)/shard_map/ppermute | solution.py:95
  107.4 5.4 %collective-permute-start.31 = (bf16[32,1024]{1,0:T(8,128)(2,1)S(1)}, bf16[32,1024]{1,0:T(8,128)(2,1)S(1)}, u32[]{:S(2)}, u32[]{:S(2)}) collective-permute-start(bf16[32,1024]{1,0:T(8,128)(2,1)S(1)} %fusion.45), channel_id=1, source_target_pairs={{0,8},{1,9},{2,10},{3,11},{4,12},{5,13},{6,14},{7,15},{8,0},{9,1},... | collective-permute-start | bytes 196616 | tf_op jit(solution)/shard_map/ppermute | solution.py:95
  108.0 5.8 %collective-permute-start.30 = (bf16[64,1024]{1,0:T(8,128)(2,1)S(1)}, bf16[64,1024]{1,0:T(8,128)(2,1)S(1)}, u32[]{:S(2)}, u32[]{:S(2)}) collective-permute-start(bf16[64,1024]{1,0:T(8,128)(2,1)S(1)} %constant_dynamic-update-slice_fusion.12), channel_id=1, source_target_pairs={{0,4},{1,5},{2,6},{3,7},{4,0},{5,1},{6,2},{7,3},{8,12},{9,13},{10,... | collective-permute-start | bytes 393224 | tf_op jit(solution)/shard_map/ppermute | solution.py:95
  110.2 7.5 %collective-permute-start.29 = (bf16[128,1024]{1,0:T(8,128)(2,1)S(1)}, bf16[128,1024]{1,0:T(8,128)(2,1)S(1)}, u32[]{:S(2)}, u32[]{:S(2)}) collective-permute-start(bf16[128,1024]{1,0:T(8,128)(2,1)S(1)} %constant_dynamic-update-slice_fusion.14), channel_id=1, source_target_pairs={{0,2},{1,3},{2,0},{3,1},{4,6},{5,7},{6,4},{7,5},{8,10},{9,11},{10,... | collective-permute-start | bytes 786440 | tf_op jit(solution)/shard_map/ppermute | solution.py:95
  111.4 7.2 %collective-permute-start.35 = (bf16[256,1024]{1,0:T(8,128)(2,1)S(1)}, bf16[256,1024]{1,0:T(8,128)(2,1)S(1)}, u32[]{:S(2)}, u32[]{:S(2)}) collective-permute-start(bf16[256,1024]{1,0:T(8,128)(2,1)S(1)} %constant_dynamic-update-slice_fusion.16), channel_id=1, source_target_pairs={{0,1},{1,0},{2,3},{3,2},{4,5},{5,4},{6,7},{7,6},{8,9},{9,8},{10,11... | collective-permute-start | bytes 1572872 | tf_op jit(solution)/shard_map/ppermute | solution.py:95
  112.9 5.7 %collective-permute-start.34 = (bf16[64,1024]{1,0:T(8,128)(2,1)S(1)}, bf16[64,1024]{1,0:T(8,128)(2,1)S(1)}, u32[]{:S(2)}, u32[]{:S(2)}) collective-permute-start(bf16[64,1024]{1,0:T(8,128)(2,1)S(1)} %constant_dynamic-update-slice_fusion.18), channel_id=1, source_target_pairs={{0,4},{1,5},{2,6},{3,7},{4,0},{5,1},{6,2},{7,3},{8,12},{9,13},{10,... | collective-permute-start | bytes 393224 | tf_op jit(solution)/shard_map/ppermute | solution.py:95
  113.9 8.8 %collective-permute-start.33 = (bf16[128,1024]{1,0:T(8,128)(2,1)S(1)}, bf16[128,1024]{1,0:T(8,128)(2,1)S(1)}, u32[]{:S(2)}, u32[]{:S(2)}) collective-permute-start(bf16[128,1024]{1,0:T(8,128)(2,1)S(1)} %constant_dynamic-update-slice_fusion.20), channel_id=1, source_target_pairs={{0,2},{1,3},{2,0},{3,1},{4,6},{5,7},{6,4},{7,5},{8,10},{9,11},{10,... | collective-permute-start | bytes 786440 | tf_op jit(solution)/shard_map/ppermute | solution.py:95
  117.8 6.5 %collective-permute-start.37 = (bf16[256,1024]{1,0:T(8,128)(2,1)S(1)}, bf16[256,1024]{1,0:T(8,128)(2,1)S(1)}, u32[]{:S(2)}, u32[]{:S(2)}) collective-permute-start(bf16[256,1024]{1,0:T(8,128)(2,1)S(1)} %constant_dynamic-update-slice_fusion.22), channel_id=1, source_target_pairs={{0,1},{1,0},{2,3},{3,2},{4,5},{5,4},{6,7},{7,6},{8,9},{9,8},{10,11... | collective-permute-start | bytes 1572872 | tf_op jit(solution)/shard_map/ppermute | solution.py:95
  118.6 9.3 %collective-permute-start.36 = (bf16[128,1024]{1,0:T(8,128)(2,1)S(1)}, bf16[128,1024]{1,0:T(8,128)(2,1)S(1)}, u32[]{:S(2)}, u32[]{:S(2)}) collective-permute-start(bf16[128,1024]{1,0:T(8,128)(2,1)S(1)} %constant_dynamic-update-slice_fusion.24), channel_id=1, source_target_pairs={{0,2},{1,3},{2,0},{3,1},{4,6},{5,7},{6,4},{7,5},{8,10},{9,11},{10,... | collective-permute-start | bytes 786440 | tf_op jit(solution)/shard_map/ppermute | solution.py:95
  122.8 6.8 %collective-permute-start.38 = (bf16[256,1024]{1,0:T(8,128)(2,1)S(1)}, bf16[256,1024]{1,0:T(8,128)(2,1)S(1)}, u32[]{:S(2)}, u32[]{:S(2)}) collective-permute-start(bf16[256,1024]{1,0:T(8,128)(2,1)S(1)} %constant_dynamic-update-slice_fusion.26), channel_id=1, source_target_pairs={{0,1},{1,0},{2,3},{3,2},{4,5},{5,4},{6,7},{7,6},{8,9},{9,8},{10,11... | collective-permute-start | bytes 1572872 | tf_op jit(solution)/shard_map/ppermute | solution.py:95
  127.9 3.2 %collective-permute-start.39 = (bf16[256,1024]{1,0:T(8,128)(2,1)S(1)}, bf16[256,1024]{1,0:T(8,128)(2,1)S(1)}, u32[]{:S(2)}, u32[]{:S(2)}) collective-permute-start(bf16[256,1024]{1,0:T(8,128)(2,1)S(1)} %constant_dynamic-update-slice_fusion.28), channel_id=1, source_target_pairs={{0,1},{1,0},{2,3},{3,2},{4,5},{5,4},{6,7},{7,6},{8,9},{9,8},{10,11... | collective-permute-start | bytes 1572872 | tf_op jit(solution)/shard_map/ppermute | solution.py:95

commit v3 on v2

--- a/solution.py
+++ b/solution.py
@@ -9,6 +9,9 @@
 
 F16, F32, BF16 = jnp.float16, jnp.float32, jnp.bfloat16
 PARTS = (4,4,4,4,4)
+SUM_Z_FIRST = (1,)
+GATHER_Z_LAST = ()
+EARLY = ((2, 1),)
 SCALE = 4.0
 FREE = pl.CostEstimate(flops=0, bytes_accessed=0, transcendentals=0)
 
@@ -21,9 +24,9 @@
 
 
 def schedule(levels, chunks):
-    steps = [(0, 0), (1, 0), (0, 1), *((c, 0) for c in range(2, chunks)), (1, 1)]
+    steps = [(0, 0), (1, 0), (0, 1), *((c, 0) for c in range(2, chunks)), (1, 1), *EARLY]
     for tick in range(chunks + 2 * levels):
-        steps += [(tick, 2), (tick + 2, 1), *((tick + 2 - s, s) for s in range(3, 2 * levels + 1))]
+        steps += [(tick, 2), *(() if (tick + 2, 1) in EARLY else ((tick + 2, 1),)), *((tick + 2 - s, s) for s in range(3, 2 * levels + 1))]
     return [(c, s) for c, s in steps if 0 <= c < chunks]
 
 
@@ -94,9 +97,21 @@
     def swap(v, mask):
         return lax.ppermute(v, "gx", [(i, i ^ mask) for i in range(n)])
 
-    def split(v):
-        half = v.shape[1] // 2
-        return v[:, :half], v[:, half:]
+    def split(v, level):
+        first, rows, w = v.shape
+        v = v.reshape(first, 2**level, 2, rows >> (level + 1), w)
+        return (v[:, :, k].reshape(first, rows // 2, w) for k in (0, 1))
+
+    def turned(chunks):
+        turn = [0, 2, 1, *range(3, levels)] if levels > 2 else list(range(levels))
+        return [turn if c in chunks else list(range(levels)) for c in range(len(PARTS))]
+
+    sums, gathers = turned(SUM_Z_FIRST), turned(GATHER_Z_LAST)
+
+    def join(parts, inner):
+        if inner:
+            parts = [half for pair in zip(*(jnp.split(v, 2) for v in parts)) for half in pair]
+        return jnp.concatenate(parts, axis=0)
 
     def add(v, got):
         return v.astype(F32) + got.astype(F32)
@@ -111,30 +126,33 @@
             ins, _ = lax.optimization_barrier((ins, last))
         if stage == 0:
             acc = jnp.stack([ins[0][:, cols], ins[1][:, cols]])
-            keep, send = split(acc)
+            keep, send = split(acc, 0)
         elif stage < levels:
-            (keep, send), (got_keep, got_send) = split(ins[0]), split(ins[1])
+            skip = 1 if sums[c][stage] > stage else 0
+            (keep, send), (got_keep, got_send) = split(ins[0], skip), split(ins[1], skip)
             keep, send = add(keep, got_keep), add(send, got_send)
         if stage < levels:
             send = send.astype(F16)
-            state[c] = (keep, swap(send, masks[stage]))
+            state[c] = (keep, swap(send, masks[sums[c][stage]]))
             last = send
         elif stage == levels:
             acc = add(*ins) * (1 / SCALE)
             last = (jax.nn.silu(acc[0]) * acc[1]).astype(BF16)
             state[c] = (last, swap(last, masks[-1]))
         elif stage < 2 * levels:
-            last = jnp.concatenate(ins, axis=0)
-            state[c] = (last, swap(last, masks[2 * levels - 1 - stage]))
+            level = 2 * levels - stage
+            last = join(ins, gathers[c][level] > level)
+            state[c] = (last, swap(last, masks[gathers[c][level - 1]]))
             if stage == 2 * levels - 1:
                 lo = jnp.dot(last, down_weight[cols], preferred_element_type=F32)
                 total[0] = lo if total[0] is None else total[0] + lo
+                last = (last, total[0])
         elif c == final:
             result = finish(order, total[0], total[1], ins[1], down_weight)
         else:
             hi = jnp.dot(ins[1], down_weight[cols], preferred_element_type=F32)
             total[1] = hi if total[1] is None else total[1] + hi
-            last = ins[1]
+            last = total[1]
     return result
 
 

time: 133 us -> 128 us (0.962)
  waiting for transfers between devices: 47.5 us -> 44.2 us
  starting transfers between devices: 48.5 us -> 46.2 us
    ppermute x40, waiting for transfers between devices: 47.5 us -> 44.2 us  [swap(): return lax.ppermute(v, 'gx', [(i, i ^ mask) for i in range(n)])]
    another operation x9 -> x0, local copies, waits for them, and re-layouts: 2.73 us -> none  [on_device(): acc = jnp.stack([ins[0][:, cols], ins[1][:, cols]])]
    slice x0 -> x10, local copies, waits for them, and re-layouts: none -> 2.64 us  [on_device(): acc = jnp.stack([ins[0][:, cols], ins[1][:, cols]])]
    ppermute x40, starting transfers between devices: 48.5 us -> 46.2 us  [swap(): return lax.ppermute(v, 'gx', [(i, i ^ mask) for i in range(n)])]
    add x11 -> x12, other arithmetic: 2.43 us -> 2.95 us  [add(): return v.astype(F32) + got.astype(F32)]
where the time goes in v3:
time: 128 us
  starting transfers between devices  46.2 us (36%)
  waiting for transfers between devices  44.2 us (35%)
  matrix products  21.3 us (17%)
  other arithmetic  7.42 us (6%)
  Pallas kernels  4.42 us (3%)
  local copies, waits for them, and re-layouts  3.02 us (2%)
    ppermute x40, starting transfers between devices, swap(): return lax.ppermute(v, 'gx', [(i, i ^ mask) for i in range(n)])  46.2 us
    ppermute x40, waiting for transfers between devices, swap(): return lax.ppermute(v, 'gx', [(i, i ^ mask) for i in range(n)])  44.2 us
    dot_general x2, matrix products, on_device(): jnp.dot(x, v, preferred_element_type=F32).astype(F16)  14.8 us
    dot_general x5, matrix products, on_device(): lo = jnp.dot(last, down_weight[cols], preferred_element_type=F32)  3.65 us
    another operation x5, other arithmetic, split(): return (v[:, :, k].reshape(first, rows // 2, w) for k in (0, 1))  3.32 us
    add x12, other arithmetic, add(): return v.astype(F32) + got.astype(F32)  2.95 us
    dot_general x4, matrix products, on_device(): hi = jnp.dot(ins[1], down_weight[cols], preferred_element_type=F32)  2.94 us
    slice x10, local copies, waits for them, and re-layouts, on_device(): acc = jnp.stack([ins[0][:, cols], ins[1][:, cols]])  2.64 us
  transfers between devices with their start and end apart: 40, of which 16 were waited for; matrix products, arithmetic and copies ran while one was open for 12% of the time, Pallas kernels for 0%

profile of v3, /device:TPU:0, one launch (start us, length us, event | category | flops | bytes accessed | tf_op | source)
XLA Modules:
  0.0 127.6 jit_solution(15772449050063236241)
XLA Ops:
  0.0 2.4 %shard_map.46 = bf16[512,1024]{1,0:T(8,128)(2,1)} custom-call(bf16[512,1024]{1,0:T(8,128)(2,1)} %x_ref.1), custom_call_target="tpu_custom_call" | custom-call | tf_op jit(solution)/shard_map/pallas_call | solution.py:42
  2.5 8.7 %convolution_convert_fusion = f16[512,5120]{1,0:T(8,128)(2,1)S(1)} fusion(bf16[512,1024]{1,0:T(8,128)(2,1)} %shard_map.46, bf16[1024,5120]{1,0:T(8,128)(2,1)} %param.6), kind=kOutput, calls=%fused_computation | convolution fusion | flops 5371330560 | bytes 16777216 | tf_op jit(solution)/shard_map/dot_general | solution.py:120
  11.5 6.0 %convolution_convert_fusion.1 = f16[512,5120]{1,0:T(8,128)(2,1)S(1)} fusion(bf16[512,1024]{1,0:T(8,128)(2,1)S(1)} %copy-done, bf16[1024,5120]{1,0:T(8,128)(2,1)S(1)} %bitcast.367), kind=kOutput, calls=%fused_computation.1 | convolution fusion | flops 5371330560 | bytes 16777216 | tf_op jit(solution)/shard_map/dot_general | solution.py:120
  17.8 0.6 fusion.53
  18.5 0.5 collective-permute-start
  19.5 0.7 fusion.51
  20.4 0.9 collective-permute-done
  21.3 0.5 fusion.54
  22.3 0.7 fusion.52
  23.4 2.7 %collective-permute-start.1 = (f16[2,128,1024]{2,1,0:T(8,128)(2,1)S(1)}, f16[2,128,1024]{2,1,0:T(8,128)(2,1)S(1)}, u32[]{:S(2)}, u32[]{:S(2)}) collective-permute-start(f16[2,128,1024]{2,1,0:T(8,128)(2,1)S(1)} %get-tuple-element.187), channel_id=1, source_target_pairs={{0,2},{1,3},{2,0},{3,1},{4,6},{5,7},{6,4},{7,5},{8,10},{9,11},{10,... | collective-permute-start | bytes 1572872 | tf_op jit(solution)/shard_map/ppermute | solution.py:98
  26.6 0.7 fusion.50
  28.0 0.7 fusion.49
  28.6 0.5 collective-permute-start.9
  29.1 0.5 convert_add_fusion
  29.6 1.6 %collective-permute-start.6 = (f16[2,128,1024]{2,1,0:T(8,128)(2,1)S(1)}, f16[2,128,1024]{2,1,0:T(8,128)(2,1)S(1)}, u32[]{:S(2)}, u32[]{:S(2)}) collective-permute-start(f16[2,128,1024]{2,1,0:T(8,128)(2,1)S(1)} %bitcast.355), channel_id=1, source_target_pairs={{0,4},{1,5},{2,6},{3,7},{4,0},{5,1},{6,2},{7,3},{8,12},{9,13},{10,... | collective-permute-start | bytes 1572872 | tf_op jit(solution)/shard_map/ppermute | solution.py:98
  31.3 0.5 add_bitcast_fusion.2
  31.7 0.6 collective-permute-start.10
  32.3 6.5 %collective-permute-done.1 = f16[2,128,1024]{2,1,0:T(8,128)(2,1)S(1)} collective-permute-done((f16[2,128,1024]{2,1,0:T(8,128)(2,1)S(1)}, f16[2,128,1024]{2,1,0:T(8,128)(2,1)S(1)}, u32[]{:S(2)}, u32[]{:S(2)}) %collective-permute-start.1) | collective-permute-done | bytes 524320 | tf_op jit(solution)/shard_map/ppermute | solution.py:98
  39.0 2.1 %collective-permute-start.4 = (f16[2,64,1024]{2,1,0:T(8,128)(2,1)S(1)}, f16[2,64,1024]{2,1,0:T(8,128)(2,1)S(1)}, u32[]{:S(2)}, u32[]{:S(2)}) collective-permute-start(f16[2,64,1024]{2,1,0:T(8,128)(2,1)S(1)} %get-tuple-element.199), channel_id=1, source_target_pairs={{0,4},{1,5},{2,6},{3,7},{4,0},{5,1},{6,2},{7,3},{8,12},{9,13},{10,... | collective-permute-start | bytes 786440 | tf_op jit(solution)/shard_map/ppermute | solution.py:98
  41.1 3.4 %collective-permute-done.6 = f16[2,128,1024]{2,1,0:T(8,128)(2,1)S(1)} collective-permute-done((f16[2,128,1024]{2,1,0:T(8,128)(2,1)S(1)}, f16[2,128,1024]{2,1,0:T(8,128)(2,1)S(1)}, u32[]{:S(2)}, u32[]{:S(2)}) %collective-permute-start.6) | collective-permute-done | bytes 524320 | tf_op jit(solution)/shard_map/ppermute | solution.py:98
  44.7 0.5 add_bitcast_fusion.1
  45.2 2.1 %collective-permute-start.14 = (f16[2,128,1024]{2,1,0:T(8,128)(2,1)S(1)}, f16[2,128,1024]{2,1,0:T(8,128)(2,1)S(1)}, u32[]{:S(2)}, u32[]{:S(2)}) collective-permute-start(f16[2,128,1024]{2,1,0:T(8,128)(2,1)S(1)} %get-tuple-element.174), channel_id=1, source_target_pairs={{0,2},{1,3},{2,0},{3,1},{4,6},{5,7},{6,4},{7,5},{8,10},{9,11},{10,... | collective-permute-start | bytes 1572872 | tf_op jit(solution)/shard_map/ppermute | solution.py:98
  47.3 1.9 %collective-permute-done.4 = f16[2,64,1024]{2,1,0:T(8,128)(2,1)S(1)} collective-permute-done((f16[2,64,1024]{2,1,0:T(8,128)(2,1)S(1)}, f16[2,64,1024]{2,1,0:T(8,128)(2,1)S(1)}, u32[]{:S(2)}, u32[]{:S(2)}) %collective-permute-start.4) | collective-permute-done | bytes 262176 | tf_op jit(solution)/shard_map/ppermute | solution.py:98
  49.3 2.6 %collective-permute-start.7 = (f16[2,32,1024]{2,1,0:T(8,128)(2,1)S(1)}, f16[2,32,1024]{2,1,0:T(8,128)(2,1)S(1)}, u32[]{:S(2)}, u32[]{:S(2)}) collective-permute-start(f16[2,32,1024]{2,1,0:T(8,128)(2,1)S(1)} %get-tuple-element.209), channel_id=1, source_target_pairs={{0,8},{1,9},{2,10},{3,11},{4,12},{5,13},{6,14},{7,15},{8,0},{9,1},... | collective-permute-start | bytes 393224 | tf_op jit(solution)/shard_map/ppermute | solution.py:98
  52.1 1.6 %collective-permute-start.13 = (f16[2,64,1024]{2,1,0:T(8,128)(2,1)S(1)}, f16[2,64,1024]{2,1,0:T(8,128)(2,1)S(1)}, u32[]{:S(2)}, u32[]{:S(2)}) collective-permute-start(f16[2,64,1024]{2,1,0:T(8,128)(2,1)S(1)} %get-tuple-element.196), channel_id=1, source_target_pairs={{0,4},{1,5},{2,6},{3,7},{4,0},{5,1},{6,2},{7,3},{8,12},{9,13},{10,... | collective-permute-start | bytes 786440 | tf_op jit(solution)/shard_map/ppermute | solution.py:98
  54.2 0.6 collective-permute-start.19
  54.8 0.9 collective-permute-done.8
  55.8 3.1 %collective-permute-start.12 = (f16[2,32,1024]{2,1,0:T(8,128)(2,1)S(1)}, f16[2,32,1024]{2,1,0:T(8,128)(2,1)S(1)}, u32[]{:S(2)}, u32[]{:S(2)}) collective-permute-start(f16[2,32,1024]{2,1,0:T(8,128)(2,1)S(1)} %get-tuple-element.208), channel_id=1, source_target_pairs={{0,8},{1,9},{2,10},{3,11},{4,12},{5,13},{6,14},{7,15},{8,0},{9,1},... | collective-permute-start | bytes 393224 | tf_op jit(solution)/shard_map/ppermute | solution.py:98
  59.4 7.6 %collective-permute-done.14 = f16[2,128,1024]{2,1,0:T(8,128)(2,1)S(1)} collective-permute-done((f16[2,128,1024]{2,1,0:T(8,128)(2,1)S(1)}, f16[2,128,1024]{2,1,0:T(8,128)(2,1)S(1)}, u32[]{:S(2)}, u32[]{:S(2)}) %collective-permute-start.14) | collective-permute-done | bytes 524320 | tf_op jit(solution)/shard_map/ppermute | solution.py:98
  67.1 2.1 %collective-permute-start.18 = (f16[2,64,1024]{2,1,0:T(8,128)(2,1)S(1)}, f16[2,64,1024]{2,1,0:T(8,128)(2,1)S(1)}, u32[]{:S(2)}, u32[]{:S(2)}) collective-permute-start(f16[2,64,1024]{2,1,0:T(8,128)(2,1)S(1)} %get-tuple-element.194), channel_id=1, source_target_pairs={{0,4},{1,5},{2,6},{3,7},{4,0},{5,1},{6,2},{7,3},{8,12},{9,13},{10,... | collective-permute-start | bytes 786440 | tf_op jit(solution)/shard_map/ppermute | solution.py:98
  69.3 2.7 %collective-permute-start.17 = (f16[2,32,1024]{2,1,0:T(8,128)(2,1)S(1)}, f16[2,32,1024]{2,1,0:T(8,128)(2,1)S(1)}, u32[]{:S(2)}, u32[]{:S(2)}) collective-permute-start(f16[2,32,1024]{2,1,0:T(8,128)(2,1)S(1)} %get-tuple-element.206), channel_id=1, source_target_pairs={{0,8},{1,9},{2,10},{3,11},{4,12},{5,13},{6,14},{7,15},{8,0},{9,1},... | collective-permute-start | bytes 393224 | tf_op jit(solution)/shard_map/ppermute | solution.py:98
  72.7 5.1 %collective-permute-done.19 = f16[2,128,1024]{2,1,0:T(8,128)(2,1)S(1)} collective-permute-done((f16[2,128,1024]{2,1,0:T(8,128)(2,1)S(1)}, f16[2,128,1024]{2,1,0:T(8,128)(2,1)S(1)}, u32[]{:S(2)}, u32[]{:S(2)}) %collective-permute-start.19) | collective-permute-done | bytes 524320 | tf_op jit(solution)/shard_map/ppermute | solution.py:98
  78.0 1.9 %collective-permute-start.24 = (f16[2,64,1024]{2,1,0:T(8,128)(2,1)S(1)}, f16[2,64,1024]{2,1,0:T(8,128)(2,1)S(1)}, u32[]{:S(2)}, u32[]{:S(2)}) collective-permute-start(f16[2,64,1024]{2,1,0:T(8,128)(2,1)S(1)} %get-tuple-element.192), channel_id=1, source_target_pairs={{0,4},{1,5},{2,6},{3,7},{4,0},{5,1},{6,2},{7,3},{8,12},{9,13},{10,... | collective-permute-start | bytes 786440 | tf_op jit(solution)/shard_map/ppermute | solution.py:98
  79.9 0.6 collective-permute-done.18
  80.6 2.1 %collective-permute-start.23 = (f16[2,32,1024]{2,1,0:T(8,128)(2,1)S(1)}, f16[2,32,1024]{2,1,0:T(8,128)(2,1)S(1)}, u32[]{:S(2)}, u32[]{:S(2)}) collective-permute-start(f16[2,32,1024]{2,1,0:T(8,128)(2,1)S(1)} %get-tuple-element.204), channel_id=1, source_target_pairs={{0,8},{1,9},{2,10},{3,11},{4,12},{5,13},{6,14},{7,15},{8,0},{9,1},... | collective-permute-start | bytes 393224 | tf_op jit(solution)/shard_map/ppermute | solution.py:98
  82.7 1.0 collective-permute-start.22
  83.7 1.3 %collective-permute-start.21 = (bf16[64,1024]{1,0:T(8,128)(2,1)S(1)}, bf16[64,1024]{1,0:T(8,128)(2,1)S(1)}, u32[]{:S(2)}, u32[]{:S(2)}) collective-permute-start(bf16[64,1024]{1,0:T(8,128)(2,1)S(1)} %constant_dynamic-update-slice_fusion.2), channel_id=1, source_target_pairs={{0,4},{1,5},{2,6},{3,7},{4,0},{5,1},{6,2},{7,3},{8,12},{9,13},{10,... | collective-permute-start | bytes 393224 | tf_op jit(solution)/shard_map/ppermute | solution.py:98
  85.1 1.6 %collective-permute-start.20 = (bf16[128,1024]{1,0:T(8,128)(2,1)S(1)}, bf16[128,1024]{1,0:T(8,128)(2,1)S(1)}, u32[]{:S(2)}, u32[]{:S(2)}) collective-permute-start(bf16[128,1024]{1,0:T(8,128)(2,1)S(1)} %constant_dynamic-update-slice_fusion.4), channel_id=1, source_target_pairs={{0,2},{1,3},{2,0},{3,1},{4,6},{5,7},{6,4},{7,5},{8,10},{9,11},{10,... | collective-permute-start | bytes 786440 | tf_op jit(solution)/shard_map/ppermute | solution.py:98
  86.7 6.4 %collective-permute-done.24 = f16[2,64,1024]{2,1,0:T(8,128)(2,1)S(1)} collective-permute-done((f16[2,64,1024]{2,1,0:T(8,128)(2,1)S(1)}, f16[2,64,1024]{2,1,0:T(8,128)(2,1)S(1)}, u32[]{:S(2)}, u32[]{:S(2)}) %collective-permute-start.24) | collective-permute-done | bytes 262176 | tf_op jit(solution)/shard_map/ppermute | solution.py:98
  93.1 1.8 %collective-permute-start.28 = (f16[2,32,1024]{2,1,0:T(8,128)(2,1)S(1)}, f16[2,32,1024]{2,1,0:T(8,128)(2,1)S(1)}, u32[]{:S(2)}, u32[]{:S(2)}) collective-permute-start(f16[2,32,1024]{2,1,0:T(8,128)(2,1)S(1)} %get-tuple-element.202), channel_id=1, source_target_pairs={{0,8},{1,9},{2,10},{3,11},{4,12},{5,13},{6,14},{7,15},{8,0},{9,1},... | collective-permute-start | bytes 393224 | tf_op jit(solution)/shard_map/ppermute | solution.py:98
  95.0 1.3 collective-permute-start.27
  96.3 1.4 %collective-permute-start.26 = (bf16[64,1024]{1,0:T(8,128)(2,1)S(1)}, bf16[64,1024]{1,0:T(8,128)(2,1)S(1)}, u32[]{:S(2)}, u32[]{:S(2)}) collective-permute-start(bf16[64,1024]{1,0:T(8,128)(2,1)S(1)} %constant_dynamic-update-slice_fusion.6), channel_id=1, source_target_pairs={{0,4},{1,5},{2,6},{3,7},{4,0},{5,1},{6,2},{7,3},{8,12},{9,13},{10,... | collective-permute-start | bytes 393224 | tf_op jit(solution)/shard_map/ppermute | solution.py:98
  97.7 1.6 %collective-permute-start.25 = (bf16[128,1024]{1,0:T(8,128)(2,1)S(1)}, bf16[128,1024]{1,0:T(8,128)(2,1)S(1)}, u32[]{:S(2)}, u32[]{:S(2)}) collective-permute-start(bf16[128,1024]{1,0:T(8,128)(2,1)S(1)} %constant_dynamic-update-slice_fusion.8), channel_id=1, source_target_pairs={{0,2},{1,3},{2,0},{3,1},{4,6},{5,7},{6,4},{7,5},{8,10},{9,11},{10,... | collective-permute-start | bytes 786440 | tf_op jit(solution)/shard_map/ppermute | solution.py:98
  99.7 0.7 fusion.16
  100.4 1.9 %collective-permute-done.28 = f16[2,32,1024]{2,1,0:T(8,128)(2,1)S(1)} collective-permute-done((f16[2,32,1024]{2,1,0:T(8,128)(2,1)S(1)}, f16[2,32,1024]{2,1,0:T(8,128)(2,1)S(1)}, u32[]{:S(2)}, u32[]{:S(2)}) %collective-permute-start.28) | collective-permute-done | bytes 131104 | tf_op jit(solution)/shard_map/ppermute | solution.py:98
  102.4 1.0 collective-permute-start.31
  103.5 2.3 %collective-permute-start.30 = (bf16[64,1024]{1,0:T(8,128)(2,1)S(1)}, bf16[64,1024]{1,0:T(8,128)(2,1)S(1)}, u32[]{:S(2)}, u32[]{:S(2)}) collective-permute-start(bf16[64,1024]{1,0:T(8,128)(2,1)S(1)} %constant_dynamic-update-slice_fusion.12), channel_id=1, source_target_pairs={{0,4},{1,5},{2,6},{3,7},{4,0},{5,1},{6,2},{7,3},{8,12},{9,13},{10,... | collective-permute-start | bytes 393224 | tf_op jit(solution)/shard_map/ppermute | solution.py:98
  105.9 1.6 %collective-permute-start.29 = (bf16[128,1024]{1,0:T(8,128)(2,1)S(1)}, bf16[128,1024]{1,0:T(8,128)(2,1)S(1)}, u32[]{:S(2)}, u32[]{:S(2)}) collective-permute-start(bf16[128,1024]{1,0:T(8,128)(2,1)S(1)} %constant_dynamic-update-slice_fusion.14), channel_id=1, source_target_pairs={{0,2},{1,3},{2,0},{3,1},{4,6},{5,7},{6,4},{7,5},{8,10},{9,11},{10,... | collective-permute-start | bytes 786440 | tf_op jit(solution)/shard_map/ppermute | solution.py:98
  107.6 0.7 fusion.18
  108.3 0.7 fusion.14
  109.2 0.7 collective-permute-done.30
  109.9 1.2 collective-permute-start.33
  111.1 1.2 collective-permute-done.29
  112.4 0.7 fusion.24
  113.2 0.7 fusion.21
  113.9 1.1 collective-permute-done.34
  115.1 1.3 %collective-permute-start.36 = (bf16[128,1024]{1,0:T(8,128)(2,1)S(1)}, bf16[128,1024]{1,0:T(8,128)(2,1)S(1)}, u32[]{:S(2)}, u32[]{:S(2)}) collective-permute-start(bf16[128,1024]{1,0:T(8,128)(2,1)S(1)} %constant_dynamic-update-slice_fusion.24), channel_id=1, source_target_pairs={{0,2},{1,3},{2,0},{3,1},{4,6},{5,7},{6,4},{7,5},{8,10},{9,11},{10,... | collective-permute-start | bytes 786440 | tf_op jit(solution)/shard_map/ppermute | solution.py:98
  116.4 1.7 %collective-permute-done.33 = bf16[128,1024]{1,0:T(8,128)(2,1)S(1)} collective-permute-done((bf16[128,1024]{1,0:T(8,128)(2,1)S(1)}, bf16[128,1024]{1,0:T(8,128)(2,1)S(1)}, u32[]{:S(2)}, u32[]{:S(2)}) %collective-permute-start.33) | collective-permute-done | bytes 262176 | tf_op jit(solution)/shard_map/ppermute | solution.py:98
  118.3 0.7 fusion.30
  119.0 0.7 fusion.27
  119.8 3.8 %collective-permute-done.36 = bf16[128,1024]{1,0:T(8,128)(2,1)S(1)} collective-permute-done((bf16[128,1024]{1,0:T(8,128)(2,1)S(1)}, bf16[128,1024]{1,0:T(8,128)(2,1)S(1)}, u32[]{:S(2)}, u32[]{:S(2)}) %collective-permute-start.36) | collective-permute-done | bytes 262176 | tf_op jit(solution)/shard_map/ppermute | solution.py:98
  123.7 0.7 fusion.36.lo_ref
  124.5 0.7 fusion.33.hi_ref
  125.6 2.0 %shard_map.47 = bf16[512,1024]{1,0:T(8,128)(2,1)} custom-call(f32[256,1024]{1,0:T(8,128)S(1)} %fusion.36.lo_ref, f32[256,1024]{1,0:T(8,128)S(1)} %fusion.33.hi_ref, bf16[256,1024]{1,0:T(8,128)(2,1)S(1)} %collective-permute-done.39.hidden_ref, bf16[5120,1024]{1,0:T(8,128)(2,1)S(1)} %bitcast.324), custom_call_target="tpu_custom_call" | custom-call | tf_op jit(solution)/shard_map/pallas_call | solution.py:69
  (115 shorter events, 7.9 us)
Async XLA Ops:
  0.0 11.5 %slice-start.3 = ((s8[10485760]{0:T(1024)(128)(4,1)}), s8[2097152]{0:T(1024)(128)(4,1)S(1)}, s32[]{:S(2)}) async-start(s8[10485760]{0:T(1024)(128)(4,1)} %bitcast.366), calls=%async_computation.3 | async-start | bytes 4194304
  2.4 9.0 %copy-start = (bf16[512,1024]{1,0:T(8,128)(2,1)S(1)}, bf16[512,1024]{1,0:T(8,128)(2,1)}, u32[]{:S(2)}) copy-start(bf16[512,1024]{1,0:T(8,128)(2,1)} %shard_map.46) | copy-start | bytes 3145732
  2.4 9.0 %slice-start.4 = ((s8[10485760]{0:T(1024)(128)(4,1)}), s8[4194304]{0:T(1024)(128)(4,1)S(1)}, s32[]{:S(2)}) async-start(s8[10485760]{0:T(1024)(128)(4,1)} %bitcast.366), calls=%async_computation.4 | async-start | bytes 8388608
  2.4 9.0 %slice-start.5 = ((s8[10485760]{0:T(1024)(128)(4,1)}), s8[4194304]{0:T(1024)(128)(4,1)S(1)}, s32[]{:S(2)}) async-start(s8[10485760]{0:T(1024)(128)(4,1)} %bitcast.366), calls=%async_computation.5 | async-start | bytes 8388608
  18.5 2.8 %collective-permute-start = (f16[2,256,1024]{2,1,0:T(8,128)(2,1)S(1)}, f16[2,256,1024]{2,1,0:T(8,128)(2,1)S(1)}, u32[]{:S(2)}, u32[]{:S(2)}) collective-permute-start(f16[2,256,1024]{2,1,0:T(8,128)(2,1)S(1)} %get-tuple-element.189), channel_id=1, source_target_pairs={{0,1},{1,0},{2,3},{3,2},{4,5},{5,4},{6,7},{7,6},{8,9},{9,8},{10,11... | collective-permute-start | bytes 3145736 | tf_op jit(solution)/shard_map/ppermute | solution.py:98
  20.2 8.9 %collective-permute-start.3 = (f16[2,256,1024]{2,1,0:T(8,128)(2,1)S(1)}, f16[2,256,1024]{2,1,0:T(8,128)(2,1)S(1)}, u32[]{:S(2)}, u32[]{:S(2)}) collective-permute-start(f16[2,256,1024]{2,1,0:T(8,128)(2,1)S(1)} %get-tuple-element.184), channel_id=1, source_target_pairs={{0,1},{1,0},{2,3},{3,2},{4,5},{5,4},{6,7},{7,6},{8,9},{9,8},{10,11... | collective-permute-start | bytes 3145736 | tf_op jit(solution)/shard_map/ppermute | solution.py:98
  23.0 8.3 %collective-permute-start.2 = (f16[2,256,1024]{2,1,0:T(8,128)(2,1)S(1)}, f16[2,256,1024]{2,1,0:T(8,128)(2,1)S(1)}, u32[]{:S(2)}, u32[]{:S(2)}) collective-permute-start(f16[2,256,1024]{2,1,0:T(8,128)(2,1)S(1)} %get-tuple-element.185), channel_id=1, source_target_pairs={{0,1},{1,0},{2,3},{3,2},{4,5},{5,4},{6,7},{7,6},{8,9},{9,8},{10,11... | collective-permute-start | bytes 3145736 | tf_op jit(solution)/shard_map/ppermute | solution.py:98
  23.4 15.4 %collective-permute-start.1 = (f16[2,128,1024]{2,1,0:T(8,128)(2,1)S(1)}, f16[2,128,1024]{2,1,0:T(8,128)(2,1)S(1)}, u32[]{:S(2)}, u32[]{:S(2)}) collective-permute-start(f16[2,128,1024]{2,1,0:T(8,128)(2,1)S(1)} %get-tuple-element.187), channel_id=1, source_target_pairs={{0,2},{1,3},{2,0},{3,1},{4,6},{5,7},{6,4},{7,5},{8,10},{9,11},{10,... | collective-permute-start | bytes 1572872 | tf_op jit(solution)/shard_map/ppermute | solution.py:98
  27.3 17.5 %collective-permute-start.5 = (f16[2,256,1024]{2,1,0:T(8,128)(2,1)S(1)}, f16[2,256,1024]{2,1,0:T(8,128)(2,1)S(1)}, u32[]{:S(2)}, u32[]{:S(2)}) collective-permute-start(f16[2,256,1024]{2,1,0:T(8,128)(2,1)S(1)} %get-tuple-element.182), channel_id=1, source_target_pairs={{0,1},{1,0},{2,3},{3,2},{4,5},{5,4},{6,7},{7,6},{8,9},{9,8},{10,11... | collective-permute-start | bytes 3145736 | tf_op jit(solution)/shard_map/ppermute | solution.py:98
  28.6 25.1 %collective-permute-start.9 = (f16[2,256,1024]{2,1,0:T(8,128)(2,1)S(1)}, f16[2,256,1024]{2,1,0:T(8,128)(2,1)S(1)}, u32[]{:S(2)}, u32[]{:S(2)}) collective-permute-start(f16[2,256,1024]{2,1,0:T(8,128)(2,1)S(1)} %get-tuple-element.178), channel_id=1, source_target_pairs={{0,1},{1,0},{2,3},{3,2},{4,5},{5,4},{6,7},{7,6},{8,9},{9,8},{10,11... | collective-permute-start | bytes 3145736 | tf_op jit(solution)/shard_map/ppermute | solution.py:98
  29.6 14.8 %collective-permute-start.6 = (f16[2,128,1024]{2,1,0:T(8,128)(2,1)S(1)}, f16[2,128,1024]{2,1,0:T(8,128)(2,1)S(1)}, u32[]{:S(2)}, u32[]{:S(2)}) collective-permute-start(f16[2,128,1024]{2,1,0:T(8,128)(2,1)S(1)} %bitcast.355), channel_id=1, source_target_pairs={{0,4},{1,5},{2,6},{3,7},{4,0},{5,1},{6,2},{7,3},{8,12},{9,13},{10,... | collective-permute-start | bytes 1572872 | tf_op jit(solution)/shard_map/ppermute | solution.py:98
  31.7 20.2 %collective-permute-start.10 = (f16[2,128,1024]{2,1,0:T(8,128)(2,1)S(1)}, f16[2,128,1024]{2,1,0:T(8,128)(2,1)S(1)}, u32[]{:S(2)}, u32[]{:S(2)}) collective-permute-start(f16[2,128,1024]{2,1,0:T(8,128)(2,1)S(1)} %get-tuple-element.176), channel_id=1, source_target_pairs={{0,2},{1,3},{2,0},{3,1},{4,6},{5,7},{6,4},{7,5},{8,10},{9,11},{10,... | collective-permute-start | bytes 1572872 | tf_op jit(solution)/shard_map/ppermute | solution.py:98
  39.0 10.2 %collective-permute-start.4 = (f16[2,64,1024]{2,1,0:T(8,128)(2,1)S(1)}, f16[2,64,1024]{2,1,0:T(8,128)(2,1)S(1)}, u32[]{:S(2)}, u32[]{:S(2)}) collective-permute-start(f16[2,64,1024]{2,1,0:T(8,128)(2,1)S(1)} %get-tuple-element.199), channel_id=1, source_target_pairs={{0,4},{1,5},{2,6},{3,7},{4,0},{5,1},{6,2},{7,3},{8,12},{9,13},{10,... | collective-permute-start | bytes 786440 | tf_op jit(solution)/shard_map/ppermute | solution.py:98
  44.7 11.0 %collective-permute-start.8 = (f16[2,64,1024]{2,1,0:T(8,128)(2,1)S(1)}, f16[2,64,1024]{2,1,0:T(8,128)(2,1)S(1)}, u32[]{:S(2)}, u32[]{:S(2)}) collective-permute-start(f16[2,64,1024]{2,1,0:T(8,128)(2,1)S(1)} %get-tuple-element.198), channel_id=1, source_target_pairs={{0,2},{1,3},{2,0},{3,1},{4,6},{5,7},{6,4},{7,5},{8,10},{9,11},{10,... | collective-permute-start | bytes 786440 | tf_op jit(solution)/shard_map/ppermute | solution.py:98
  45.2 21.7 %collective-permute-start.14 = (f16[2,128,1024]{2,1,0:T(8,128)(2,1)S(1)}, f16[2,128,1024]{2,1,0:T(8,128)(2,1)S(1)}, u32[]{:S(2)}, u32[]{:S(2)}) collective-permute-start(f16[2,128,1024]{2,1,0:T(8,128)(2,1)S(1)} %get-tuple-element.174), channel_id=1, source_target_pairs={{0,2},{1,3},{2,0},{3,1},{4,6},{5,7},{6,4},{7,5},{8,10},{9,11},{10,... | collective-permute-start | bytes 1572872 | tf_op jit(solution)/shard_map/ppermute | solution.py:98
  49.3 9.6 %collective-permute-start.7 = (f16[2,32,1024]{2,1,0:T(8,128)(2,1)S(1)}, f16[2,32,1024]{2,1,0:T(8,128)(2,1)S(1)}, u32[]{:S(2)}, u32[]{:S(2)}) collective-permute-start(f16[2,32,1024]{2,1,0:T(8,128)(2,1)S(1)} %get-tuple-element.209), channel_id=1, source_target_pairs={{0,8},{1,9},{2,10},{3,11},{4,12},{5,13},{6,14},{7,15},{8,0},{9,1},... | collective-permute-start | bytes 393224 | tf_op jit(solution)/shard_map/ppermute | solution.py:98
  51.9 47.5 %slice-start = ((s8[10485760]{0:T(1024)(128)(4,1)}), s8[4194304]{0:T(1024)(128)(4,1)S(1)}, s32[]{:S(2)}) async-start(s8[10485760]{0:T(1024)(128)(4,1)} %bitcast.323), calls=%async_computation | async-start | bytes 8388608
  52.1 17.1 %collective-permute-start.13 = (f16[2,64,1024]{2,1,0:T(8,128)(2,1)S(1)}, f16[2,64,1024]{2,1,0:T(8,128)(2,1)S(1)}, u32[]{:S(2)}, u32[]{:S(2)}) collective-permute-start(f16[2,64,1024]{2,1,0:T(8,128)(2,1)S(1)} %get-tuple-element.196), channel_id=1, source_target_pairs={{0,4},{1,5},{2,6},{3,7},{4,0},{5,1},{6,2},{7,3},{8,12},{9,13},{10,... | collective-permute-start | bytes 786440 | tf_op jit(solution)/shard_map/ppermute | solution.py:98
  54.2 23.6 %collective-permute-start.19 = (f16[2,128,1024]{2,1,0:T(8,128)(2,1)S(1)}, f16[2,128,1024]{2,1,0:T(8,128)(2,1)S(1)}, u32[]{:S(2)}, u32[]{:S(2)}) collective-permute-start(f16[2,128,1024]{2,1,0:T(8,128)(2,1)S(1)} %get-tuple-element.172), channel_id=1, source_target_pairs={{0,2},{1,3},{2,0},{3,1},{4,6},{5,7},{6,4},{7,5},{8,10},{9,11},{10,... | collective-permute-start | bytes 1572872 | tf_op jit(solution)/shard_map/ppermute | solution.py:98
  55.8 16.2 %collective-permute-start.12 = (f16[2,32,1024]{2,1,0:T(8,128)(2,1)S(1)}, f16[2,32,1024]{2,1,0:T(8,128)(2,1)S(1)}, u32[]{:S(2)}, u32[]{:S(2)}) collective-permute-start(f16[2,32,1024]{2,1,0:T(8,128)(2,1)S(1)} %get-tuple-element.208), channel_id=1, source_target_pairs={{0,8},{1,9},{2,10},{3,11},{4,12},{5,13},{6,14},{7,15},{8,0},{9,1},... | collective-permute-start | bytes 393224 | tf_op jit(solution)/shard_map/ppermute | solution.py:98
  58.9 40.5 %slice-start.1 = ((s8[10485760]{0:T(1024)(128)(4,1)}), s8[4194304]{0:T(1024)(128)(4,1)S(1)}, s32[]{:S(2)}) async-start(s8[10485760]{0:T(1024)(128)(4,1)} %bitcast.323), calls=%async_computation.1 | async-start | bytes 8388608
  59.0 13.5 %collective-permute-start.11 = (bf16[32,1024]{1,0:T(8,128)(2,1)S(1)}, bf16[32,1024]{1,0:T(8,128)(2,1)S(1)}, u32[]{:S(2)}, u32[]{:S(2)}) collective-permute-start(bf16[32,1024]{1,0:T(8,128)(2,1)S(1)} %fusion.107), channel_id=1, source_target_pairs={{0,8},{1,9},{2,10},{3,11},{4,12},{5,13},{6,14},{7,15},{8,0},{9,1},... | collective-permute-start | bytes 196616 | tf_op jit(solution)/shard_map/ppermute | solution.py:98
  67.1 13.4 %collective-permute-start.18 = (f16[2,64,1024]{2,1,0:T(8,128)(2,1)S(1)}, f16[2,64,1024]{2,1,0:T(8,128)(2,1)S(1)}, u32[]{:S(2)}, u32[]{:S(2)}) collective-permute-start(f16[2,64,1024]{2,1,0:T(8,128)(2,1)S(1)} %get-tuple-element.194), channel_id=1, source_target_pairs={{0,4},{1,5},{2,6},{3,7},{4,0},{5,1},{6,2},{7,3},{8,12},{9,13},{10,... | collective-permute-start | bytes 786440 | tf_op jit(solution)/shard_map/ppermute | solution.py:98
  69.3 13.3 %collective-permute-start.17 = (f16[2,32,1024]{2,1,0:T(8,128)(2,1)S(1)}, f16[2,32,1024]{2,1,0:T(8,128)(2,1)S(1)}, u32[]{:S(2)}, u32[]{:S(2)}) collective-permute-start(f16[2,32,1024]{2,1,0:T(8,128)(2,1)S(1)} %get-tuple-element.206), channel_id=1, source_target_pairs={{0,8},{1,9},{2,10},{3,11},{4,12},{5,13},{6,14},{7,15},{8,0},{9,1},... | collective-permute-start | bytes 393224 | tf_op jit(solution)/shard_map/ppermute | solution.py:98
  72.1 11.7 %collective-permute-start.16 = (bf16[32,1024]{1,0:T(8,128)(2,1)S(1)}, bf16[32,1024]{1,0:T(8,128)(2,1)S(1)}, u32[]{:S(2)}, u32[]{:S(2)}) collective-permute-start(bf16[32,1024]{1,0:T(8,128)(2,1)S(1)} %fusion.105), channel_id=1, source_target_pairs={{0,8},{1,9},{2,10},{3,11},{4,12},{5,13},{6,14},{7,15},{8,0},{9,1},... | collective-permute-start | bytes 196616 | tf_op jit(solution)/shard_map/ppermute | solution.py:98
  72.5 12.5 %collective-permute-start.15 = (bf16[64,1024]{1,0:T(8,128)(2,1)S(1)}, bf16[64,1024]{1,0:T(8,128)(2,1)S(1)}, u32[]{:S(2)}, u32[]{:S(2)}) collective-permute-start(bf16[64,1024]{1,0:T(8,128)(2,1)S(1)} %constant_dynamic-update-slice_fusion), channel_id=1, source_target_pairs={{0,4},{1,5},{2,6},{3,7},{4,0},{5,1},{6,2},{7,3},{8,12},{9,13},{10,... | collective-permute-start | bytes 393224 | tf_op jit(solution)/shard_map/ppermute | solution.py:98
  77.8 21.6 %slice-start.2 = ((s8[10485760]{0:T(1024)(128)(4,1)}), s8[2097152]{0:T(1024)(128)(4,1)S(1)}, s32[]{:S(2)}) async-start(s8[10485760]{0:T(1024)(128)(4,1)} %bitcast.323), calls=%async_computation.2 | async-start | bytes 4194304
  78.0 15.0 %collective-permute-start.24 = (f16[2,64,1024]{2,1,0:T(8,128)(2,1)S(1)}, f16[2,64,1024]{2,1,0:T(8,128)(2,1)S(1)}, u32[]{:S(2)}, u32[]{:S(2)}) collective-permute-start(f16[2,64,1024]{2,1,0:T(8,128)(2,1)S(1)} %get-tuple-element.192), channel_id=1, source_target_pairs={{0,4},{1,5},{2,6},{3,7},{4,0},{5,1},{6,2},{7,3},{8,12},{9,13},{10,... | collective-permute-start | bytes 786440 | tf_op jit(solution)/shard_map/ppermute | solution.py:98
  80.6 14.4 %collective-permute-start.23 = (f16[2,32,1024]{2,1,0:T(8,128)(2,1)S(1)}, f16[2,32,1024]{2,1,0:T(8,128)(2,1)S(1)}, u32[]{:S(2)}, u32[]{:S(2)}) collective-permute-start(f16[2,32,1024]{2,1,0:T(8,128)(2,1)S(1)} %get-tuple-element.204), channel_id=1, source_target_pairs={{0,8},{1,9},{2,10},{3,11},{4,12},{5,13},{6,14},{7,15},{8,0},{9,1},... | collective-permute-start | bytes 393224 | tf_op jit(solution)/shard_map/ppermute | solution.py:98
  82.7 13.5 %collective-permute-start.22 = (bf16[32,1024]{1,0:T(8,128)(2,1)S(1)}, bf16[32,1024]{1,0:T(8,128)(2,1)S(1)}, u32[]{:S(2)}, u32[]{:S(2)}) collective-permute-start(bf16[32,1024]{1,0:T(8,128)(2,1)S(1)} %fusion.103), channel_id=1, source_target_pairs={{0,8},{1,9},{2,10},{3,11},{4,12},{5,13},{6,14},{7,15},{8,0},{9,1},... | collective-permute-start | bytes 196616 | tf_op jit(solution)/shard_map/ppermute | solution.py:98
  83.7 13.9 %collective-permute-start.21 = (bf16[64,1024]{1,0:T(8,128)(2,1)S(1)}, bf16[64,1024]{1,0:T(8,128)(2,1)S(1)}, u32[]{:S(2)}, u32[]{:S(2)}) collective-permute-start(bf16[64,1024]{1,0:T(8,128)(2,1)S(1)} %constant_dynamic-update-slice_fusion.2), channel_id=1, source_target_pairs={{0,4},{1,5},{2,6},{3,7},{4,0},{5,1},{6,2},{7,3},{8,12},{9,13},{10,... | collective-permute-start | bytes 393224 | tf_op jit(solution)/shard_map/ppermute | solution.py:98
  85.1 14.2 %collective-permute-start.20 = (bf16[128,1024]{1,0:T(8,128)(2,1)S(1)}, bf16[128,1024]{1,0:T(8,128)(2,1)S(1)}, u32[]{:S(2)}, u32[]{:S(2)}) collective-permute-start(bf16[128,1024]{1,0:T(8,128)(2,1)S(1)} %constant_dynamic-update-slice_fusion.4), channel_id=1, source_target_pairs={{0,2},{1,3},{2,0},{3,1},{4,6},{5,7},{6,4},{7,5},{8,10},{9,11},{10,... | collective-permute-start | bytes 786440 | tf_op jit(solution)/shard_map/ppermute | solution.py:98
  93.1 9.2 %collective-permute-start.28 = (f16[2,32,1024]{2,1,0:T(8,128)(2,1)S(1)}, f16[2,32,1024]{2,1,0:T(8,128)(2,1)S(1)}, u32[]{:S(2)}, u32[]{:S(2)}) collective-permute-start(f16[2,32,1024]{2,1,0:T(8,128)(2,1)S(1)} %get-tuple-element.202), channel_id=1, source_target_pairs={{0,8},{1,9},{2,10},{3,11},{4,12},{5,13},{6,14},{7,15},{8,0},{9,1},... | collective-permute-start | bytes 393224 | tf_op jit(solution)/shard_map/ppermute | solution.py:98
  95.0 8.5 %collective-permute-start.27 = (bf16[32,1024]{1,0:T(8,128)(2,1)S(1)}, bf16[32,1024]{1,0:T(8,128)(2,1)S(1)}, u32[]{:S(2)}, u32[]{:S(2)}) collective-permute-start(bf16[32,1024]{1,0:T(8,128)(2,1)S(1)} %fusion.101), channel_id=1, source_target_pairs={{0,8},{1,9},{2,10},{3,11},{4,12},{5,13},{6,14},{7,15},{8,0},{9,1},... | collective-permute-start | bytes 196616 | tf_op jit(solution)/shard_map/ppermute | solution.py:98
  96.3 9.5 %collective-permute-start.26 = (bf16[64,1024]{1,0:T(8,128)(2,1)S(1)}, bf16[64,1024]{1,0:T(8,128)(2,1)S(1)}, u32[]{:S(2)}, u32[]{:S(2)}) collective-permute-start(bf16[64,1024]{1,0:T(8,128)(2,1)S(1)} %constant_dynamic-update-slice_fusion.6), channel_id=1, source_target_pairs={{0,4},{1,5},{2,6},{3,7},{4,0},{5,1},{6,2},{7,3},{8,12},{9,13},{10,... | collective-permute-start | bytes 393224 | tf_op jit(solution)/shard_map/ppermute | solution.py:98
  97.7 9.7 %collective-permute-start.25 = (bf16[128,1024]{1,0:T(8,128)(2,1)S(1)}, bf16[128,1024]{1,0:T(8,128)(2,1)S(1)}, u32[]{:S(2)}, u32[]{:S(2)}) collective-permute-start(bf16[128,1024]{1,0:T(8,128)(2,1)S(1)} %constant_dynamic-update-slice_fusion.8), channel_id=1, source_target_pairs={{0,2},{1,3},{2,0},{3,1},{4,6},{5,7},{6,4},{7,5},{8,10},{9,11},{10,... | collective-permute-start | bytes 786440 | tf_op jit(solution)/shard_map/ppermute | solution.py:98
  99.3 9.0 %collective-permute-start.32 = (bf16[256,1024]{1,0:T(8,128)(2,1)S(1)}, bf16[256,1024]{1,0:T(8,128)(2,1)S(1)}, u32[]{:S(2)}, u32[]{:S(2)}) collective-permute-start(bf16[256,1024]{1,0:T(8,128)(2,1)S(1)} %constant_dynamic-update-slice_fusion.10), channel_id=1, source_target_pairs={{0,1},{1,0},{2,3},{3,2},{4,5},{5,4},{6,7},{7,6},{8,9},{9,8},{10,11... | collective-permute-start | bytes 1572872 | tf_op jit(solution)/shard_map/ppermute | solution.py:98
  102.4 6.6 %collective-permute-start.31 = (bf16[32,1024]{1,0:T(8,128)(2,1)S(1)}, bf16[32,1024]{1,0:T(8,128)(2,1)S(1)}, u32[]{:S(2)}, u32[]{:S(2)}) collective-permute-start(bf16[32,1024]{1,0:T(8,128)(2,1)S(1)} %fusion.99), channel_id=1, source_target_pairs={{0,8},{1,9},{2,10},{3,11},{4,12},{5,13},{6,14},{7,15},{8,0},{9,1},... | collective-permute-start | bytes 196616 | tf_op jit(solution)/shard_map/ppermute | solution.py:98
  103.5 6.4 %collective-permute-start.30 = (bf16[64,1024]{1,0:T(8,128)(2,1)S(1)}, bf16[64,1024]{1,0:T(8,128)(2,1)S(1)}, u32[]{:S(2)}, u32[]{:S(2)}) collective-permute-start(bf16[64,1024]{1,0:T(8,128)(2,1)S(1)} %constant_dynamic-update-slice_fusion.12), channel_id=1, source_target_pairs={{0,4},{1,5},{2,6},{3,7},{4,0},{5,1},{6,2},{7,3},{8,12},{9,13},{10,... | collective-permute-start | bytes 393224 | tf_op jit(solution)/shard_map/ppermute | solution.py:98
  105.9 6.4 %collective-permute-start.29 = (bf16[128,1024]{1,0:T(8,128)(2,1)S(1)}, bf16[128,1024]{1,0:T(8,128)(2,1)S(1)}, u32[]{:S(2)}, u32[]{:S(2)}) collective-permute-start(bf16[128,1024]{1,0:T(8,128)(2,1)S(1)} %constant_dynamic-update-slice_fusion.14), channel_id=1, source_target_pairs={{0,2},{1,3},{2,0},{3,1},{4,6},{5,7},{6,4},{7,5},{8,10},{9,11},{10,... | collective-permute-start | bytes 786440 | tf_op jit(solution)/shard_map/ppermute | solution.py:98
  107.5 5.7 %collective-permute-start.35 = (bf16[256,1024]{1,0:T(8,128)(2,1)S(1)}, bf16[256,1024]{1,0:T(8,128)(2,1)S(1)}, u32[]{:S(2)}, u32[]{:S(2)}) collective-permute-start(bf16[256,1024]{1,0:T(8,128)(2,1)S(1)} %constant_dynamic-update-slice_fusion.16), channel_id=1, source_target_pairs={{0,1},{1,0},{2,3},{3,2},{4,5},{5,4},{6,7},{7,6},{8,9},{9,8},{10,11... | collective-permute-start | bytes 1572872 | tf_op jit(solution)/shard_map/ppermute | solution.py:98
  109.1 6.0 %collective-permute-start.34 = (bf16[64,1024]{1,0:T(8,128)(2,1)S(1)}, bf16[64,1024]{1,0:T(8,128)(2,1)S(1)}, u32[]{:S(2)}, u32[]{:S(2)}) collective-permute-start(bf16[64,1024]{1,0:T(8,128)(2,1)S(1)} %constant_dynamic-update-slice_fusion.18), channel_id=1, source_target_pairs={{0,4},{1,5},{2,6},{3,7},{4,0},{5,1},{6,2},{7,3},{8,12},{9,13},{10,... | collective-permute-start | bytes 393224 | tf_op jit(solution)/shard_map/ppermute | solution.py:98
  109.9 8.3 %collective-permute-start.33 = (bf16[128,1024]{1,0:T(8,128)(2,1)S(1)}, bf16[128,1024]{1,0:T(8,128)(2,1)S(1)}, u32[]{:S(2)}, u32[]{:S(2)}) collective-permute-start(bf16[128,1024]{1,0:T(8,128)(2,1)S(1)} %constant_dynamic-update-slice_fusion.20), channel_id=1, source_target_pairs={{0,2},{1,3},{2,0},{3,1},{4,6},{5,7},{6,4},{7,5},{8,10},{9,11},{10,... | collective-permute-start | bytes 786440 | tf_op jit(solution)/shard_map/ppermute | solution.py:98
  112.3 6.7 %collective-permute-start.37 = (bf16[256,1024]{1,0:T(8,128)(2,1)S(1)}, bf16[256,1024]{1,0:T(8,128)(2,1)S(1)}, u32[]{:S(2)}, u32[]{:S(2)}) collective-permute-start(bf16[256,1024]{1,0:T(8,128)(2,1)S(1)} %constant_dynamic-update-slice_fusion.22), channel_id=1, source_target_pairs={{0,1},{1,0},{2,3},{3,2},{4,5},{5,4},{6,7},{7,6},{8,9},{9,8},{10,11... | collective-permute-start | bytes 1572872 | tf_op jit(solution)/shard_map/ppermute | solution.py:98
  115.1 8.5 %collective-permute-start.36 = (bf16[128,1024]{1,0:T(8,128)(2,1)S(1)}, bf16[128,1024]{1,0:T(8,128)(2,1)S(1)}, u32[]{:S(2)}, u32[]{:S(2)}) collective-permute-start(bf16[128,1024]{1,0:T(8,128)(2,1)S(1)} %constant_dynamic-update-slice_fusion.24), channel_id=1, source_target_pairs={{0,2},{1,3},{2,0},{3,1},{4,6},{5,7},{6,4},{7,5},{8,10},{9,11},{10,... | collective-permute-start | bytes 786440 | tf_op jit(solution)/shard_map/ppermute | solution.py:98
  118.2 6.3 %collective-permute-start.38 = (bf16[256,1024]{1,0:T(8,128)(2,1)S(1)}, bf16[256,1024]{1,0:T(8,128)(2,1)S(1)}, u32[]{:S(2)}, u32[]{:S(2)}) collective-permute-start(bf16[256,1024]{1,0:T(8,128)(2,1)S(1)} %constant_dynamic-update-slice_fusion.26), channel_id=1, source_target_pairs={{0,1},{1,0},{2,3},{3,2},{4,5},{5,4},{6,7},{7,6},{8,9},{9,8},{10,11... | collective-permute-start | bytes 1572872 | tf_op jit(solution)/shard_map/ppermute | solution.py:98
  123.7 2.0 %collective-permute-start.39 = (bf16[256,1024]{1,0:T(8,128)(2,1)S(1)}, bf16[256,1024]{1,0:T(8,128)(2,1)S(1)}, u32[]{:S(2)}, u32[]{:S(2)}) collective-permute-start(bf16[256,1024]{1,0:T(8,128)(2,1)S(1)} %constant_dynamic-update-slice_fusion.28), channel_id=1, source_target_pairs={{0,1},{1,0},{2,3},{3,2},{4,5},{5,4},{6,7},{7,6},{8,9},{9,8},{10,11... | collective-permute-start | bytes 1572872 | tf_op jit(solution)/shard_map/ppermute | solution.py:98

commit v4 on v3

--- a/solution.py
+++ b/solution.py
@@ -9,7 +9,7 @@
 
 F16, F32, BF16 = jnp.float16, jnp.float32, jnp.bfloat16
 PARTS = (4,4,4,4,4)
-SUM_Z_FIRST = (1,)
+SUM_Z_FIRST = (2,)
 GATHER_Z_LAST = ()
 EARLY = ((2, 1),)
 SCALE = 4.0

time: 128 us -> 129 us (level)
  waiting for transfers between devices: 44.2 us -> 48.9 us
  starting transfers between devices: 46.2 us -> 43.2 us
    ppermute x40, waiting for transfers between devices: 44.2 us -> 48.9 us  [swap(): return lax.ppermute(v, 'gx', [(i, i ^ mask) for i in range(n)])]
    ppermute x40, starting transfers between devices: 46.2 us -> 43.2 us  [swap(): return lax.ppermute(v, 'gx', [(i, i ^ mask) for i in range(n)])]
where the time goes in v4:
time: 129 us
  waiting for transfers between devices  48.9 us (38%)
  starting transfers between devices  43.2 us (33%)
  matrix products  21.4 us (17%)
  other arithmetic  7.46 us (6%)
  Pallas kernels  4.42 us (3%)
  local copies, waits for them, and re-layouts  3.01 us (2%)
    ppermute x40, waiting for transfers between devices, swap(): return lax.ppermute(v, 'gx', [(i, i ^ mask) for i in range(n)])  48.9 us
    ppermute x40, starting transfers between devices, swap(): return lax.ppermute(v, 'gx', [(i, i ^ mask) for i in range(n)])  43.2 us
    dot_general x2, matrix products, on_device(): jnp.dot(x, v, preferred_element_type=F32).astype(F16)  14.8 us
    dot_general x5, matrix products, on_device(): lo = jnp.dot(last, down_weight[cols], preferred_element_type=F32)  3.66 us
    another operation x5, other arithmetic, split(): return (v[:, :, k].reshape(first, rows // 2, w) for k in (0, 1))  3.32 us
    add x12, other arithmetic, add(): return v.astype(F32) + got.astype(F32)  2.99 us
    dot_general x4, matrix products, on_device(): hi = jnp.dot(ins[1], down_weight[cols], preferred_element_type=F32)  2.94 us
    slice x10, local copies, waits for them, and re-layouts, on_device(): acc = jnp.stack([ins[0][:, cols], ins[1][:, cols]])  2.64 us
  transfers between devices with their start and end apart: 40, of which 16 were waited for; matrix products, arithmetic and copies ran while one was open for 12% of the time, Pallas kernels for 0%

profile of v4, /device:TPU:0, one launch (start us, length us, event | category | flops | bytes accessed | tf_op | source)
XLA Modules:
  0.0 129.2 jit_solution(720690055423649433)
XLA Ops:
  0.0 2.4 %shard_map.46 = bf16[512,1024]{1,0:T(8,128)(2,1)} custom-call(bf16[512,1024]{1,0:T(8,128)(2,1)} %x_ref.1), custom_call_target="tpu_custom_call" | custom-call | tf_op jit(solution)/shard_map/pallas_call | solution.py:42
  2.5 8.7 %convolution_convert_fusion = f16[512,5120]{1,0:T(8,128)(2,1)S(1)} fusion(bf16[512,1024]{1,0:T(8,128)(2,1)} %shard_map.46, bf16[1024,5120]{1,0:T(8,128)(2,1)} %param.6), kind=kOutput, calls=%fused_computation | convolution fusion | flops 5371330560 | bytes 16777216 | tf_op jit(solution)/shard_map/dot_general | solution.py:120
  11.5 6.0 %convolution_convert_fusion.1 = f16[512,5120]{1,0:T(8,128)(2,1)S(1)} fusion(bf16[512,1024]{1,0:T(8,128)(2,1)S(1)} %copy-done, bf16[1024,5120]{1,0:T(8,128)(2,1)S(1)} %bitcast.367), kind=kOutput, calls=%fused_computation.1 | convolution fusion | flops 5371330560 | bytes 16777216 | tf_op jit(solution)/shard_map/dot_general | solution.py:120
  17.8 0.6 fusion.53
  18.5 0.5 collective-permute-start
  19.5 0.7 fusion.51
  20.4 0.9 collective-permute-done
  21.3 0.5 fusion.54
  22.3 0.7 fusion.52
  23.0 0.4 collective-permute-start.2
  23.4 2.7 %collective-permute-start.1 = (f16[2,128,1024]{2,1,0:T(8,128)(2,1)S(1)}, f16[2,128,1024]{2,1,0:T(8,128)(2,1)S(1)}, u32[]{:S(2)}, u32[]{:S(2)}) collective-permute-start(f16[2,128,1024]{2,1,0:T(8,128)(2,1)S(1)} %get-tuple-element.187), channel_id=1, source_target_pairs={{0,2},{1,3},{2,0},{3,1},{4,6},{5,7},{6,4},{7,5},{8,10},{9,11},{10,... | collective-permute-start | bytes 1572872 | tf_op jit(solution)/shard_map/ppermute | solution.py:98
  26.6 0.7 fusion.50
  28.0 0.7 fusion.49
  28.6 0.5 collective-permute-start.9
  29.1 0.5 add_bitcast_fusion.2
  29.7 0.5 convert_add_fusion
  30.2 2.1 %collective-permute-start.10 = (f16[2,128,1024]{2,1,0:T(8,128)(2,1)S(1)}, f16[2,128,1024]{2,1,0:T(8,128)(2,1)S(1)}, u32[]{:S(2)}, u32[]{:S(2)}) collective-permute-start(f16[2,128,1024]{2,1,0:T(8,128)(2,1)S(1)} %bitcast.355), channel_id=1, source_target_pairs={{0,4},{1,5},{2,6},{3,7},{4,0},{5,1},{6,2},{7,3},{8,12},{9,13},{10,... | collective-permute-start | bytes 1572872 | tf_op jit(solution)/shard_map/ppermute | solution.py:98
  32.3 6.5 %collective-permute-done.1 = f16[2,128,1024]{2,1,0:T(8,128)(2,1)S(1)} collective-permute-done((f16[2,128,1024]{2,1,0:T(8,128)(2,1)S(1)}, f16[2,128,1024]{2,1,0:T(8,128)(2,1)S(1)}, u32[]{:S(2)}, u32[]{:S(2)}) %collective-permute-start.1) | collective-permute-done | bytes 524320 | tf_op jit(solution)/shard_map/ppermute | solution.py:98
  39.0 2.1 %collective-permute-start.4 = (f16[2,64,1024]{2,1,0:T(8,128)(2,1)S(1)}, f16[2,64,1024]{2,1,0:T(8,128)(2,1)S(1)}, u32[]{:S(2)}, u32[]{:S(2)}) collective-permute-start(f16[2,64,1024]{2,1,0:T(8,128)(2,1)S(1)} %get-tuple-element.199), channel_id=1, source_target_pairs={{0,4},{1,5},{2,6},{3,7},{4,0},{5,1},{6,2},{7,3},{8,12},{9,13},{10,... | collective-permute-start | bytes 786440 | tf_op jit(solution)/shard_map/ppermute | solution.py:98
  41.1 8.6 %collective-permute-done.6 = f16[2,128,1024]{2,1,0:T(8,128)(2,1)S(1)} collective-permute-done((f16[2,128,1024]{2,1,0:T(8,128)(2,1)S(1)}, f16[2,128,1024]{2,1,0:T(8,128)(2,1)S(1)}, u32[]{:S(2)}, u32[]{:S(2)}) %collective-permute-start.6) | collective-permute-done | bytes 524320 | tf_op jit(solution)/shard_map/ppermute | solution.py:98
  49.9 1.9 %collective-permute-start.8 = (f16[2,64,1024]{2,1,0:T(8,128)(2,1)S(1)}, f16[2,64,1024]{2,1,0:T(8,128)(2,1)S(1)}, u32[]{:S(2)}, u32[]{:S(2)}) collective-permute-start(f16[2,64,1024]{2,1,0:T(8,128)(2,1)S(1)} %get-tuple-element.198), channel_id=1, source_target_pairs={{0,4},{1,5},{2,6},{3,7},{4,0},{5,1},{6,2},{7,3},{8,12},{9,13},{10,... | collective-permute-start | bytes 786440 | tf_op jit(solution)/shard_map/ppermute | solution.py:98
  51.8 0.5 add_bitcast_fusion.1
  52.3 1.6 %collective-permute-start.14 = (f16[2,128,1024]{2,1,0:T(8,128)(2,1)S(1)}, f16[2,128,1024]{2,1,0:T(8,128)(2,1)S(1)}, u32[]{:S(2)}, u32[]{:S(2)}) collective-permute-start(f16[2,128,1024]{2,1,0:T(8,128)(2,1)S(1)} %get-tuple-element.174), channel_id=1, source_target_pairs={{0,2},{1,3},{2,0},{3,1},{4,6},{5,7},{6,4},{7,5},{8,10},{9,11},{10,... | collective-permute-start | bytes 1572872 | tf_op jit(solution)/shard_map/ppermute | solution.py:98
  54.0 2.7 %collective-permute-start.7 = (f16[2,32,1024]{2,1,0:T(8,128)(2,1)S(1)}, f16[2,32,1024]{2,1,0:T(8,128)(2,1)S(1)}, u32[]{:S(2)}, u32[]{:S(2)}) collective-permute-start(f16[2,32,1024]{2,1,0:T(8,128)(2,1)S(1)} %get-tuple-element.209), channel_id=1, source_target_pairs={{0,8},{1,9},{2,10},{3,11},{4,12},{5,13},{6,14},{7,15},{8,0},{9,1},... | collective-permute-start | bytes 393224 | tf_op jit(solution)/shard_map/ppermute | solution.py:98
  56.8 0.6 collective-permute-start.13
  57.4 0.5 add_bitcast_fusion
  57.9 1.6 %collective-permute-start.19 = (f16[2,128,1024]{2,1,0:T(8,128)(2,1)S(1)}, f16[2,128,1024]{2,1,0:T(8,128)(2,1)S(1)}, u32[]{:S(2)}, u32[]{:S(2)}) collective-permute-start(f16[2,128,1024]{2,1,0:T(8,128)(2,1)S(1)} %get-tuple-element.172), channel_id=1, source_target_pairs={{0,2},{1,3},{2,0},{3,1},{4,6},{5,7},{6,4},{7,5},{8,10},{9,11},{10,... | collective-permute-start | bytes 1572872 | tf_op jit(solution)/shard_map/ppermute | solution.py:98
  59.5 1.0 collective-permute-done.8
  60.5 1.7 %collective-permute-start.12 = (f16[2,32,1024]{2,1,0:T(8,128)(2,1)S(1)}, f16[2,32,1024]{2,1,0:T(8,128)(2,1)S(1)}, u32[]{:S(2)}, u32[]{:S(2)}) collective-permute-start(f16[2,32,1024]{2,1,0:T(8,128)(2,1)S(1)} %get-tuple-element.208), channel_id=1, source_target_pairs={{0,8},{1,9},{2,10},{3,11},{4,12},{5,13},{6,14},{7,15},{8,0},{9,1},... | collective-permute-start | bytes 393224 | tf_op jit(solution)/shard_map/ppermute | solution.py:98
  62.3 1.4 %collective-permute-start.11 = (bf16[32,1024]{1,0:T(8,128)(2,1)S(1)}, bf16[32,1024]{1,0:T(8,128)(2,1)S(1)}, u32[]{:S(2)}, u32[]{:S(2)}) collective-permute-start(bf16[32,1024]{1,0:T(8,128)(2,1)S(1)} %fusion.107), channel_id=1, source_target_pairs={{0,8},{1,9},{2,10},{3,11},{4,12},{5,13},{6,14},{7,15},{8,0},{9,1},... | collective-permute-start | bytes 196616 | tf_op jit(solution)/shard_map/ppermute | solution.py:98
  63.7 3.6 %collective-permute-done.14 = f16[2,128,1024]{2,1,0:T(8,128)(2,1)S(1)} collective-permute-done((f16[2,128,1024]{2,1,0:T(8,128)(2,1)S(1)}, f16[2,128,1024]{2,1,0:T(8,128)(2,1)S(1)}, u32[]{:S(2)}, u32[]{:S(2)}) %collective-permute-start.14) | collective-permute-done | bytes 524320 | tf_op jit(solution)/shard_map/ppermute | solution.py:98
  67.7 5.1 %collective-permute-done.13 = f16[2,64,1024]{2,1,0:T(8,128)(2,1)S(1)} collective-permute-done((f16[2,64,1024]{2,1,0:T(8,128)(2,1)S(1)}, f16[2,64,1024]{2,1,0:T(8,128)(2,1)S(1)}, u32[]{:S(2)}, u32[]{:S(2)}) %collective-permute-start.13) | collective-permute-done | bytes 262176 | tf_op jit(solution)/shard_map/ppermute | solution.py:98
  72.9 2.7 %collective-permute-start.17 = (f16[2,32,1024]{2,1,0:T(8,128)(2,1)S(1)}, f16[2,32,1024]{2,1,0:T(8,128)(2,1)S(1)}, u32[]{:S(2)}, u32[]{:S(2)}) collective-permute-start(f16[2,32,1024]{2,1,0:T(8,128)(2,1)S(1)} %get-tuple-element.206), channel_id=1, source_target_pairs={{0,8},{1,9},{2,10},{3,11},{4,12},{5,13},{6,14},{7,15},{8,0},{9,1},... | collective-permute-start | bytes 393224 | tf_op jit(solution)/shard_map/ppermute | solution.py:98
  76.4 5.9 %collective-permute-done.19 = f16[2,128,1024]{2,1,0:T(8,128)(2,1)S(1)} collective-permute-done((f16[2,128,1024]{2,1,0:T(8,128)(2,1)S(1)}, f16[2,128,1024]{2,1,0:T(8,128)(2,1)S(1)}, u32[]{:S(2)}, u32[]{:S(2)}) %collective-permute-start.19) | collective-permute-done | bytes 524320 | tf_op jit(solution)/shard_map/ppermute | solution.py:98
  82.5 0.5 collective-permute-start.24
  83.1 2.6 %collective-permute-start.23 = (f16[2,32,1024]{2,1,0:T(8,128)(2,1)S(1)}, f16[2,32,1024]{2,1,0:T(8,128)(2,1)S(1)}, u32[]{:S(2)}, u32[]{:S(2)}) collective-permute-start(f16[2,32,1024]{2,1,0:T(8,128)(2,1)S(1)} %get-tuple-element.204), channel_id=1, source_target_pairs={{0,8},{1,9},{2,10},{3,11},{4,12},{5,13},{6,14},{7,15},{8,0},{9,1},... | collective-permute-start | bytes 393224 | tf_op jit(solution)/shard_map/ppermute | solution.py:98
  86.3 1.6 %collective-permute-start.21 = (bf16[64,1024]{1,0:T(8,128)(2,1)S(1)}, bf16[64,1024]{1,0:T(8,128)(2,1)S(1)}, u32[]{:S(2)}, u32[]{:S(2)}) collective-permute-start(bf16[64,1024]{1,0:T(8,128)(2,1)S(1)} %constant_dynamic-update-slice_fusion.2), channel_id=1, source_target_pairs={{0,4},{1,5},{2,6},{3,7},{4,0},{5,1},{6,2},{7,3},{8,12},{9,13},{10,... | collective-permute-start | bytes 393224 | tf_op jit(solution)/shard_map/ppermute | solution.py:98
  88.0 1.6 %collective-permute-start.20 = (bf16[128,1024]{1,0:T(8,128)(2,1)S(1)}, bf16[128,1024]{1,0:T(8,128)(2,1)S(1)}, u32[]{:S(2)}, u32[]{:S(2)}) collective-permute-start(bf16[128,1024]{1,0:T(8,128)(2,1)S(1)} %constant_dynamic-update-slice_fusion.4), channel_id=1, source_target_pairs={{0,2},{1,3},{2,0},{3,1},{4,6},{5,7},{6,4},{7,5},{8,10},{9,11},{10,... | collective-permute-start | bytes 786440 | tf_op jit(solution)/shard_map/ppermute | solution.py:98
  89.6 5.2 %collective-permute-done.24 = f16[2,64,1024]{2,1,0:T(8,128)(2,1)S(1)} collective-permute-done((f16[2,64,1024]{2,1,0:T(8,128)(2,1)S(1)}, f16[2,64,1024]{2,1,0:T(8,128)(2,1)S(1)}, u32[]{:S(2)}, u32[]{:S(2)}) %collective-permute-start.24) | collective-permute-done | bytes 262176 | tf_op jit(solution)/shard_map/ppermute | solution.py:98
  94.8 1.8 %collective-permute-start.28 = (f16[2,32,1024]{2,1,0:T(8,128)(2,1)S(1)}, f16[2,32,1024]{2,1,0:T(8,128)(2,1)S(1)}, u32[]{:S(2)}, u32[]{:S(2)}) collective-permute-start(f16[2,32,1024]{2,1,0:T(8,128)(2,1)S(1)} %get-tuple-element.202), channel_id=1, source_target_pairs={{0,8},{1,9},{2,10},{3,11},{4,12},{5,13},{6,14},{7,15},{8,0},{9,1},... | collective-permute-start | bytes 393224 | tf_op jit(solution)/shard_map/ppermute | solution.py:98
  96.7 1.3 collective-permute-start.27
  98.0 1.9 %collective-permute-start.26 = (bf16[64,1024]{1,0:T(8,128)(2,1)S(1)}, bf16[64,1024]{1,0:T(8,128)(2,1)S(1)}, u32[]{:S(2)}, u32[]{:S(2)}) collective-permute-start(bf16[64,1024]{1,0:T(8,128)(2,1)S(1)} %constant_dynamic-update-slice_fusion.6), channel_id=1, source_target_pairs={{0,4},{1,5},{2,6},{3,7},{4,0},{5,1},{6,2},{7,3},{8,12},{9,13},{10,... | collective-permute-start | bytes 393224 | tf_op jit(solution)/shard_map/ppermute | solution.py:98
  99.9 0.9 collective-permute-start.25
  101.3 0.7 fusion.16
  102.0 2.5 %collective-permute-done.28 = f16[2,32,1024]{2,1,0:T(8,128)(2,1)S(1)} collective-permute-done((f16[2,32,1024]{2,1,0:T(8,128)(2,1)S(1)}, f16[2,32,1024]{2,1,0:T(8,128)(2,1)S(1)}, u32[]{:S(2)}, u32[]{:S(2)}) %collective-permute-start.28) | collective-permute-done | bytes 131104 | tf_op jit(solution)/shard_map/ppermute | solution.py:98
  104.6 0.5 collective-permute-start.31
  105.2 1.4 %collective-permute-start.30 = (bf16[64,1024]{1,0:T(8,128)(2,1)S(1)}, bf16[64,1024]{1,0:T(8,128)(2,1)S(1)}, u32[]{:S(2)}, u32[]{:S(2)}) collective-permute-start(bf16[64,1024]{1,0:T(8,128)(2,1)S(1)} %constant_dynamic-update-slice_fusion.12), channel_id=1, source_target_pairs={{0,4},{1,5},{2,6},{3,7},{4,0},{5,1},{6,2},{7,3},{8,12},{9,13},{10,... | collective-permute-start | bytes 393224 | tf_op jit(solution)/shard_map/ppermute | solution.py:98
  106.6 1.4 %collective-permute-start.29 = (bf16[128,1024]{1,0:T(8,128)(2,1)S(1)}, bf16[128,1024]{1,0:T(8,128)(2,1)S(1)}, u32[]{:S(2)}, u32[]{:S(2)}) collective-permute-start(bf16[128,1024]{1,0:T(8,128)(2,1)S(1)} %constant_dynamic-update-slice_fusion.14), channel_id=1, source_target_pairs={{0,2},{1,3},{2,0},{3,1},{4,6},{5,7},{6,4},{7,5},{8,10},{9,11},{10,... | collective-permute-start | bytes 786440 | tf_op jit(solution)/shard_map/ppermute | solution.py:98
  108.1 0.7 fusion.18
  108.9 0.7 fusion.14
  110.0 0.7 collective-permute-start.34
  110.7 0.8 collective-permute-done.30
  111.5 1.2 collective-permute-start.33
  112.7 1.5 %collective-permute-done.29 = bf16[128,1024]{1,0:T(8,128)(2,1)S(1)} collective-permute-done((bf16[128,1024]{1,0:T(8,128)(2,1)S(1)}, bf16[128,1024]{1,0:T(8,128)(2,1)S(1)}, u32[]{:S(2)}, u32[]{:S(2)}) %collective-permute-start.29) | collective-permute-done | bytes 262176 | tf_op jit(solution)/shard_map/ppermute | solution.py:98
  114.4 0.7 fusion.24
  115.1 0.7 fusion.21
  115.9 1.4 %collective-permute-start.36 = (bf16[128,1024]{1,0:T(8,128)(2,1)S(1)}, bf16[128,1024]{1,0:T(8,128)(2,1)S(1)}, u32[]{:S(2)}, u32[]{:S(2)}) collective-permute-start(bf16[128,1024]{1,0:T(8,128)(2,1)S(1)} %constant_dynamic-update-slice_fusion.24), channel_id=1, source_target_pairs={{0,2},{1,3},{2,0},{3,1},{4,6},{5,7},{6,4},{7,5},{8,10},{9,11},{10,... | collective-permute-start | bytes 786440 | tf_op jit(solution)/shard_map/ppermute | solution.py:98
  117.3 2.7 %collective-permute-done.33 = bf16[128,1024]{1,0:T(8,128)(2,1)S(1)} collective-permute-done((bf16[128,1024]{1,0:T(8,128)(2,1)S(1)}, bf16[128,1024]{1,0:T(8,128)(2,1)S(1)}, u32[]{:S(2)}, u32[]{:S(2)}) %collective-permute-start.33) | collective-permute-done | bytes 262176 | tf_op jit(solution)/shard_map/ppermute | solution.py:98
  120.1 0.7 fusion.30
  120.9 0.7 fusion.27
  121.6 3.6 %collective-permute-done.36 = bf16[128,1024]{1,0:T(8,128)(2,1)S(1)} collective-permute-done((bf16[128,1024]{1,0:T(8,128)(2,1)S(1)}, bf16[128,1024]{1,0:T(8,128)(2,1)S(1)}, u32[]{:S(2)}, u32[]{:S(2)}) %collective-permute-start.36) | collective-permute-done | bytes 262176 | tf_op jit(solution)/shard_map/ppermute | solution.py:98
  125.3 0.7 fusion.36.lo_ref
  126.0 0.7 fusion.33.hi_ref
  127.2 2.0 %shard_map.47 = bf16[512,1024]{1,0:T(8,128)(2,1)} custom-call(f32[256,1024]{1,0:T(8,128)S(1)} %fusion.36.lo_ref, f32[256,1024]{1,0:T(8,128)S(1)} %fusion.33.hi_ref, bf16[256,1024]{1,0:T(8,128)(2,1)S(1)} %collective-permute-done.39.hidden_ref, bf16[5120,1024]{1,0:T(8,128)(2,1)S(1)} %bitcast.324), custom_call_target="tpu_custom_call" | custom-call | tf_op jit(solution)/shard_map/pallas_call | solution.py:69
  (115 shorter events, 7.8 us)
Async XLA Ops:
  0.0 11.5 %slice-start.3 = ((s8[10485760]{0:T(1024)(128)(4,1)}), s8[2097152]{0:T(1024)(128)(4,1)S(1)}, s32[]{:S(2)}) async-start(s8[10485760]{0:T(1024)(128)(4,1)} %bitcast.366), calls=%async_computation.3 | async-start | bytes 4194304
  2.4 9.0 %copy-start = (bf16[512,1024]{1,0:T(8,128)(2,1)S(1)}, bf16[512,1024]{1,0:T(8,128)(2,1)}, u32[]{:S(2)}) copy-start(bf16[512,1024]{1,0:T(8,128)(2,1)} %shard_map.46) | copy-start | bytes 3145732
  2.4 9.0 %slice-start.4 = ((s8[10485760]{0:T(1024)(128)(4,1)}), s8[4194304]{0:T(1024)(128)(4,1)S(1)}, s32[]{:S(2)}) async-start(s8[10485760]{0:T(1024)(128)(4,1)} %bitcast.366), calls=%async_computation.4 | async-start | bytes 8388608
  2.4 9.0 %slice-start.5 = ((s8[10485760]{0:T(1024)(128)(4,1)}), s8[4194304]{0:T(1024)(128)(4,1)S(1)}, s32[]{:S(2)}) async-start(s8[10485760]{0:T(1024)(128)(4,1)} %bitcast.366), calls=%async_computation.5 | async-start | bytes 8388608
  18.5 2.8 %collective-permute-start = (f16[2,256,1024]{2,1,0:T(8,128)(2,1)S(1)}, f16[2,256,1024]{2,1,0:T(8,128)(2,1)S(1)}, u32[]{:S(2)}, u32[]{:S(2)}) collective-permute-start(f16[2,256,1024]{2,1,0:T(8,128)(2,1)S(1)} %get-tuple-element.189), channel_id=1, source_target_pairs={{0,1},{1,0},{2,3},{3,2},{4,5},{5,4},{6,7},{7,6},{8,9},{9,8},{10,11... | collective-permute-start | bytes 3145736 | tf_op jit(solution)/shard_map/ppermute | solution.py:98
  20.2 8.9 %collective-permute-start.3 = (f16[2,256,1024]{2,1,0:T(8,128)(2,1)S(1)}, f16[2,256,1024]{2,1,0:T(8,128)(2,1)S(1)}, u32[]{:S(2)}, u32[]{:S(2)}) collective-permute-start(f16[2,256,1024]{2,1,0:T(8,128)(2,1)S(1)} %get-tuple-element.184), channel_id=1, source_target_pairs={{0,1},{1,0},{2,3},{3,2},{4,5},{5,4},{6,7},{7,6},{8,9},{9,8},{10,11... | collective-permute-start | bytes 3145736 | tf_op jit(solution)/shard_map/ppermute | solution.py:98
  23.0 6.7 %collective-permute-start.2 = (f16[2,256,1024]{2,1,0:T(8,128)(2,1)S(1)}, f16[2,256,1024]{2,1,0:T(8,128)(2,1)S(1)}, u32[]{:S(2)}, u32[]{:S(2)}) collective-permute-start(f16[2,256,1024]{2,1,0:T(8,128)(2,1)S(1)} %get-tuple-element.185), channel_id=1, source_target_pairs={{0,1},{1,0},{2,3},{3,2},{4,5},{5,4},{6,7},{7,6},{8,9},{9,8},{10,11... | collective-permute-start | bytes 3145736 | tf_op jit(solution)/shard_map/ppermute | solution.py:98
  23.4 15.4 %collective-permute-start.1 = (f16[2,128,1024]{2,1,0:T(8,128)(2,1)S(1)}, f16[2,128,1024]{2,1,0:T(8,128)(2,1)S(1)}, u32[]{:S(2)}, u32[]{:S(2)}) collective-permute-start(f16[2,128,1024]{2,1,0:T(8,128)(2,1)S(1)} %get-tuple-element.187), channel_id=1, source_target_pairs={{0,2},{1,3},{2,0},{3,1},{4,6},{5,7},{6,4},{7,5},{8,10},{9,11},{10,... | collective-permute-start | bytes 1572872 | tf_op jit(solution)/shard_map/ppermute | solution.py:98
  27.3 24.5 %collective-permute-start.5 = (f16[2,256,1024]{2,1,0:T(8,128)(2,1)S(1)}, f16[2,256,1024]{2,1,0:T(8,128)(2,1)S(1)}, u32[]{:S(2)}, u32[]{:S(2)}) collective-permute-start(f16[2,256,1024]{2,1,0:T(8,128)(2,1)S(1)} %get-tuple-element.182), channel_id=1, source_target_pairs={{0,1},{1,0},{2,3},{3,2},{4,5},{5,4},{6,7},{7,6},{8,9},{9,8},{10,11... | collective-permute-start | bytes 3145736 | tf_op jit(solution)/shard_map/ppermute | solution.py:98
  28.6 28.8 %collective-permute-start.9 = (f16[2,256,1024]{2,1,0:T(8,128)(2,1)S(1)}, f16[2,256,1024]{2,1,0:T(8,128)(2,1)S(1)}, u32[]{:S(2)}, u32[]{:S(2)}) collective-permute-start(f16[2,256,1024]{2,1,0:T(8,128)(2,1)S(1)} %get-tuple-element.178), channel_id=1, source_target_pairs={{0,1},{1,0},{2,3},{3,2},{4,5},{5,4},{6,7},{7,6},{8,9},{9,8},{10,11... | collective-permute-start | bytes 3145736 | tf_op jit(solution)/shard_map/ppermute | solution.py:98
  29.6 20.1 %collective-permute-start.6 = (f16[2,128,1024]{2,1,0:T(8,128)(2,1)S(1)}, f16[2,128,1024]{2,1,0:T(8,128)(2,1)S(1)}, u32[]{:S(2)}, u32[]{:S(2)}) collective-permute-start(f16[2,128,1024]{2,1,0:T(8,128)(2,1)S(1)} %get-tuple-element.180), channel_id=1, source_target_pairs={{0,2},{1,3},{2,0},{3,1},{4,6},{5,7},{6,4},{7,5},{8,10},{9,11},{10,... | collective-permute-start | bytes 1572872 | tf_op jit(solution)/shard_map/ppermute | solution.py:98
  30.2 26.4 %collective-permute-start.10 = (f16[2,128,1024]{2,1,0:T(8,128)(2,1)S(1)}, f16[2,128,1024]{2,1,0:T(8,128)(2,1)S(1)}, u32[]{:S(2)}, u32[]{:S(2)}) collective-permute-start(f16[2,128,1024]{2,1,0:T(8,128)(2,1)S(1)} %bitcast.355), channel_id=1, source_target_pairs={{0,4},{1,5},{2,6},{3,7},{4,0},{5,1},{6,2},{7,3},{8,12},{9,13},{10,... | collective-permute-start | bytes 1572872 | tf_op jit(solution)/shard_map/ppermute | solution.py:98
  39.0 14.9 %collective-permute-start.4 = (f16[2,64,1024]{2,1,0:T(8,128)(2,1)S(1)}, f16[2,64,1024]{2,1,0:T(8,128)(2,1)S(1)}, u32[]{:S(2)}, u32[]{:S(2)}) collective-permute-start(f16[2,64,1024]{2,1,0:T(8,128)(2,1)S(1)} %get-tuple-element.199), channel_id=1, source_target_pairs={{0,4},{1,5},{2,6},{3,7},{4,0},{5,1},{6,2},{7,3},{8,12},{9,13},{10,... | collective-permute-start | bytes 786440 | tf_op jit(solution)/shard_map/ppermute | solution.py:98
  49.9 10.5 %collective-permute-start.8 = (f16[2,64,1024]{2,1,0:T(8,128)(2,1)S(1)}, f16[2,64,1024]{2,1,0:T(8,128)(2,1)S(1)}, u32[]{:S(2)}, u32[]{:S(2)}) collective-permute-start(f16[2,64,1024]{2,1,0:T(8,128)(2,1)S(1)} %get-tuple-element.198), channel_id=1, source_target_pairs={{0,4},{1,5},{2,6},{3,7},{4,0},{5,1},{6,2},{7,3},{8,12},{9,13},{10,... | collective-permute-start | bytes 786440 | tf_op jit(solution)/shard_map/ppermute | solution.py:98
  52.3 14.9 %collective-permute-start.14 = (f16[2,128,1024]{2,1,0:T(8,128)(2,1)S(1)}, f16[2,128,1024]{2,1,0:T(8,128)(2,1)S(1)}, u32[]{:S(2)}, u32[]{:S(2)}) collective-permute-start(f16[2,128,1024]{2,1,0:T(8,128)(2,1)S(1)} %get-tuple-element.174), channel_id=1, source_target_pairs={{0,2},{1,3},{2,0},{3,1},{4,6},{5,7},{6,4},{7,5},{8,10},{9,11},{10,... | collective-permute-start | bytes 1572872 | tf_op jit(solution)/shard_map/ppermute | solution.py:98
  54.0 8.2 %collective-permute-start.7 = (f16[2,32,1024]{2,1,0:T(8,128)(2,1)S(1)}, f16[2,32,1024]{2,1,0:T(8,128)(2,1)S(1)}, u32[]{:S(2)}, u32[]{:S(2)}) collective-permute-start(f16[2,32,1024]{2,1,0:T(8,128)(2,1)S(1)} %get-tuple-element.209), channel_id=1, source_target_pairs={{0,8},{1,9},{2,10},{3,11},{4,12},{5,13},{6,14},{7,15},{8,0},{9,1},... | collective-permute-start | bytes 393224 | tf_op jit(solution)/shard_map/ppermute | solution.py:98
  56.6 44.4 %slice-start = ((s8[10485760]{0:T(1024)(128)(4,1)}), s8[4194304]{0:T(1024)(128)(4,1)S(1)}, s32[]{:S(2)}) async-start(s8[10485760]{0:T(1024)(128)(4,1)} %bitcast.323), calls=%async_computation | async-start | bytes 8388608
  56.8 16.0 %collective-permute-start.13 = (f16[2,64,1024]{2,1,0:T(8,128)(2,1)S(1)}, f16[2,64,1024]{2,1,0:T(8,128)(2,1)S(1)}, u32[]{:S(2)}, u32[]{:S(2)}) collective-permute-start(f16[2,64,1024]{2,1,0:T(8,128)(2,1)S(1)} %get-tuple-element.196), channel_id=1, source_target_pairs={{0,2},{1,3},{2,0},{3,1},{4,6},{5,7},{6,4},{7,5},{8,10},{9,11},{10,... | collective-permute-start | bytes 786440 | tf_op jit(solution)/shard_map/ppermute | solution.py:98
  57.9 24.4 %collective-permute-start.19 = (f16[2,128,1024]{2,1,0:T(8,128)(2,1)S(1)}, f16[2,128,1024]{2,1,0:T(8,128)(2,1)S(1)}, u32[]{:S(2)}, u32[]{:S(2)}) collective-permute-start(f16[2,128,1024]{2,1,0:T(8,128)(2,1)S(1)} %get-tuple-element.172), channel_id=1, source_target_pairs={{0,2},{1,3},{2,0},{3,1},{4,6},{5,7},{6,4},{7,5},{8,10},{9,11},{10,... | collective-permute-start | bytes 1572872 | tf_op jit(solution)/shard_map/ppermute | solution.py:98
  60.5 15.1 %collective-permute-start.12 = (f16[2,32,1024]{2,1,0:T(8,128)(2,1)S(1)}, f16[2,32,1024]{2,1,0:T(8,128)(2,1)S(1)}, u32[]{:S(2)}, u32[]{:S(2)}) collective-permute-start(f16[2,32,1024]{2,1,0:T(8,128)(2,1)S(1)} %get-tuple-element.208), channel_id=1, source_target_pairs={{0,8},{1,9},{2,10},{3,11},{4,12},{5,13},{6,14},{7,15},{8,0},{9,1},... | collective-permute-start | bytes 393224 | tf_op jit(solution)/shard_map/ppermute | solution.py:98
  62.2 38.8 %slice-start.1 = ((s8[10485760]{0:T(1024)(128)(4,1)}), s8[4194304]{0:T(1024)(128)(4,1)S(1)}, s32[]{:S(2)}) async-start(s8[10485760]{0:T(1024)(128)(4,1)} %bitcast.323), calls=%async_computation.1 | async-start | bytes 8388608
  62.3 13.8 %collective-permute-start.11 = (bf16[32,1024]{1,0:T(8,128)(2,1)S(1)}, bf16[32,1024]{1,0:T(8,128)(2,1)S(1)}, u32[]{:S(2)}, u32[]{:S(2)}) collective-permute-start(bf16[32,1024]{1,0:T(8,128)(2,1)S(1)} %fusion.107), channel_id=1, source_target_pairs={{0,8},{1,9},{2,10},{3,11},{4,12},{5,13},{6,14},{7,15},{8,0},{9,1},... | collective-permute-start | bytes 196616 | tf_op jit(solution)/shard_map/ppermute | solution.py:98
  67.4 15.6 %collective-permute-start.18 = (f16[2,64,1024]{2,1,0:T(8,128)(2,1)S(1)}, f16[2,64,1024]{2,1,0:T(8,128)(2,1)S(1)}, u32[]{:S(2)}, u32[]{:S(2)}) collective-permute-start(f16[2,64,1024]{2,1,0:T(8,128)(2,1)S(1)} %get-tuple-element.194), channel_id=1, source_target_pairs={{0,4},{1,5},{2,6},{3,7},{4,0},{5,1},{6,2},{7,3},{8,12},{9,13},{10,... | collective-permute-start | bytes 786440 | tf_op jit(solution)/shard_map/ppermute | solution.py:98
  72.9 12.8 %collective-permute-start.17 = (f16[2,32,1024]{2,1,0:T(8,128)(2,1)S(1)}, f16[2,32,1024]{2,1,0:T(8,128)(2,1)S(1)}, u32[]{:S(2)}, u32[]{:S(2)}) collective-permute-start(f16[2,32,1024]{2,1,0:T(8,128)(2,1)S(1)} %get-tuple-element.206), channel_id=1, source_target_pairs={{0,8},{1,9},{2,10},{3,11},{4,12},{5,13},{6,14},{7,15},{8,0},{9,1},... | collective-permute-start | bytes 393224 | tf_op jit(solution)/shard_map/ppermute | solution.py:98
  75.7 10.6 %collective-permute-start.16 = (bf16[32,1024]{1,0:T(8,128)(2,1)S(1)}, bf16[32,1024]{1,0:T(8,128)(2,1)S(1)}, u32[]{:S(2)}, u32[]{:S(2)}) collective-permute-start(bf16[32,1024]{1,0:T(8,128)(2,1)S(1)} %fusion.105), channel_id=1, source_target_pairs={{0,8},{1,9},{2,10},{3,11},{4,12},{5,13},{6,14},{7,15},{8,0},{9,1},... | collective-permute-start | bytes 196616 | tf_op jit(solution)/shard_map/ppermute | solution.py:98
  76.1 11.8 %collective-permute-start.15 = (bf16[64,1024]{1,0:T(8,128)(2,1)S(1)}, bf16[64,1024]{1,0:T(8,128)(2,1)S(1)}, u32[]{:S(2)}, u32[]{:S(2)}) collective-permute-start(bf16[64,1024]{1,0:T(8,128)(2,1)S(1)} %constant_dynamic-update-slice_fusion), channel_id=1, source_target_pairs={{0,4},{1,5},{2,6},{3,7},{4,0},{5,1},{6,2},{7,3},{8,12},{9,13},{10,... | collective-permute-start | bytes 393224 | tf_op jit(solution)/shard_map/ppermute | solution.py:98
  82.3 18.7 %slice-start.2 = ((s8[10485760]{0:T(1024)(128)(4,1)}), s8[2097152]{0:T(1024)(128)(4,1)S(1)}, s32[]{:S(2)}) async-start(s8[10485760]{0:T(1024)(128)(4,1)} %bitcast.323), calls=%async_computation.2 | async-start | bytes 4194304
  82.5 12.2 %collective-permute-start.24 = (f16[2,64,1024]{2,1,0:T(8,128)(2,1)S(1)}, f16[2,64,1024]{2,1,0:T(8,128)(2,1)S(1)}, u32[]{:S(2)}, u32[]{:S(2)}) collective-permute-start(f16[2,64,1024]{2,1,0:T(8,128)(2,1)S(1)} %get-tuple-element.192), channel_id=1, source_target_pairs={{0,4},{1,5},{2,6},{3,7},{4,0},{5,1},{6,2},{7,3},{8,12},{9,13},{10,... | collective-permute-start | bytes 786440 | tf_op jit(solution)/shard_map/ppermute | solution.py:98
  83.1 13.5 %collective-permute-start.23 = (f16[2,32,1024]{2,1,0:T(8,128)(2,1)S(1)}, f16[2,32,1024]{2,1,0:T(8,128)(2,1)S(1)}, u32[]{:S(2)}, u32[]{:S(2)}) collective-permute-start(f16[2,32,1024]{2,1,0:T(8,128)(2,1)S(1)} %get-tuple-element.204), channel_id=1, source_target_pairs={{0,8},{1,9},{2,10},{3,11},{4,12},{5,13},{6,14},{7,15},{8,0},{9,1},... | collective-permute-start | bytes 393224 | tf_op jit(solution)/shard_map/ppermute | solution.py:98
  85.9 12.1 %collective-permute-start.22 = (bf16[32,1024]{1,0:T(8,128)(2,1)S(1)}, bf16[32,1024]{1,0:T(8,128)(2,1)S(1)}, u32[]{:S(2)}, u32[]{:S(2)}) collective-permute-start(bf16[32,1024]{1,0:T(8,128)(2,1)S(1)} %fusion.103), channel_id=1, source_target_pairs={{0,8},{1,9},{2,10},{3,11},{4,12},{5,13},{6,14},{7,15},{8,0},{9,1},... | collective-permute-start | bytes 196616 | tf_op jit(solution)/shard_map/ppermute | solution.py:98
  86.3 13.6 %collective-permute-start.21 = (bf16[64,1024]{1,0:T(8,128)(2,1)S(1)}, bf16[64,1024]{1,0:T(8,128)(2,1)S(1)}, u32[]{:S(2)}, u32[]{:S(2)}) collective-permute-start(bf16[64,1024]{1,0:T(8,128)(2,1)S(1)} %constant_dynamic-update-slice_fusion.2), channel_id=1, source_target_pairs={{0,4},{1,5},{2,6},{3,7},{4,0},{5,1},{6,2},{7,3},{8,12},{9,13},{10,... | collective-permute-start | bytes 393224 | tf_op jit(solution)/shard_map/ppermute | solution.py:98
  88.0 12.9 %collective-permute-start.20 = (bf16[128,1024]{1,0:T(8,128)(2,1)S(1)}, bf16[128,1024]{1,0:T(8,128)(2,1)S(1)}, u32[]{:S(2)}, u32[]{:S(2)}) collective-permute-start(bf16[128,1024]{1,0:T(8,128)(2,1)S(1)} %constant_dynamic-update-slice_fusion.4), channel_id=1, source_target_pairs={{0,2},{1,3},{2,0},{3,1},{4,6},{5,7},{6,4},{7,5},{8,10},{9,11},{10,... | collective-permute-start | bytes 786440 | tf_op jit(solution)/shard_map/ppermute | solution.py:98
  94.8 9.6 %collective-permute-start.28 = (f16[2,32,1024]{2,1,0:T(8,128)(2,1)S(1)}, f16[2,32,1024]{2,1,0:T(8,128)(2,1)S(1)}, u32[]{:S(2)}, u32[]{:S(2)}) collective-permute-start(f16[2,32,1024]{2,1,0:T(8,128)(2,1)S(1)} %get-tuple-element.202), channel_id=1, source_target_pairs={{0,8},{1,9},{2,10},{3,11},{4,12},{5,13},{6,14},{7,15},{8,0},{9,1},... | collective-permute-start | bytes 393224 | tf_op jit(solution)/shard_map/ppermute | solution.py:98
  96.7 8.4 %collective-permute-start.27 = (bf16[32,1024]{1,0:T(8,128)(2,1)S(1)}, bf16[32,1024]{1,0:T(8,128)(2,1)S(1)}, u32[]{:S(2)}, u32[]{:S(2)}) collective-permute-start(bf16[32,1024]{1,0:T(8,128)(2,1)S(1)} %fusion.101), channel_id=1, source_target_pairs={{0,8},{1,9},{2,10},{3,11},{4,12},{5,13},{6,14},{7,15},{8,0},{9,1},... | collective-permute-start | bytes 196616 | tf_op jit(solution)/shard_map/ppermute | solution.py:98
  98.0 8.6 %collective-permute-start.26 = (bf16[64,1024]{1,0:T(8,128)(2,1)S(1)}, bf16[64,1024]{1,0:T(8,128)(2,1)S(1)}, u32[]{:S(2)}, u32[]{:S(2)}) collective-permute-start(bf16[64,1024]{1,0:T(8,128)(2,1)S(1)} %constant_dynamic-update-slice_fusion.6), channel_id=1, source_target_pairs={{0,4},{1,5},{2,6},{3,7},{4,0},{5,1},{6,2},{7,3},{8,12},{9,13},{10,... | collective-permute-start | bytes 393224 | tf_op jit(solution)/shard_map/ppermute | solution.py:98
  99.9 8.0 %collective-permute-start.25 = (bf16[128,1024]{1,0:T(8,128)(2,1)S(1)}, bf16[128,1024]{1,0:T(8,128)(2,1)S(1)}, u32[]{:S(2)}, u32[]{:S(2)}) collective-permute-start(bf16[128,1024]{1,0:T(8,128)(2,1)S(1)} %constant_dynamic-update-slice_fusion.8), channel_id=1, source_target_pairs={{0,2},{1,3},{2,0},{3,1},{4,6},{5,7},{6,4},{7,5},{8,10},{9,11},{10,... | collective-permute-start | bytes 786440 | tf_op jit(solution)/shard_map/ppermute | solution.py:98
  100.9 7.9 %collective-permute-start.32 = (bf16[256,1024]{1,0:T(8,128)(2,1)S(1)}, bf16[256,1024]{1,0:T(8,128)(2,1)S(1)}, u32[]{:S(2)}, u32[]{:S(2)}) collective-permute-start(bf16[256,1024]{1,0:T(8,128)(2,1)S(1)} %constant_dynamic-update-slice_fusion.10), channel_id=1, source_target_pairs={{0,1},{1,0},{2,3},{3,2},{4,5},{5,4},{6,7},{7,6},{8,9},{9,8},{10,11... | collective-permute-start | bytes 1572872 | tf_op jit(solution)/shard_map/ppermute | solution.py:98
  104.6 5.4 %collective-permute-start.31 = (bf16[32,1024]{1,0:T(8,128)(2,1)S(1)}, bf16[32,1024]{1,0:T(8,128)(2,1)S(1)}, u32[]{:S(2)}, u32[]{:S(2)}) collective-permute-start(bf16[32,1024]{1,0:T(8,128)(2,1)S(1)} %fusion.99), channel_id=1, source_target_pairs={{0,8},{1,9},{2,10},{3,11},{4,12},{5,13},{6,14},{7,15},{8,0},{9,1},... | collective-permute-start | bytes 196616 | tf_op jit(solution)/shard_map/ppermute | solution.py:98
  105.2 6.3 %collective-permute-start.30 = (bf16[64,1024]{1,0:T(8,128)(2,1)S(1)}, bf16[64,1024]{1,0:T(8,128)(2,1)S(1)}, u32[]{:S(2)}, u32[]{:S(2)}) collective-permute-start(bf16[64,1024]{1,0:T(8,128)(2,1)S(1)} %constant_dynamic-update-slice_fusion.12), channel_id=1, source_target_pairs={{0,4},{1,5},{2,6},{3,7},{4,0},{5,1},{6,2},{7,3},{8,12},{9,13},{10,... | collective-permute-start | bytes 393224 | tf_op jit(solution)/shard_map/ppermute | solution.py:98
  106.6 7.6 %collective-permute-start.29 = (bf16[128,1024]{1,0:T(8,128)(2,1)S(1)}, bf16[128,1024]{1,0:T(8,128)(2,1)S(1)}, u32[]{:S(2)}, u32[]{:S(2)}) collective-permute-start(bf16[128,1024]{1,0:T(8,128)(2,1)S(1)} %constant_dynamic-update-slice_fusion.14), channel_id=1, source_target_pairs={{0,2},{1,3},{2,0},{3,1},{4,6},{5,7},{6,4},{7,5},{8,10},{9,11},{10,... | collective-permute-start | bytes 786440 | tf_op jit(solution)/shard_map/ppermute | solution.py:98
  108.0 7.1 %collective-permute-start.35 = (bf16[256,1024]{1,0:T(8,128)(2,1)S(1)}, bf16[256,1024]{1,0:T(8,128)(2,1)S(1)}, u32[]{:S(2)}, u32[]{:S(2)}) collective-permute-start(bf16[256,1024]{1,0:T(8,128)(2,1)S(1)} %constant_dynamic-update-slice_fusion.16), channel_id=1, source_target_pairs={{0,1},{1,0},{2,3},{3,2},{4,5},{5,4},{6,7},{7,6},{8,9},{9,8},{10,11... | collective-permute-start | bytes 1572872 | tf_op jit(solution)/shard_map/ppermute | solution.py:98
  110.0 5.9 %collective-permute-start.34 = (bf16[64,1024]{1,0:T(8,128)(2,1)S(1)}, bf16[64,1024]{1,0:T(8,128)(2,1)S(1)}, u32[]{:S(2)}, u32[]{:S(2)}) collective-permute-start(bf16[64,1024]{1,0:T(8,128)(2,1)S(1)} %constant_dynamic-update-slice_fusion.18), channel_id=1, source_target_pairs={{0,4},{1,5},{2,6},{3,7},{4,0},{5,1},{6,2},{7,3},{8,12},{9,13},{10,... | collective-permute-start | bytes 393224 | tf_op jit(solution)/shard_map/ppermute | solution.py:98
  111.5 8.5 %collective-permute-start.33 = (bf16[128,1024]{1,0:T(8,128)(2,1)S(1)}, bf16[128,1024]{1,0:T(8,128)(2,1)S(1)}, u32[]{:S(2)}, u32[]{:S(2)}) collective-permute-start(bf16[128,1024]{1,0:T(8,128)(2,1)S(1)} %constant_dynamic-update-slice_fusion.20), channel_id=1, source_target_pairs={{0,2},{1,3},{2,0},{3,1},{4,6},{5,7},{6,4},{7,5},{8,10},{9,11},{10,... | collective-permute-start | bytes 786440 | tf_op jit(solution)/shard_map/ppermute | solution.py:98
  114.3 6.6 %collective-permute-start.37 = (bf16[256,1024]{1,0:T(8,128)(2,1)S(1)}, bf16[256,1024]{1,0:T(8,128)(2,1)S(1)}, u32[]{:S(2)}, u32[]{:S(2)}) collective-permute-start(bf16[256,1024]{1,0:T(8,128)(2,1)S(1)} %constant_dynamic-update-slice_fusion.22), channel_id=1, source_target_pairs={{0,1},{1,0},{2,3},{3,2},{4,5},{5,4},{6,7},{7,6},{8,9},{9,8},{10,11... | collective-permute-start | bytes 1572872 | tf_op jit(solution)/shard_map/ppermute | solution.py:98
  115.9 9.3 %collective-permute-start.36 = (bf16[128,1024]{1,0:T(8,128)(2,1)S(1)}, bf16[128,1024]{1,0:T(8,128)(2,1)S(1)}, u32[]{:S(2)}, u32[]{:S(2)}) collective-permute-start(bf16[128,1024]{1,0:T(8,128)(2,1)S(1)} %constant_dynamic-update-slice_fusion.24), channel_id=1, source_target_pairs={{0,2},{1,3},{2,0},{3,1},{4,6},{5,7},{6,4},{7,5},{8,10},{9,11},{10,... | collective-permute-start | bytes 786440 | tf_op jit(solution)/shard_map/ppermute | solution.py:98
  120.0 6.0 %collective-permute-start.38 = (bf16[256,1024]{1,0:T(8,128)(2,1)S(1)}, bf16[256,1024]{1,0:T(8,128)(2,1)S(1)}, u32[]{:S(2)}, u32[]{:S(2)}) collective-permute-start(bf16[256,1024]{1,0:T(8,128)(2,1)S(1)} %constant_dynamic-update-slice_fusion.26), channel_id=1, source_target_pairs={{0,1},{1,0},{2,3},{3,2},{4,5},{5,4},{6,7},{7,6},{8,9},{9,8},{10,11... | collective-permute-start | bytes 1572872 | tf_op jit(solution)/shard_map/ppermute | solution.py:98
  125.2 2.0 %collective-permute-start.39 = (bf16[256,1024]{1,0:T(8,128)(2,1)S(1)}, bf16[256,1024]{1,0:T(8,128)(2,1)S(1)}, u32[]{:S(2)}, u32[]{:S(2)}) collective-permute-start(bf16[256,1024]{1,0:T(8,128)(2,1)S(1)} %constant_dynamic-update-slice_fusion.28), channel_id=1, source_target_pairs={{0,1},{1,0},{2,3},{3,2},{4,5},{5,4},{6,7},{7,6},{8,9},{9,8},{10,11... | collective-permute-start | bytes 1572872 | tf_op jit(solution)/shard_map/ppermute | solution.py:98

commit v5 on v3

--- a/solution.py
+++ b/solution.py
@@ -24,7 +24,7 @@
 
 
 def schedule(levels, chunks):
-    steps = [(0, 0), (1, 0), (0, 1), *((c, 0) for c in range(2, chunks)), (1, 1), *EARLY]
+    steps = [(0, 0), (1, 0), (0, 1), (2, 0), (1, 1), (3, 0), *EARLY, *((c, 0) for c in range(4, chunks))]
     for tick in range(chunks + 2 * levels):
         steps += [(tick, 2), *(() if (tick + 2, 1) in EARLY else ((tick + 2, 1),)), *((tick + 2 - s, s) for s in range(3, 2 * levels + 1))]
     return [(c, s) for c, s in steps if 0 <= c < chunks]

time: 128 us -> 128 us (level)
  no operation moved by 1% of the time
where the time goes in v5:
time: 128 us
  starting transfers between devices  46.4 us (36%)
  waiting for transfers between devices  44.2 us (35%)
  matrix products  21.3 us (17%)
  other arithmetic  7.25 us (6%)
  Pallas kernels  4.42 us (3%)
  local copies, waits for them, and re-layouts  3.02 us (2%)
    ppermute x40, starting transfers between devices, swap(): return lax.ppermute(v, 'gx', [(i, i ^ mask) for i in range(n)])  46.4 us
    ppermute x40, waiting for transfers between devices, swap(): return lax.ppermute(v, 'gx', [(i, i ^ mask) for i in range(n)])  44.2 us
    dot_general x2, matrix products, on_device(): jnp.dot(x, v, preferred_element_type=F32).astype(F16)  14.8 us
    dot_general x5, matrix products, on_device(): lo = jnp.dot(last, down_weight[cols], preferred_element_type=F32)  3.65 us
    another operation x5, other arithmetic, split(): return (v[:, :, k].reshape(first, rows // 2, w) for k in (0, 1))  3.24 us
    dot_general x4, matrix products, on_device(): hi = jnp.dot(ins[1], down_weight[cols], preferred_element_type=F32)  2.94 us
    add x12, other arithmetic, add(): return v.astype(F32) + got.astype(F32)  2.89 us
    slice x10, local copies, waits for them, and re-layouts, on_device(): acc = jnp.stack([ins[0][:, cols], ins[1][:, cols]])  2.65 us
  transfers between devices with their start and end apart: 40, of which 16 were waited for; matrix products, arithmetic and copies ran while one was open for 12% of the time, Pallas kernels for 0%

profile of v5, /device:TPU:0, one launch (start us, length us, event | category | flops | bytes accessed | tf_op | source)
XLA Modules:
  0.0 127.6 jit_solution(5388551506549909988)
XLA Ops:
  0.0 2.4 %shard_map.46 = bf16[512,1024]{1,0:T(8,128)(2,1)} custom-call(bf16[512,1024]{1,0:T(8,128)(2,1)} %x_ref.1), custom_call_target="tpu_custom_call" | custom-call | tf_op jit(solution)/shard_map/pallas_call | solution.py:42
  2.5 8.7 %convolution_convert_fusion = f16[512,5120]{1,0:T(8,128)(2,1)S(1)} fusion(bf16[512,1024]{1,0:T(8,128)(2,1)} %shard_map.46, bf16[1024,5120]{1,0:T(8,128)(2,1)} %param.6), kind=kOutput, calls=%fused_computation | convolution fusion | flops 5371330560 | bytes 16777216 | tf_op jit(solution)/shard_map/dot_general | solution.py:120
  11.5 6.0 %convolution_convert_fusion.1 = f16[512,5120]{1,0:T(8,128)(2,1)S(1)} fusion(bf16[512,1024]{1,0:T(8,128)(2,1)S(1)} %copy-done, bf16[1024,5120]{1,0:T(8,128)(2,1)S(1)} %bitcast.367), kind=kOutput, calls=%fused_computation.1 | convolution fusion | flops 5371330560 | bytes 16777216 | tf_op jit(solution)/shard_map/dot_general | solution.py:120
  17.8 0.6 fusion.53
  18.5 0.5 collective-permute-start
  19.5 0.7 fusion.51
  20.3 1.0 collective-permute-done
  21.3 0.5 fusion.54
  22.3 0.6 fusion.52
  23.4 2.7 %collective-permute-start.1 = (f16[2,128,1024]{2,1,0:T(8,128)(2,1)S(1)}, f16[2,128,1024]{2,1,0:T(8,128)(2,1)S(1)}, u32[]{:S(2)}, u32[]{:S(2)}) collective-permute-start(f16[2,128,1024]{2,1,0:T(8,128)(2,1)S(1)} %get-tuple-element.187), channel_id=1, source_target_pairs={{0,2},{1,3},{2,0},{3,1},{4,6},{5,7},{6,4},{7,5},{8,10},{9,11},{10,... | collective-permute-start | bytes 1572872 | tf_op jit(solution)/shard_map/ppermute | solution.py:98
  26.1 0.5 convert_add_fusion
  27.1 0.7 fusion.50
  27.9 1.6 %collective-permute-start.6 = (f16[2,128,1024]{2,1,0:T(8,128)(2,1)S(1)}, f16[2,128,1024]{2,1,0:T(8,128)(2,1)S(1)}, u32[]{:S(2)}, u32[]{:S(2)}) collective-permute-start(f16[2,128,1024]{2,1,0:T(8,128)(2,1)S(1)} %bitcast.355), channel_id=1, source_target_pairs={{0,4},{1,5},{2,6},{3,7},{4,0},{5,1},{6,2},{7,3},{8,12},{9,13},{10,... | collective-permute-start | bytes 1572872 | tf_op jit(solution)/shard_map/ppermute | solution.py:98
  29.5 0.5 add_bitcast_fusion.2
  30.0 0.6 collective-permute-start.10
  31.1 0.7 fusion.49
  31.9 7.0 %collective-permute-done.1 = f16[2,128,1024]{2,1,0:T(8,128)(2,1)S(1)} collective-permute-done((f16[2,128,1024]{2,1,0:T(8,128)(2,1)S(1)}, f16[2,128,1024]{2,1,0:T(8,128)(2,1)S(1)}, u32[]{:S(2)}, u32[]{:S(2)}) %collective-permute-start.1) | collective-permute-done | bytes 524320 | tf_op jit(solution)/shard_map/ppermute | solution.py:98
  39.0 2.1 %collective-permute-start.4 = (f16[2,64,1024]{2,1,0:T(8,128)(2,1)S(1)}, f16[2,64,1024]{2,1,0:T(8,128)(2,1)S(1)}, u32[]{:S(2)}, u32[]{:S(2)}) collective-permute-start(f16[2,64,1024]{2,1,0:T(8,128)(2,1)S(1)} %get-tuple-element.199), channel_id=1, source_target_pairs={{0,4},{1,5},{2,6},{3,7},{4,0},{5,1},{6,2},{7,3},{8,12},{9,13},{10,... | collective-permute-start | bytes 786440 | tf_op jit(solution)/shard_map/ppermute | solution.py:98
  41.1 1.6 %collective-permute-done.6 = f16[2,128,1024]{2,1,0:T(8,128)(2,1)S(1)} collective-permute-done((f16[2,128,1024]{2,1,0:T(8,128)(2,1)S(1)}, f16[2,128,1024]{2,1,0:T(8,128)(2,1)S(1)}, u32[]{:S(2)}, u32[]{:S(2)}) %collective-permute-start.6) | collective-permute-done | bytes 524320 | tf_op jit(solution)/shard_map/ppermute | solution.py:98
  42.9 0.5 add_bitcast_fusion.1
  43.4 2.1 %collective-permute-start.14 = (f16[2,128,1024]{2,1,0:T(8,128)(2,1)S(1)}, f16[2,128,1024]{2,1,0:T(8,128)(2,1)S(1)}, u32[]{:S(2)}, u32[]{:S(2)}) collective-permute-start(f16[2,128,1024]{2,1,0:T(8,128)(2,1)S(1)} %get-tuple-element.174), channel_id=1, source_target_pairs={{0,2},{1,3},{2,0},{3,1},{4,6},{5,7},{6,4},{7,5},{8,10},{9,11},{10,... | collective-permute-start | bytes 1572872 | tf_op jit(solution)/shard_map/ppermute | solution.py:98
  45.5 2.3 %collective-permute-done.4 = f16[2,64,1024]{2,1,0:T(8,128)(2,1)S(1)} collective-permute-done((f16[2,64,1024]{2,1,0:T(8,128)(2,1)S(1)}, f16[2,64,1024]{2,1,0:T(8,128)(2,1)S(1)}, u32[]{:S(2)}, u32[]{:S(2)}) %collective-permute-start.4) | collective-permute-done | bytes 262176 | tf_op jit(solution)/shard_map/ppermute | solution.py:98
  47.9 2.7 %collective-permute-start.7 = (f16[2,32,1024]{2,1,0:T(8,128)(2,1)S(1)}, f16[2,32,1024]{2,1,0:T(8,128)(2,1)S(1)}, u32[]{:S(2)}, u32[]{:S(2)}) collective-permute-start(f16[2,32,1024]{2,1,0:T(8,128)(2,1)S(1)} %get-tuple-element.209), channel_id=1, source_target_pairs={{0,8},{1,9},{2,10},{3,11},{4,12},{5,13},{6,14},{7,15},{8,0},{9,1},... | collective-permute-start | bytes 393224 | tf_op jit(solution)/shard_map/ppermute | solution.py:98
  50.7 1.6 %collective-permute-start.13 = (f16[2,64,1024]{2,1,0:T(8,128)(2,1)S(1)}, f16[2,64,1024]{2,1,0:T(8,128)(2,1)S(1)}, u32[]{:S(2)}, u32[]{:S(2)}) collective-permute-start(f16[2,64,1024]{2,1,0:T(8,128)(2,1)S(1)} %get-tuple-element.196), channel_id=1, source_target_pairs={{0,4},{1,5},{2,6},{3,7},{4,0},{5,1},{6,2},{7,3},{8,12},{9,13},{10,... | collective-permute-start | bytes 786440 | tf_op jit(solution)/shard_map/ppermute | solution.py:98
  52.3 0.5 add_bitcast_fusion
  52.8 1.6 %collective-permute-start.19 = (f16[2,128,1024]{2,1,0:T(8,128)(2,1)S(1)}, f16[2,128,1024]{2,1,0:T(8,128)(2,1)S(1)}, u32[]{:S(2)}, u32[]{:S(2)}) collective-permute-start(f16[2,128,1024]{2,1,0:T(8,128)(2,1)S(1)} %get-tuple-element.172), channel_id=1, source_target_pairs={{0,2},{1,3},{2,0},{3,1},{4,6},{5,7},{6,4},{7,5},{8,10},{9,11},{10,... | collective-permute-start | bytes 1572872 | tf_op jit(solution)/shard_map/ppermute | solution.py:98
  54.4 1.3 collective-permute-done.8
  55.7 3.1 %collective-permute-start.12 = (f16[2,32,1024]{2,1,0:T(8,128)(2,1)S(1)}, f16[2,32,1024]{2,1,0:T(8,128)(2,1)S(1)}, u32[]{:S(2)}, u32[]{:S(2)}) collective-permute-start(f16[2,32,1024]{2,1,0:T(8,128)(2,1)S(1)} %get-tuple-element.208), channel_id=1, source_target_pairs={{0,8},{1,9},{2,10},{3,11},{4,12},{5,13},{6,14},{7,15},{8,0},{9,1},... | collective-permute-start | bytes 393224 | tf_op jit(solution)/shard_map/ppermute | solution.py:98
  59.1 7.8 %collective-permute-done.14 = f16[2,128,1024]{2,1,0:T(8,128)(2,1)S(1)} collective-permute-done((f16[2,128,1024]{2,1,0:T(8,128)(2,1)S(1)}, f16[2,128,1024]{2,1,0:T(8,128)(2,1)S(1)}, u32[]{:S(2)}, u32[]{:S(2)}) %collective-permute-start.14) | collective-permute-done | bytes 524320 | tf_op jit(solution)/shard_map/ppermute | solution.py:98
  67.1 2.1 %collective-permute-start.18 = (f16[2,64,1024]{2,1,0:T(8,128)(2,1)S(1)}, f16[2,64,1024]{2,1,0:T(8,128)(2,1)S(1)}, u32[]{:S(2)}, u32[]{:S(2)}) collective-permute-start(f16[2,64,1024]{2,1,0:T(8,128)(2,1)S(1)} %get-tuple-element.194), channel_id=1, source_target_pairs={{0,4},{1,5},{2,6},{3,7},{4,0},{5,1},{6,2},{7,3},{8,12},{9,13},{10,... | collective-permute-start | bytes 786440 | tf_op jit(solution)/shard_map/ppermute | solution.py:98
  69.3 2.7 %collective-permute-start.17 = (f16[2,32,1024]{2,1,0:T(8,128)(2,1)S(1)}, f16[2,32,1024]{2,1,0:T(8,128)(2,1)S(1)}, u32[]{:S(2)}, u32[]{:S(2)}) collective-permute-start(f16[2,32,1024]{2,1,0:T(8,128)(2,1)S(1)} %get-tuple-element.206), channel_id=1, source_target_pairs={{0,8},{1,9},{2,10},{3,11},{4,12},{5,13},{6,14},{7,15},{8,0},{9,1},... | collective-permute-start | bytes 393224 | tf_op jit(solution)/shard_map/ppermute | solution.py:98
  72.6 5.2 %collective-permute-done.19 = f16[2,128,1024]{2,1,0:T(8,128)(2,1)S(1)} collective-permute-done((f16[2,128,1024]{2,1,0:T(8,128)(2,1)S(1)}, f16[2,128,1024]{2,1,0:T(8,128)(2,1)S(1)}, u32[]{:S(2)}, u32[]{:S(2)}) %collective-permute-start.19) | collective-permute-done | bytes 524320 | tf_op jit(solution)/shard_map/ppermute | solution.py:98
  78.0 1.9 %collective-permute-start.24 = (f16[2,64,1024]{2,1,0:T(8,128)(2,1)S(1)}, f16[2,64,1024]{2,1,0:T(8,128)(2,1)S(1)}, u32[]{:S(2)}, u32[]{:S(2)}) collective-permute-start(f16[2,64,1024]{2,1,0:T(8,128)(2,1)S(1)} %get-tuple-element.192), channel_id=1, source_target_pairs={{0,4},{1,5},{2,6},{3,7},{4,0},{5,1},{6,2},{7,3},{8,12},{9,13},{10,... | collective-permute-start | bytes 786440 | tf_op jit(solution)/shard_map/ppermute | solution.py:98
  79.8 0.6 collective-permute-done.18
  80.5 2.0 %collective-permute-start.23 = (f16[2,32,1024]{2,1,0:T(8,128)(2,1)S(1)}, f16[2,32,1024]{2,1,0:T(8,128)(2,1)S(1)}, u32[]{:S(2)}, u32[]{:S(2)}) collective-permute-start(f16[2,32,1024]{2,1,0:T(8,128)(2,1)S(1)} %get-tuple-element.204), channel_id=1, source_target_pairs={{0,8},{1,9},{2,10},{3,11},{4,12},{5,13},{6,14},{7,15},{8,0},{9,1},... | collective-permute-start | bytes 393224 | tf_op jit(solution)/shard_map/ppermute | solution.py:98
  82.7 1.0 collective-permute-start.22
  83.7 1.3 %collective-permute-start.21 = (bf16[64,1024]{1,0:T(8,128)(2,1)S(1)}, bf16[64,1024]{1,0:T(8,128)(2,1)S(1)}, u32[]{:S(2)}, u32[]{:S(2)}) collective-permute-start(bf16[64,1024]{1,0:T(8,128)(2,1)S(1)} %constant_dynamic-update-slice_fusion.2), channel_id=1, source_target_pairs={{0,4},{1,5},{2,6},{3,7},{4,0},{5,1},{6,2},{7,3},{8,12},{9,13},{10,... | collective-permute-start | bytes 393224 | tf_op jit(solution)/shard_map/ppermute | solution.py:98
  85.0 1.6 %collective-permute-start.20 = (bf16[128,1024]{1,0:T(8,128)(2,1)S(1)}, bf16[128,1024]{1,0:T(8,128)(2,1)S(1)}, u32[]{:S(2)}, u32[]{:S(2)}) collective-permute-start(bf16[128,1024]{1,0:T(8,128)(2,1)S(1)} %constant_dynamic-update-slice_fusion.4), channel_id=1, source_target_pairs={{0,2},{1,3},{2,0},{3,1},{4,6},{5,7},{6,4},{7,5},{8,10},{9,11},{10,... | collective-permute-start | bytes 786440 | tf_op jit(solution)/shard_map/ppermute | solution.py:98
  86.6 6.4 %collective-permute-done.24 = f16[2,64,1024]{2,1,0:T(8,128)(2,1)S(1)} collective-permute-done((f16[2,64,1024]{2,1,0:T(8,128)(2,1)S(1)}, f16[2,64,1024]{2,1,0:T(8,128)(2,1)S(1)}, u32[]{:S(2)}, u32[]{:S(2)}) %collective-permute-start.24) | collective-permute-done | bytes 262176 | tf_op jit(solution)/shard_map/ppermute | solution.py:98
  93.1 1.7 %collective-permute-start.28 = (f16[2,32,1024]{2,1,0:T(8,128)(2,1)S(1)}, f16[2,32,1024]{2,1,0:T(8,128)(2,1)S(1)}, u32[]{:S(2)}, u32[]{:S(2)}) collective-permute-start(f16[2,32,1024]{2,1,0:T(8,128)(2,1)S(1)} %get-tuple-element.202), channel_id=1, source_target_pairs={{0,8},{1,9},{2,10},{3,11},{4,12},{5,13},{6,14},{7,15},{8,0},{9,1},... | collective-permute-start | bytes 393224 | tf_op jit(solution)/shard_map/ppermute | solution.py:98
  95.0 1.3 %collective-permute-start.27 = (bf16[32,1024]{1,0:T(8,128)(2,1)S(1)}, bf16[32,1024]{1,0:T(8,128)(2,1)S(1)}, u32[]{:S(2)}, u32[]{:S(2)}) collective-permute-start(bf16[32,1024]{1,0:T(8,128)(2,1)S(1)} %fusion.101), channel_id=1, source_target_pairs={{0,8},{1,9},{2,10},{3,11},{4,12},{5,13},{6,14},{7,15},{8,0},{9,1},... | collective-permute-start | bytes 196616 | tf_op jit(solution)/shard_map/ppermute | solution.py:98
  96.3 1.3 %collective-permute-start.26 = (bf16[64,1024]{1,0:T(8,128)(2,1)S(1)}, bf16[64,1024]{1,0:T(8,128)(2,1)S(1)}, u32[]{:S(2)}, u32[]{:S(2)}) collective-permute-start(bf16[64,1024]{1,0:T(8,128)(2,1)S(1)} %constant_dynamic-update-slice_fusion.6), channel_id=1, source_target_pairs={{0,4},{1,5},{2,6},{3,7},{4,0},{5,1},{6,2},{7,3},{8,12},{9,13},{10,... | collective-permute-start | bytes 393224 | tf_op jit(solution)/shard_map/ppermute | solution.py:98
  97.7 1.6 %collective-permute-start.25 = (bf16[128,1024]{1,0:T(8,128)(2,1)S(1)}, bf16[128,1024]{1,0:T(8,128)(2,1)S(1)}, u32[]{:S(2)}, u32[]{:S(2)}) collective-permute-start(bf16[128,1024]{1,0:T(8,128)(2,1)S(1)} %constant_dynamic-update-slice_fusion.8), channel_id=1, source_target_pairs={{0,2},{1,3},{2,0},{3,1},{4,6},{5,7},{6,4},{7,5},{8,10},{9,11},{10,... | collective-permute-start | bytes 786440 | tf_op jit(solution)/shard_map/ppermute | solution.py:98
  99.7 0.7 fusion.16
  100.4 2.0 %collective-permute-done.28 = f16[2,32,1024]{2,1,0:T(8,128)(2,1)S(1)} collective-permute-done((f16[2,32,1024]{2,1,0:T(8,128)(2,1)S(1)}, f16[2,32,1024]{2,1,0:T(8,128)(2,1)S(1)}, u32[]{:S(2)}, u32[]{:S(2)}) %collective-permute-start.28) | collective-permute-done | bytes 131104 | tf_op jit(solution)/shard_map/ppermute | solution.py:98
  102.5 1.0 collective-permute-start.31
  103.5 2.3 %collective-permute-start.30 = (bf16[64,1024]{1,0:T(8,128)(2,1)S(1)}, bf16[64,1024]{1,0:T(8,128)(2,1)S(1)}, u32[]{:S(2)}, u32[]{:S(2)}) collective-permute-start(bf16[64,1024]{1,0:T(8,128)(2,1)S(1)} %constant_dynamic-update-slice_fusion.12), channel_id=1, source_target_pairs={{0,4},{1,5},{2,6},{3,7},{4,0},{5,1},{6,2},{7,3},{8,12},{9,13},{10,... | collective-permute-start | bytes 393224 | tf_op jit(solution)/shard_map/ppermute | solution.py:98
  105.9 1.6 %collective-permute-start.29 = (bf16[128,1024]{1,0:T(8,128)(2,1)S(1)}, bf16[128,1024]{1,0:T(8,128)(2,1)S(1)}, u32[]{:S(2)}, u32[]{:S(2)}) collective-permute-start(bf16[128,1024]{1,0:T(8,128)(2,1)S(1)} %constant_dynamic-update-slice_fusion.14), channel_id=1, source_target_pairs={{0,2},{1,3},{2,0},{3,1},{4,6},{5,7},{6,4},{7,5},{8,10},{9,11},{10,... | collective-permute-start | bytes 786440 | tf_op jit(solution)/shard_map/ppermute | solution.py:98
  107.6 0.7 fusion.18
  108.3 0.7 fusion.14
  109.2 0.7 collective-permute-done.30
  109.9 1.2 collective-permute-start.33
  111.0 1.2 collective-permute-done.29
  112.4 0.7 fusion.24
  113.2 0.7 fusion.21
  113.9 1.1 collective-permute-done.34
  115.1 1.3 %collective-permute-start.36 = (bf16[128,1024]{1,0:T(8,128)(2,1)S(1)}, bf16[128,1024]{1,0:T(8,128)(2,1)S(1)}, u32[]{:S(2)}, u32[]{:S(2)}) collective-permute-start(bf16[128,1024]{1,0:T(8,128)(2,1)S(1)} %constant_dynamic-update-slice_fusion.24), channel_id=1, source_target_pairs={{0,2},{1,3},{2,0},{3,1},{4,6},{5,7},{6,4},{7,5},{8,10},{9,11},{10,... | collective-permute-start | bytes 786440 | tf_op jit(solution)/shard_map/ppermute | solution.py:98
  116.4 1.7 %collective-permute-done.33 = bf16[128,1024]{1,0:T(8,128)(2,1)S(1)} collective-permute-done((bf16[128,1024]{1,0:T(8,128)(2,1)S(1)}, bf16[128,1024]{1,0:T(8,128)(2,1)S(1)}, u32[]{:S(2)}, u32[]{:S(2)}) %collective-permute-start.33) | collective-permute-done | bytes 262176 | tf_op jit(solution)/shard_map/ppermute | solution.py:98
  118.3 0.7 fusion.30
  119.0 0.7 fusion.27
  119.8 3.8 %collective-permute-done.36 = bf16[128,1024]{1,0:T(8,128)(2,1)S(1)} collective-permute-done((bf16[128,1024]{1,0:T(8,128)(2,1)S(1)}, bf16[128,1024]{1,0:T(8,128)(2,1)S(1)}, u32[]{:S(2)}, u32[]{:S(2)}) %collective-permute-start.36) | collective-permute-done | bytes 262176 | tf_op jit(solution)/shard_map/ppermute | solution.py:98
  123.7 0.7 fusion.36.lo_ref
  124.5 0.7 fusion.33.hi_ref
  125.6 2.0 %shard_map.47 = bf16[512,1024]{1,0:T(8,128)(2,1)} custom-call(f32[256,1024]{1,0:T(8,128)S(1)} %fusion.36.lo_ref, f32[256,1024]{1,0:T(8,128)S(1)} %fusion.33.hi_ref, bf16[256,1024]{1,0:T(8,128)(2,1)S(1)} %collective-permute-done.39.hidden_ref, bf16[5120,1024]{1,0:T(8,128)(2,1)S(1)} %bitcast.324), custom_call_target="tpu_custom_call" | custom-call | tf_op jit(solution)/shard_map/pallas_call | solution.py:69
  (115 shorter events, 7.1 us)
Async XLA Ops:
  0.0 11.5 %slice-start.3 = ((s8[10485760]{0:T(1024)(128)(4,1)}), s8[2097152]{0:T(1024)(128)(4,1)S(1)}, s32[]{:S(2)}) async-start(s8[10485760]{0:T(1024)(128)(4,1)} %bitcast.366), calls=%async_computation.3 | async-start | bytes 4194304
  2.4 9.0 %copy-start = (bf16[512,1024]{1,0:T(8,128)(2,1)S(1)}, bf16[512,1024]{1,0:T(8,128)(2,1)}, u32[]{:S(2)}) copy-start(bf16[512,1024]{1,0:T(8,128)(2,1)} %shard_map.46) | copy-start | bytes 3145732
  2.4 9.0 %slice-start.4 = ((s8[10485760]{0:T(1024)(128)(4,1)}), s8[4194304]{0:T(1024)(128)(4,1)S(1)}, s32[]{:S(2)}) async-start(s8[10485760]{0:T(1024)(128)(4,1)} %bitcast.366), calls=%async_computation.4 | async-start | bytes 8388608
  2.4 9.0 %slice-start.5 = ((s8[10485760]{0:T(1024)(128)(4,1)}), s8[4194304]{0:T(1024)(128)(4,1)S(1)}, s32[]{:S(2)}) async-start(s8[10485760]{0:T(1024)(128)(4,1)} %bitcast.366), calls=%async_computation.5 | async-start | bytes 8388608
  18.5 2.8 %collective-permute-start = (f16[2,256,1024]{2,1,0:T(8,128)(2,1)S(1)}, f16[2,256,1024]{2,1,0:T(8,128)(2,1)S(1)}, u32[]{:S(2)}, u32[]{:S(2)}) collective-permute-start(f16[2,256,1024]{2,1,0:T(8,128)(2,1)S(1)} %get-tuple-element.189), channel_id=1, source_target_pairs={{0,1},{1,0},{2,3},{3,2},{4,5},{5,4},{6,7},{7,6},{8,9},{9,8},{10,11... | collective-permute-start | bytes 3145736 | tf_op jit(solution)/shard_map/ppermute | solution.py:98
  20.2 5.9 %collective-permute-start.3 = (f16[2,256,1024]{2,1,0:T(8,128)(2,1)S(1)}, f16[2,256,1024]{2,1,0:T(8,128)(2,1)S(1)}, u32[]{:S(2)}, u32[]{:S(2)}) collective-permute-start(f16[2,256,1024]{2,1,0:T(8,128)(2,1)S(1)} %get-tuple-element.184), channel_id=1, source_target_pairs={{0,1},{1,0},{2,3},{3,2},{4,5},{5,4},{6,7},{7,6},{8,9},{9,8},{10,11... | collective-permute-start | bytes 3145736 | tf_op jit(solution)/shard_map/ppermute | solution.py:98
  22.9 6.5 %collective-permute-start.2 = (f16[2,256,1024]{2,1,0:T(8,128)(2,1)S(1)}, f16[2,256,1024]{2,1,0:T(8,128)(2,1)S(1)}, u32[]{:S(2)}, u32[]{:S(2)}) collective-permute-start(f16[2,256,1024]{2,1,0:T(8,128)(2,1)S(1)} %get-tuple-element.185), channel_id=1, source_target_pairs={{0,1},{1,0},{2,3},{3,2},{4,5},{5,4},{6,7},{7,6},{8,9},{9,8},{10,11... | collective-permute-start | bytes 3145736 | tf_op jit(solution)/shard_map/ppermute | solution.py:98
  23.4 15.4 %collective-permute-start.1 = (f16[2,128,1024]{2,1,0:T(8,128)(2,1)S(1)}, f16[2,128,1024]{2,1,0:T(8,128)(2,1)S(1)}, u32[]{:S(2)}, u32[]{:S(2)}) collective-permute-start(f16[2,128,1024]{2,1,0:T(8,128)(2,1)S(1)} %get-tuple-element.187), channel_id=1, source_target_pairs={{0,2},{1,3},{2,0},{3,1},{4,6},{5,7},{6,4},{7,5},{8,10},{9,11},{10,... | collective-permute-start | bytes 1572872 | tf_op jit(solution)/shard_map/ppermute | solution.py:98
  27.8 15.1 %collective-permute-start.5 = (f16[2,256,1024]{2,1,0:T(8,128)(2,1)S(1)}, f16[2,256,1024]{2,1,0:T(8,128)(2,1)S(1)}, u32[]{:S(2)}, u32[]{:S(2)}) collective-permute-start(f16[2,256,1024]{2,1,0:T(8,128)(2,1)S(1)} %get-tuple-element.182), channel_id=1, source_target_pairs={{0,1},{1,0},{2,3},{3,2},{4,5},{5,4},{6,7},{7,6},{8,9},{9,8},{10,11... | collective-permute-start | bytes 3145736 | tf_op jit(solution)/shard_map/ppermute | solution.py:98
  27.9 14.7 %collective-permute-start.6 = (f16[2,128,1024]{2,1,0:T(8,128)(2,1)S(1)}, f16[2,128,1024]{2,1,0:T(8,128)(2,1)S(1)}, u32[]{:S(2)}, u32[]{:S(2)}) collective-permute-start(f16[2,128,1024]{2,1,0:T(8,128)(2,1)S(1)} %bitcast.355), channel_id=1, source_target_pairs={{0,4},{1,5},{2,6},{3,7},{4,0},{5,1},{6,2},{7,3},{8,12},{9,13},{10,... | collective-permute-start | bytes 1572872 | tf_op jit(solution)/shard_map/ppermute | solution.py:98
  30.0 20.5 %collective-permute-start.10 = (f16[2,128,1024]{2,1,0:T(8,128)(2,1)S(1)}, f16[2,128,1024]{2,1,0:T(8,128)(2,1)S(1)}, u32[]{:S(2)}, u32[]{:S(2)}) collective-permute-start(f16[2,128,1024]{2,1,0:T(8,128)(2,1)S(1)} %get-tuple-element.176), channel_id=1, source_target_pairs={{0,2},{1,3},{2,0},{3,1},{4,6},{5,7},{6,4},{7,5},{8,10},{9,11},{10,... | collective-permute-start | bytes 1572872 | tf_op jit(solution)/shard_map/ppermute | solution.py:98
  31.8 20.6 %collective-permute-start.9 = (f16[2,256,1024]{2,1,0:T(8,128)(2,1)S(1)}, f16[2,256,1024]{2,1,0:T(8,128)(2,1)S(1)}, u32[]{:S(2)}, u32[]{:S(2)}) collective-permute-start(f16[2,256,1024]{2,1,0:T(8,128)(2,1)S(1)} %get-tuple-element.178), channel_id=1, source_target_pairs={{0,1},{1,0},{2,3},{3,2},{4,5},{5,4},{6,7},{7,6},{8,9},{9,8},{10,11... | collective-permute-start | bytes 3145736 | tf_op jit(solution)/shard_map/ppermute | solution.py:98
  39.0 8.8 %collective-permute-start.4 = (f16[2,64,1024]{2,1,0:T(8,128)(2,1)S(1)}, f16[2,64,1024]{2,1,0:T(8,128)(2,1)S(1)}, u32[]{:S(2)}, u32[]{:S(2)}) collective-permute-start(f16[2,64,1024]{2,1,0:T(8,128)(2,1)S(1)} %get-tuple-element.199), channel_id=1, source_target_pairs={{0,4},{1,5},{2,6},{3,7},{4,0},{5,1},{6,2},{7,3},{8,12},{9,13},{10,... | collective-permute-start | bytes 786440 | tf_op jit(solution)/shard_map/ppermute | solution.py:98
  42.8 12.9 %collective-permute-start.8 = (f16[2,64,1024]{2,1,0:T(8,128)(2,1)S(1)}, f16[2,64,1024]{2,1,0:T(8,128)(2,1)S(1)}, u32[]{:S(2)}, u32[]{:S(2)}) collective-permute-start(f16[2,64,1024]{2,1,0:T(8,128)(2,1)S(1)} %get-tuple-element.198), channel_id=1, source_target_pairs={{0,2},{1,3},{2,0},{3,1},{4,6},{5,7},{6,4},{7,5},{8,10},{9,11},{10,... | collective-permute-start | bytes 786440 | tf_op jit(solution)/shard_map/ppermute | solution.py:98
  43.4 23.5 %collective-permute-start.14 = (f16[2,128,1024]{2,1,0:T(8,128)(2,1)S(1)}, f16[2,128,1024]{2,1,0:T(8,128)(2,1)S(1)}, u32[]{:S(2)}, u32[]{:S(2)}) collective-permute-start(f16[2,128,1024]{2,1,0:T(8,128)(2,1)S(1)} %get-tuple-element.174), channel_id=1, source_target_pairs={{0,2},{1,3},{2,0},{3,1},{4,6},{5,7},{6,4},{7,5},{8,10},{9,11},{10,... | collective-permute-start | bytes 1572872 | tf_op jit(solution)/shard_map/ppermute | solution.py:98
  47.9 11.0 %collective-permute-start.7 = (f16[2,32,1024]{2,1,0:T(8,128)(2,1)S(1)}, f16[2,32,1024]{2,1,0:T(8,128)(2,1)S(1)}, u32[]{:S(2)}, u32[]{:S(2)}) collective-permute-start(f16[2,32,1024]{2,1,0:T(8,128)(2,1)S(1)} %get-tuple-element.209), channel_id=1, source_target_pairs={{0,8},{1,9},{2,10},{3,11},{4,12},{5,13},{6,14},{7,15},{8,0},{9,1},... | collective-permute-start | bytes 393224 | tf_op jit(solution)/shard_map/ppermute | solution.py:98
  50.5 48.9 %slice-start = ((s8[10485760]{0:T(1024)(128)(4,1)}), s8[4194304]{0:T(1024)(128)(4,1)S(1)}, s32[]{:S(2)}) async-start(s8[10485760]{0:T(1024)(128)(4,1)} %bitcast.323), calls=%async_computation | async-start | bytes 8388608
  50.7 18.5 %collective-permute-start.13 = (f16[2,64,1024]{2,1,0:T(8,128)(2,1)S(1)}, f16[2,64,1024]{2,1,0:T(8,128)(2,1)S(1)}, u32[]{:S(2)}, u32[]{:S(2)}) collective-permute-start(f16[2,64,1024]{2,1,0:T(8,128)(2,1)S(1)} %get-tuple-element.196), channel_id=1, source_target_pairs={{0,4},{1,5},{2,6},{3,7},{4,0},{5,1},{6,2},{7,3},{8,12},{9,13},{10,... | collective-permute-start | bytes 786440 | tf_op jit(solution)/shard_map/ppermute | solution.py:98
  52.8 25.0 %collective-permute-start.19 = (f16[2,128,1024]{2,1,0:T(8,128)(2,1)S(1)}, f16[2,128,1024]{2,1,0:T(8,128)(2,1)S(1)}, u32[]{:S(2)}, u32[]{:S(2)}) collective-permute-start(f16[2,128,1024]{2,1,0:T(8,128)(2,1)S(1)} %get-tuple-element.172), channel_id=1, source_target_pairs={{0,2},{1,3},{2,0},{3,1},{4,6},{5,7},{6,4},{7,5},{8,10},{9,11},{10,... | collective-permute-start | bytes 1572872 | tf_op jit(solution)/shard_map/ppermute | solution.py:98
  55.7 16.2 %collective-permute-start.12 = (f16[2,32,1024]{2,1,0:T(8,128)(2,1)S(1)}, f16[2,32,1024]{2,1,0:T(8,128)(2,1)S(1)}, u32[]{:S(2)}, u32[]{:S(2)}) collective-permute-start(f16[2,32,1024]{2,1,0:T(8,128)(2,1)S(1)} %get-tuple-element.208), channel_id=1, source_target_pairs={{0,8},{1,9},{2,10},{3,11},{4,12},{5,13},{6,14},{7,15},{8,0},{9,1},... | collective-permute-start | bytes 393224 | tf_op jit(solution)/shard_map/ppermute | solution.py:98
  58.9 40.6 %slice-start.1 = ((s8[10485760]{0:T(1024)(128)(4,1)}), s8[4194304]{0:T(1024)(128)(4,1)S(1)}, s32[]{:S(2)}) async-start(s8[10485760]{0:T(1024)(128)(4,1)} %bitcast.323), calls=%async_computation.1 | async-start | bytes 8388608
  59.0 13.5 %collective-permute-start.11 = (bf16[32,1024]{1,0:T(8,128)(2,1)S(1)}, bf16[32,1024]{1,0:T(8,128)(2,1)S(1)}, u32[]{:S(2)}, u32[]{:S(2)}) collective-permute-start(bf16[32,1024]{1,0:T(8,128)(2,1)S(1)} %fusion.107), channel_id=1, source_target_pairs={{0,8},{1,9},{2,10},{3,11},{4,12},{5,13},{6,14},{7,15},{8,0},{9,1},... | collective-permute-start | bytes 196616 | tf_op jit(solution)/shard_map/ppermute | solution.py:98
  67.1 13.4 %collective-permute-start.18 = (f16[2,64,1024]{2,1,0:T(8,128)(2,1)S(1)}, f16[2,64,1024]{2,1,0:T(8,128)(2,1)S(1)}, u32[]{:S(2)}, u32[]{:S(2)}) collective-permute-start(f16[2,64,1024]{2,1,0:T(8,128)(2,1)S(1)} %get-tuple-element.194), channel_id=1, source_target_pairs={{0,4},{1,5},{2,6},{3,7},{4,0},{5,1},{6,2},{7,3},{8,12},{9,13},{10,... | collective-permute-start | bytes 786440 | tf_op jit(solution)/shard_map/ppermute | solution.py:98
  69.3 13.3 %collective-permute-start.17 = (f16[2,32,1024]{2,1,0:T(8,128)(2,1)S(1)}, f16[2,32,1024]{2,1,0:T(8,128)(2,1)S(1)}, u32[]{:S(2)}, u32[]{:S(2)}) collective-permute-start(f16[2,32,1024]{2,1,0:T(8,128)(2,1)S(1)} %get-tuple-element.206), channel_id=1, source_target_pairs={{0,8},{1,9},{2,10},{3,11},{4,12},{5,13},{6,14},{7,15},{8,0},{9,1},... | collective-permute-start | bytes 393224 | tf_op jit(solution)/shard_map/ppermute | solution.py:98
  72.0 11.7 %collective-permute-start.16 = (bf16[32,1024]{1,0:T(8,128)(2,1)S(1)}, bf16[32,1024]{1,0:T(8,128)(2,1)S(1)}, u32[]{:S(2)}, u32[]{:S(2)}) collective-permute-start(bf16[32,1024]{1,0:T(8,128)(2,1)S(1)} %fusion.105), channel_id=1, source_target_pairs={{0,8},{1,9},{2,10},{3,11},{4,12},{5,13},{6,14},{7,15},{8,0},{9,1},... | collective-permute-start | bytes 196616 | tf_op jit(solution)/shard_map/ppermute | solution.py:98
  72.4 12.6 %collective-permute-start.15 = (bf16[64,1024]{1,0:T(8,128)(2,1)S(1)}, bf16[64,1024]{1,0:T(8,128)(2,1)S(1)}, u32[]{:S(2)}, u32[]{:S(2)}) collective-permute-start(bf16[64,1024]{1,0:T(8,128)(2,1)S(1)} %constant_dynamic-update-slice_fusion), channel_id=1, source_target_pairs={{0,4},{1,5},{2,6},{3,7},{4,0},{5,1},{6,2},{7,3},{8,12},{9,13},{10,... | collective-permute-start | bytes 393224 | tf_op jit(solution)/shard_map/ppermute | solution.py:98
  77.8 21.6 %slice-start.2 = ((s8[10485760]{0:T(1024)(128)(4,1)}), s8[2097152]{0:T(1024)(128)(4,1)S(1)}, s32[]{:S(2)}) async-start(s8[10485760]{0:T(1024)(128)(4,1)} %bitcast.323), calls=%async_computation.2 | async-start | bytes 4194304
  78.0 15.1 %collective-permute-start.24 = (f16[2,64,1024]{2,1,0:T(8,128)(2,1)S(1)}, f16[2,64,1024]{2,1,0:T(8,128)(2,1)S(1)}, u32[]{:S(2)}, u32[]{:S(2)}) collective-permute-start(f16[2,64,1024]{2,1,0:T(8,128)(2,1)S(1)} %get-tuple-element.192), channel_id=1, source_target_pairs={{0,4},{1,5},{2,6},{3,7},{4,0},{5,1},{6,2},{7,3},{8,12},{9,13},{10,... | collective-permute-start | bytes 786440 | tf_op jit(solution)/shard_map/ppermute | solution.py:98
  80.5 14.3 %collective-permute-start.23 = (f16[2,32,1024]{2,1,0:T(8,128)(2,1)S(1)}, f16[2,32,1024]{2,1,0:T(8,128)(2,1)S(1)}, u32[]{:S(2)}, u32[]{:S(2)}) collective-permute-start(f16[2,32,1024]{2,1,0:T(8,128)(2,1)S(1)} %get-tuple-element.204), channel_id=1, source_target_pairs={{0,8},{1,9},{2,10},{3,11},{4,12},{5,13},{6,14},{7,15},{8,0},{9,1},... | collective-permute-start | bytes 393224 | tf_op jit(solution)/shard_map/ppermute | solution.py:98
  82.7 13.6 %collective-permute-start.22 = (bf16[32,1024]{1,0:T(8,128)(2,1)S(1)}, bf16[32,1024]{1,0:T(8,128)(2,1)S(1)}, u32[]{:S(2)}, u32[]{:S(2)}) collective-permute-start(bf16[32,1024]{1,0:T(8,128)(2,1)S(1)} %fusion.103), channel_id=1, source_target_pairs={{0,8},{1,9},{2,10},{3,11},{4,12},{5,13},{6,14},{7,15},{8,0},{9,1},... | collective-permute-start | bytes 196616 | tf_op jit(solution)/shard_map/ppermute | solution.py:98
  83.7 13.9 %collective-permute-start.21 = (bf16[64,1024]{1,0:T(8,128)(2,1)S(1)}, bf16[64,1024]{1,0:T(8,128)(2,1)S(1)}, u32[]{:S(2)}, u32[]{:S(2)}) collective-permute-start(bf16[64,1024]{1,0:T(8,128)(2,1)S(1)} %constant_dynamic-update-slice_fusion.2), channel_id=1, source_target_pairs={{0,4},{1,5},{2,6},{3,7},{4,0},{5,1},{6,2},{7,3},{8,12},{9,13},{10,... | collective-permute-start | bytes 393224 | tf_op jit(solution)/shard_map/ppermute | solution.py:98
  85.0 14.2 %collective-permute-start.20 = (bf16[128,1024]{1,0:T(8,128)(2,1)S(1)}, bf16[128,1024]{1,0:T(8,128)(2,1)S(1)}, u32[]{:S(2)}, u32[]{:S(2)}) collective-permute-start(bf16[128,1024]{1,0:T(8,128)(2,1)S(1)} %constant_dynamic-update-slice_fusion.4), channel_id=1, source_target_pairs={{0,2},{1,3},{2,0},{3,1},{4,6},{5,7},{6,4},{7,5},{8,10},{9,11},{10,... | collective-permute-start | bytes 786440 | tf_op jit(solution)/shard_map/ppermute | solution.py:98
  93.1 9.2 %collective-permute-start.28 = (f16[2,32,1024]{2,1,0:T(8,128)(2,1)S(1)}, f16[2,32,1024]{2,1,0:T(8,128)(2,1)S(1)}, u32[]{:S(2)}, u32[]{:S(2)}) collective-permute-start(f16[2,32,1024]{2,1,0:T(8,128)(2,1)S(1)} %get-tuple-element.202), channel_id=1, source_target_pairs={{0,8},{1,9},{2,10},{3,11},{4,12},{5,13},{6,14},{7,15},{8,0},{9,1},... | collective-permute-start | bytes 393224 | tf_op jit(solution)/shard_map/ppermute | solution.py:98
  95.0 8.5 %collective-permute-start.27 = (bf16[32,1024]{1,0:T(8,128)(2,1)S(1)}, bf16[32,1024]{1,0:T(8,128)(2,1)S(1)}, u32[]{:S(2)}, u32[]{:S(2)}) collective-permute-start(bf16[32,1024]{1,0:T(8,128)(2,1)S(1)} %fusion.101), channel_id=1, source_target_pairs={{0,8},{1,9},{2,10},{3,11},{4,12},{5,13},{6,14},{7,15},{8,0},{9,1},... | collective-permute-start | bytes 196616 | tf_op jit(solution)/shard_map/ppermute | solution.py:98
  96.3 9.5 %collective-permute-start.26 = (bf16[64,1024]{1,0:T(8,128)(2,1)S(1)}, bf16[64,1024]{1,0:T(8,128)(2,1)S(1)}, u32[]{:S(2)}, u32[]{:S(2)}) collective-permute-start(bf16[64,1024]{1,0:T(8,128)(2,1)S(1)} %constant_dynamic-update-slice_fusion.6), channel_id=1, source_target_pairs={{0,4},{1,5},{2,6},{3,7},{4,0},{5,1},{6,2},{7,3},{8,12},{9,13},{10,... | collective-permute-start | bytes 393224 | tf_op jit(solution)/shard_map/ppermute | solution.py:98
  97.7 9.8 %collective-permute-start.25 = (bf16[128,1024]{1,0:T(8,128)(2,1)S(1)}, bf16[128,1024]{1,0:T(8,128)(2,1)S(1)}, u32[]{:S(2)}, u32[]{:S(2)}) collective-permute-start(bf16[128,1024]{1,0:T(8,128)(2,1)S(1)} %constant_dynamic-update-slice_fusion.8), channel_id=1, source_target_pairs={{0,2},{1,3},{2,0},{3,1},{4,6},{5,7},{6,4},{7,5},{8,10},{9,11},{10,... | collective-permute-start | bytes 786440 | tf_op jit(solution)/shard_map/ppermute | solution.py:98
  99.3 9.0 %collective-permute-start.32 = (bf16[256,1024]{1,0:T(8,128)(2,1)S(1)}, bf16[256,1024]{1,0:T(8,128)(2,1)S(1)}, u32[]{:S(2)}, u32[]{:S(2)}) collective-permute-start(bf16[256,1024]{1,0:T(8,128)(2,1)S(1)} %constant_dynamic-update-slice_fusion.10), channel_id=1, source_target_pairs={{0,1},{1,0},{2,3},{3,2},{4,5},{5,4},{6,7},{7,6},{8,9},{9,8},{10,11... | collective-permute-start | bytes 1572872 | tf_op jit(solution)/shard_map/ppermute | solution.py:98
  102.5 6.6 %collective-permute-start.31 = (bf16[32,1024]{1,0:T(8,128)(2,1)S(1)}, bf16[32,1024]{1,0:T(8,128)(2,1)S(1)}, u32[]{:S(2)}, u32[]{:S(2)}) collective-permute-start(bf16[32,1024]{1,0:T(8,128)(2,1)S(1)} %fusion.99), channel_id=1, source_target_pairs={{0,8},{1,9},{2,10},{3,11},{4,12},{5,13},{6,14},{7,15},{8,0},{9,1},... | collective-permute-start | bytes 196616 | tf_op jit(solution)/shard_map/ppermute | solution.py:98
  103.5 6.4 %collective-permute-start.30 = (bf16[64,1024]{1,0:T(8,128)(2,1)S(1)}, bf16[64,1024]{1,0:T(8,128)(2,1)S(1)}, u32[]{:S(2)}, u32[]{:S(2)}) collective-permute-start(bf16[64,1024]{1,0:T(8,128)(2,1)S(1)} %constant_dynamic-update-slice_fusion.12), channel_id=1, source_target_pairs={{0,4},{1,5},{2,6},{3,7},{4,0},{5,1},{6,2},{7,3},{8,12},{9,13},{10,... | collective-permute-start | bytes 393224 | tf_op jit(solution)/shard_map/ppermute | solution.py:98
  105.9 6.4 %collective-permute-start.29 = (bf16[128,1024]{1,0:T(8,128)(2,1)S(1)}, bf16[128,1024]{1,0:T(8,128)(2,1)S(1)}, u32[]{:S(2)}, u32[]{:S(2)}) collective-permute-start(bf16[128,1024]{1,0:T(8,128)(2,1)S(1)} %constant_dynamic-update-slice_fusion.14), channel_id=1, source_target_pairs={{0,2},{1,3},{2,0},{3,1},{4,6},{5,7},{6,4},{7,5},{8,10},{9,11},{10,... | collective-permute-start | bytes 786440 | tf_op jit(solution)/shard_map/ppermute | solution.py:98
  107.5 5.7 %collective-permute-start.35 = (bf16[256,1024]{1,0:T(8,128)(2,1)S(1)}, bf16[256,1024]{1,0:T(8,128)(2,1)S(1)}, u32[]{:S(2)}, u32[]{:S(2)}) collective-permute-start(bf16[256,1024]{1,0:T(8,128)(2,1)S(1)} %constant_dynamic-update-slice_fusion.16), channel_id=1, source_target_pairs={{0,1},{1,0},{2,3},{3,2},{4,5},{5,4},{6,7},{7,6},{8,9},{9,8},{10,11... | collective-permute-start | bytes 1572872 | tf_op jit(solution)/shard_map/ppermute | solution.py:98
  109.1 6.0 %collective-permute-start.34 = (bf16[64,1024]{1,0:T(8,128)(2,1)S(1)}, bf16[64,1024]{1,0:T(8,128)(2,1)S(1)}, u32[]{:S(2)}, u32[]{:S(2)}) collective-permute-start(bf16[64,1024]{1,0:T(8,128)(2,1)S(1)} %constant_dynamic-update-slice_fusion.18), channel_id=1, source_target_pairs={{0,4},{1,5},{2,6},{3,7},{4,0},{5,1},{6,2},{7,3},{8,12},{9,13},{10,... | collective-permute-start | bytes 393224 | tf_op jit(solution)/shard_map/ppermute | solution.py:98
  109.9 8.3 %collective-permute-start.33 = (bf16[128,1024]{1,0:T(8,128)(2,1)S(1)}, bf16[128,1024]{1,0:T(8,128)(2,1)S(1)}, u32[]{:S(2)}, u32[]{:S(2)}) collective-permute-start(bf16[128,1024]{1,0:T(8,128)(2,1)S(1)} %constant_dynamic-update-slice_fusion.20), channel_id=1, source_target_pairs={{0,2},{1,3},{2,0},{3,1},{4,6},{5,7},{6,4},{7,5},{8,10},{9,11},{10,... | collective-permute-start | bytes 786440 | tf_op jit(solution)/shard_map/ppermute | solution.py:98
  112.3 6.7 %collective-permute-start.37 = (bf16[256,1024]{1,0:T(8,128)(2,1)S(1)}, bf16[256,1024]{1,0:T(8,128)(2,1)S(1)}, u32[]{:S(2)}, u32[]{:S(2)}) collective-permute-start(bf16[256,1024]{1,0:T(8,128)(2,1)S(1)} %constant_dynamic-update-slice_fusion.22), channel_id=1, source_target_pairs={{0,1},{1,0},{2,3},{3,2},{4,5},{5,4},{6,7},{7,6},{8,9},{9,8},{10,11... | collective-permute-start | bytes 1572872 | tf_op jit(solution)/shard_map/ppermute | solution.py:98
  115.1 8.5 %collective-permute-start.36 = (bf16[128,1024]{1,0:T(8,128)(2,1)S(1)}, bf16[128,1024]{1,0:T(8,128)(2,1)S(1)}, u32[]{:S(2)}, u32[]{:S(2)}) collective-permute-start(bf16[128,1024]{1,0:T(8,128)(2,1)S(1)} %constant_dynamic-update-slice_fusion.24), channel_id=1, source_target_pairs={{0,2},{1,3},{2,0},{3,1},{4,6},{5,7},{6,4},{7,5},{8,10},{9,11},{10,... | collective-permute-start | bytes 786440 | tf_op jit(solution)/shard_map/ppermute | solution.py:98
  118.2 6.3 %collective-permute-start.38 = (bf16[256,1024]{1,0:T(8,128)(2,1)S(1)}, bf16[256,1024]{1,0:T(8,128)(2,1)S(1)}, u32[]{:S(2)}, u32[]{:S(2)}) collective-permute-start(bf16[256,1024]{1,0:T(8,128)(2,1)S(1)} %constant_dynamic-update-slice_fusion.26), channel_id=1, source_target_pairs={{0,1},{1,0},{2,3},{3,2},{4,5},{5,4},{6,7},{7,6},{8,9},{9,8},{10,11... | collective-permute-start | bytes 1572872 | tf_op jit(solution)/shard_map/ppermute | solution.py:98
  123.7 2.0 %collective-permute-start.39 = (bf16[256,1024]{1,0:T(8,128)(2,1)S(1)}, bf16[256,1024]{1,0:T(8,128)(2,1)S(1)}, u32[]{:S(2)}, u32[]{:S(2)}) collective-permute-start(bf16[256,1024]{1,0:T(8,128)(2,1)S(1)} %constant_dynamic-update-slice_fusion.28), channel_id=1, source_target_pairs={{0,1},{1,0},{2,3},{3,2},{4,5},{5,4},{6,7},{7,6},{8,9},{9,8},{10,11... | collective-permute-start | bytes 1572872 | tf_op jit(solution)/shard_map/ppermute | solution.py:98
